TPU v7x, 128 devices: a whole 4x4x4 slice. The times are simulated.
128 devices in a mesh: ha: 4 (over x), wa: 16 (over z, y), ba: 2 (over core).
Axes of the slice: x: 4, y: 4, z: 4, core: 2. Of those that a mesh axis runs over, the one named last changes fastest.
Arguments:
- frames: bfloat16 [2, 4, 128, 79872], P('ba', None, 'ha', 'wa'), may hold values from -6 to 6
- cache: bfloat16 [2, 2, 128, 79872], P('ba', None, 'ha', 'wa'), may hold values from -6 to 6
- norm_gain: float32 [96], replicated, may hold values from 0.5 to 2
- conv_weight: bfloat16 [27, 9216], replicated, may hold values from -0.125 to 0.125
- conv_bias: float32 [96], replicated, may hold values from -3 to 3
- down_weight: bfloat16 [9, 9216], replicated, may hold values from -0.21875 to 0.21875
- down_bias: float32 [96], replicated, may hold values from -3 to 3
- latent_weight: bfloat16 [96, 16], replicated, may hold values from -0.625 to 0.625
- latent_bias: float32 [16], replicated, may hold values from -3 to 3
- valid_frames: int32 [2], P('ba'), may hold values from 1 to 4, as said below
- owners: int32 [2, 4, 16, 64, 1], P('ba', 'ha', 'wa'), may hold values from 0 to 3; in each aligned block of 64 rows (0 to 63, 64 to 127, ..., all dimensions but the last counted through in order) at most 32 rows name the same one
Outputs:
- routed: bfloat16 [2, 4, 16, 128, 416], P('ba', 'ha', 'wa')
Inputs may be any that keep to these rules, and one draw needn't show every extreme that they name: `valid_frames`: some clip has all 4 frames valid. `owners`: among the 64 rows of one tile, no owner is named more than 32 times.
All inputs are finite; a program needn't handle non-finite values.
Results may differ from a plain program's by a relative error of at most 0.0058.
Values may be sent and summed in bfloat16 or wider, within the bound.
A program may use at most 128 MiB of HBM per device.

v0:
```python
import jax
import jax.numpy as jnp
from jax import lax
from jax.sharding import PartitionSpec as P

EPS = 1e-06
SHAPES = ("NDHWC", "DHWIO", "NDHWC")


def with_halo(array, sides, width):
    for axis, dim in sides:
        size, length = (lax.axis_size(axis), array.shape[dim])
        up = [(i, (i + 1) % size) for i in range(size - 1)]
        down = [(j, i) for i, j in up]
        last = lax.slice_in_dim(array, length - width, length, axis=dim)
        initial = lax.slice_in_dim(array, 0, width, axis=dim)
        before = lax.ppermute(last, axis, up)
        after = lax.ppermute(initial, axis, down)
        array = jnp.concatenate([before, array, after], axis=dim)
    return array


def from_behind(value, axis, steps):
    count = lax.axis_size(axis)
    initial, last = (max(0, -steps), min(count, count - steps))
    return lax.ppermute(value, axis, [(source, source + steps) for source in range(initial, last)])


def per_device(
    frames,
    cache,
    norm_gain,
    conv_weight,
    conv_bias,
    down_weight,
    down_bias,
    latent_weight,
    latent_bias,
    valid_frames,
    owners,
):
    clips = frames.shape[0]
    frame_count = frames.shape[1]
    tile_rows = frames.shape[2]
    channels = norm_gain.shape[0]
    tile_cols = frames.shape[3] // channels
    as_float = frames.astype(jnp.float32).reshape(
        clips, frame_count, tile_rows, tile_cols, channels
    )
    mean_square = jnp.mean(as_float * as_float, axis=-1, keepdims=True)
    normed = as_float * lax.rsqrt(mean_square + EPS) * norm_gain
    activated = jax.nn.silu(normed).astype(jnp.bfloat16)
    earlier = cache.reshape(clips, cache.shape[1], tile_rows, tile_cols, channels)
    stacked = jnp.concatenate([earlier, activated], axis=1)
    padded = with_halo(stacked, (("ha", 2), ("wa", 3)), 1)
    kernel = conv_weight.reshape(3, 3, 3, channels, channels)
    convolved = lax.conv_general_dilated(
        padded,
        kernel,
        (1, 1, 1),
        "VALID",
        dimension_numbers=SHAPES,
        preferred_element_type=jnp.float32,
    )
    hidden = (as_float + convolved + conv_bias).astype(jnp.bfloat16)
    below_row = from_behind(hidden[:, :, :1], "ha", -1)
    extended = jnp.concatenate([hidden, below_row], axis=2)
    down_kernel = down_weight.reshape(1, 3, 3, channels, channels)
    right_col = from_behind(extended[:, :, :, :1], "wa", -1)
    widened = jnp.concatenate([extended, right_col], axis=3)
    reduced = lax.conv_general_dilated(
        widened,
        down_kernel,
        (1, 2, 2),
        "VALID",
        dimension_numbers=SHAPES,
        preferred_element_type=jnp.float32,
    )
    reduced = (reduced + down_bias).astype(jnp.bfloat16)
    latent_f = jnp.einsum(
        "bfhwc,cz->bfhwz", reduced, latent_weight, preferred_element_type=jnp.float32
    )
    latent_f = latent_f + latent_bias
    present = jnp.arange(frame_count)[None, :] < valid_frames[:, None]
    latent = jnp.where(present[:, :, None, None, None], latent_f, 0.0).astype(jnp.bfloat16)
    row_count = owners.shape[3]
    row_data = latent.reshape(clips, row_count, -1)
    num_owners = lax.axis_size("ha")
    capacity = 2 * row_count // num_owners
    owner_ids = owners.reshape(clips, row_count)
    one_hot = (
        owner_ids[:, :, None] == jnp.arange(num_owners, dtype=jnp.int32)[None, None, :]
    ).astype(jnp.int32)
    ranking = jnp.cumsum(one_hot, axis=1) - 1
    slot_index = jnp.sum(one_hot * ranking, axis=-1)
    target = owner_ids * capacity + slot_index
    selector = (
        target[:, None, :] == jnp.arange(num_owners * capacity, dtype=jnp.int32)[None, :, None]
    ).astype(jnp.bfloat16)
    outgoing = jnp.einsum(
        "bsr,brl->bsl", selector, row_data, preferred_element_type=jnp.float32
    ).astype(jnp.bfloat16)
    received = lax.all_to_all(outgoing, "ha", split_axis=1, concat_axis=1, tiled=True)
    return received.reshape(clips, 1, 1, num_owners * capacity, received.shape[2])


def solution(mesh):
    in_specs = (
        P("ba", None, "ha", "wa"),
        P("ba", None, "ha", "wa"),
        P(),
        P(),
        P(),
        P(),
        P(),
        P(),
        P(),
        P("ba"),
        P("ba", "ha", "wa", None, None),
    )
    out_specs = P("ba", "ha", "wa", None, None)
    return jax.shard_map(
        per_device, mesh=mesh, in_specs=in_specs, out_specs=out_specs, check_vma=False
    )
```

profile of v0, /device:TPU:24, one launch (start us, length us, event | category | flops | bytes accessed | tf_op | source)
XLA Modules:
  0.0 98.1 jit_solution(4943897832613615348)
XLA Ops:
  0.0 4.8 %reshape.274 = f32[1,4,32,52,96]{4,3,2,1,0:T(8,128)} reshape(bf16[1,4,32,4992]{3,2,1,0:T(8,128)(2,1)} %param.11) | data formatting | bytes 3833856 | tf_op jit(solution)/shard_map/reshape | solution.py:47
  4.8 3.1 %multiply_reduce_fusion = f32[4,32,52]{2,1,0:T(8,128)S(1)} fusion(f32[1,4,32,52,96]{4,3,2,1,0:T(8,128)} %reshape.274), kind=kLoop, calls=%fused_computation.15 | loop fusion | flops 1271296 | bytes 2582528 | tf_op jit(solution)/shard_map/reduce_sum | solution.py:50
  7.9 1.3 %reshape.253 = bf16[1,2,32,52,96]{4,3,2,1,0:T(8,128)(2,1)S(1)} reshape(bf16[1,2,32,4992]{3,2,1,0:T(8,128)(2,1)S(1)} %copy-done.3) | data formatting | bytes 1277952 | tf_op jit(solution)/shard_map/reshape | solution.py:53
  9.2 2.7 %multiply_convert_fusion = bf16[1,4,32,52,96]{4,3,2,1,0:T(8,128)(2,1)S(1)} fusion(f32[1,4,32,52,96]{4,3,2,1,0:T(8,128)} %reshape.274, f32[96]{0:T(128)S(1)} %copy-done.7, f32[4,32,52]{2,1,0:T(8,128)S(1)} %add_rsqrt_fusion), kind=kLoop, calls=%fused_computation.14 | loop fusion | flops 4472832 | bytes 3860864 | tf_op jit(solution)/shard_map/convert_element_type | solution.py:52
  11.9 0.7 pad_maximum_fusion.5
  12.6 3.4 %collective-permute-start = (bf16[1,6,1,52,96]{4,3,2,1,0:T(8,128)(2,1)}, bf16[1,6,1,52,96]{4,3,2,1,0:T(8,128)(2,1)S(1)}, u32[]{:S(2)}, u32[]{:S(2)}) collective-permute-start(bf16[1,6,1,52,96]{4,3,2,1,0:T(8,128)(2,1)} %get-tuple-element.7), channel_id=1, source_target_pairs={{0,32},{32,64},{64,96},{1,33},{33,65},{65,97},{2,34},{34,66},{66,9... | collective-permute-start | bytes 179720 | tf_op jit(solution)/shard_map/ppermute | solution.py:17
  15.9 1.3 %collective-permute-start.1 = (bf16[1,6,1,52,96]{4,3,2,1,0:T(8,128)(2,1)}, bf16[1,6,1,52,96]{4,3,2,1,0:T(8,128)(2,1)S(1)}, u32[]{:S(2)}, u32[]{:S(2)}) collective-permute-start(bf16[1,6,1,52,96]{4,3,2,1,0:T(8,128)(2,1)} %get-tuple-element.8), channel_id=1, source_target_pairs={{32,0},{64,32},{96,64},{33,1},{65,33},{97,65},{34,2},{66,34},{98,6... | collective-permute-start | bytes 179720 | tf_op jit(solution)/shard_map/ppermute | solution.py:18
  17.9 0.9 reduce_window_sum.11
  18.8 3.7 %collective-permute-done.1 = bf16[1,6,1,52,96]{4,3,2,1,0:T(8,128)(2,1)S(1)} collective-permute-done((bf16[1,6,1,52,96]{4,3,2,1,0:T(8,128)(2,1)}, bf16[1,6,1,52,96]{4,3,2,1,0:T(8,128)(2,1)S(1)}, u32[]{:S(2)}, u32[]{:S(2)}) %collective-permute-start.1) | collective-permute-done | bytes 59936 | tf_op jit(solution)/shard_map/ppermute | solution.py:18
  22.5 0.9 pad_maximum_fusion.3
  23.5 3.5 %collective-permute-start.2 = (bf16[1,6,34,1,96]{4,3,2,1,0:T(2,128)(2,1)}, bf16[1,6,34,1,96]{4,3,2,1,0:T(2,128)(2,1)}, u32[]{:S(2)}, u32[]{:S(2)}) collective-permute-start(bf16[1,6,34,1,96]{4,3,2,1,0:T(2,128)(2,1)} %get-tuple-element.5), channel_id=1, source_target_pairs={{0,2},{2,4},{4,6},{6,8},{8,10},{10,12},{12,14},{14,16},{16,18},{18... | collective-permute-start | bytes 117512 | tf_op jit(solution)/shard_map/ppermute | solution.py:17
  26.9 2.5 %collective-permute-start.3 = (bf16[1,6,34,1,96]{4,3,2,1,0:T(2,128)(2,1)}, bf16[1,6,34,1,96]{4,3,2,1,0:T(2,128)(2,1)}, u32[]{:S(2)}, u32[]{:S(2)}) collective-permute-start(bf16[1,6,34,1,96]{4,3,2,1,0:T(2,128)(2,1)} %get-tuple-element.6), channel_id=1, source_target_pairs={{2,0},{4,2},{6,4},{8,6},{10,8},{12,10},{14,12},{16,14},{18,16},{20... | collective-permute-start | bytes 117512 | tf_op jit(solution)/shard_map/ppermute | solution.py:18
  29.5 0.7 select_reduce_fusion
  30.2 1.5 %reshape.254 = bf16[3,3,3,96,96]{4,3,2,1,0:T(8,128)(2,1)} reshape(bf16[27,9216]{1,0:T(8,128)(2,1)S(1)} %copy-done.4) | data formatting | bytes 995328 | tf_op jit(solution)/shard_map/reshape | solution.py:56
  31.8 4.2 %collective-permute-done.3 = bf16[1,6,34,1,96]{4,3,2,1,0:T(2,128)(2,1)} collective-permute-done((bf16[1,6,34,1,96]{4,3,2,1,0:T(2,128)(2,1)}, bf16[1,6,34,1,96]{4,3,2,1,0:T(2,128)(2,1)}, u32[]{:S(2)}, u32[]{:S(2)}) %collective-permute-start.3) | collective-permute-done | bytes 39200 | tf_op jit(solution)/shard_map/ppermute | solution.py:18
  35.9 4.3 %maximum_bitcast_fusion = bf16[6,34,1,54,96]{4,3,1,0,2:T(8,128)(2,1)S(1)} fusion(bf16[1,6,34,1,96]{4,3,2,1,0:T(2,128)(2,1)} %collective-permute-done.3, bf16[1,6,1,52,96]{4,3,2,1,0:T(8,128)(2,1)S(1)} %collective-permute-done.1, bf16[1,4,32,52,96]{4,3,2,1,0:T(8,128)(2,1)S(1)} %multiply_convert_fusion, bf16[1,2,32,52,96]{4,3,2,1,0:T(8,128)(2,1)S(1)} %reshape.253, ...), kind=kLoop, calls=%fused_computation.16 | loop fusion | flops 12690432 | bytes 4230144 | tf_op jit(solution)/shard_map/concatenate | solution.py:19
  40.2 2.2 %pad = bf16[6,34,1,56,96]{4,3,1,0,2:T(8,128)(2,1)} pad(bf16[6,34,1,54,96]{4,3,1,0,2:T(8,128)(2,1)S(1)} %maximum_bitcast_fusion, bf16[]{:T(256)} %constant.25), padding=0_0x0_0x0_0x0_2x0_0 | pad | bytes 4308482 | tf_op jit(solution)/shard_map/concatenate | solution.py:19
  42.4 4.2 %reshape.261 = bf16[6,34,1,8,7,96]{5,4,3,1,0,2:T(8,128)(2,1)S(1)} reshape(bf16[6,34,1,56,96]{4,3,1,0,2:T(8,128)(2,1)} %pad) | data formatting | bytes 4386816 | tf_op jit(solution)/shard_map/conv_general_dilated | solution.py:57
  46.7 0.7 copy.33
  47.7 12.0 %broadcast_select_fusion = f32[4,32,8,7,96]{4,2,3,1,0:T(8,128)S(1)} fusion(pred[8,7]{0,1:T(8,128)(4,1)S(1)} %copy-done.12, bf16[3,3,3,96,96]{4,3,2,1,0:T(8,128)(2,1)S(1)} %copy-done.2, bf16[6,34,1,7,2,96]{5,3,4,1,0,2:T(8,128)(2,1)S(1)} %slice.28, bf16[6,34,1,8,7,96]{5,3,4,1,0,2:T(8,128)(2,1)S(1)} %copy.33), kind=kOutput, calls=%fused_computation.26 | convolution fusion | flops 3576403968 | bytes 5991992 | tf_op jit(solution)/shard_map/conv_general_dilated | solution.py:57
  60.7 1.7 %copy-done.1 = f32[1,4,32,52,96]{4,3,2,1,0:T(8,128)S(1)} copy-done((f32[1,4,32,52,96]{4,3,2,1,0:T(8,128)S(1)}, f32[1,4,32,52,96]{4,3,2,1,0:T(8,128)}, u32[]{:S(2)}) %copy-start.1) | copy-done | bytes 2555928
  62.4 2.1 %fusion.11 = bf16[1,4,32,52,96]{4,3,2,1,0:T(8,128)(2,1)S(1)} fusion(f32[1,4,32,52,96]{4,3,2,1,0:T(8,128)S(1)} %copy-done.1, f32[4,32,1,52,96]{4,1,3,0,2:T(8,128)S(1)} %slice.29, f32[96]{0:T(128)S(1)} %copy-done.8), kind=kLoop, calls=%fused_computation.13 | loop fusion | flops 1916928 | bytes 6390144 | tf_op jit(solution)/shard_map/convert_element_type | solution.py:65
  64.6 1.3 %collective-permute-start.4 = (bf16[1,4,1,52,96]{4,3,2,1,0:T(8,128)(2,1)S(1)}, bf16[1,4,1,52,96]{4,3,2,1,0:T(8,128)(2,1)S(1)}, u32[]{:S(2)}, u32[]{:S(2)}) collective-permute-start(bf16[1,4,1,52,96]{4,3,2,1,0:T(8,128)(2,1)S(1)} %slice.30), channel_id=1, source_target_pairs={{32,0},{64,32},{96,64},{33,1},{65,33},{97,65},{34,2},{66,34},{98,6... | collective-permute-start | bytes 119816 | tf_op jit(solution)/shard_map/ppermute | solution.py:26
  66.5 4.1 %collective-permute-done.4 = bf16[1,4,1,52,96]{4,3,2,1,0:T(8,128)(2,1)S(1)} collective-permute-done((bf16[1,4,1,52,96]{4,3,2,1,0:T(8,128)(2,1)S(1)}, bf16[1,4,1,52,96]{4,3,2,1,0:T(8,128)(2,1)S(1)}, u32[]{:S(2)}, u32[]{:S(2)}) %collective-permute-start.4) | collective-permute-done | bytes 39968 | tf_op jit(solution)/shard_map/ppermute | solution.py:26
  70.7 1.9 %collective-permute-start.5 = (bf16[1,4,33,1,96]{4,3,2,1,0:T(2,128)(2,1)S(1)}, bf16[1,4,33,1,96]{4,3,2,1,0:T(2,128)(2,1)S(1)}, u32[]{:S(2)}, u32[]{:S(2)}) collective-permute-start(bf16[1,4,33,1,96]{4,3,2,1,0:T(2,128)(2,1)S(1)} %pad_maximum_fusion.6), channel_id=1, source_target_pairs={{2,0},{4,2},{6,4},{8,6},{10,8},{12,10},{14,12},{16,14},{18,16},{20... | collective-permute-start | bytes 76040 | tf_op jit(solution)/shard_map/ppermute | solution.py:26
  72.9 6.1 %collective-permute-done.5 = bf16[1,4,33,1,96]{4,3,2,1,0:T(2,128)(2,1)S(1)} collective-permute-done((bf16[1,4,33,1,96]{4,3,2,1,0:T(2,128)(2,1)S(1)}, bf16[1,4,33,1,96]{4,3,2,1,0:T(2,128)(2,1)S(1)}, u32[]{:S(2)}, u32[]{:S(2)}) %collective-permute-start.5) | collective-permute-done | bytes 25376 | tf_op jit(solution)/shard_map/ppermute | solution.py:26
  80.9 1.6 %fusion.29 = bf16[4,16,8,4,96]{4,2,3,1,0:T(8,128)(2,1)S(1)} fusion(bf16[1,3,3,96,96]{4,3,2,1,0:T(8,128)(2,1)S(1)} %reshape.255, bf16[4,33,1,7,2,96]{5,3,4,1,0,2:T(8,128)(2,1)S(1)} %slice.31, bf16[4,33,1,8,8,96]{5,3,4,1,0,2:T(8,128)(2,1)S(1)} %copy.37, f32[96]{0:T(128)S(1)} %copy-done.10, pred[8,4]{0,1:T(4,128)(4,1)S(1)} %copy-done.13), kind=kOutput, calls=%fused_computation.30 | convolution fusion | flops 346411008 | bytes 2536352 | tf_op jit(solution)/shard_map/conv_general_dilated | solution.py:71
  82.8 0.8 fusion.33
  83.6 0.9 copy.40
  85.7 1.5 %reduce.2 = bf16[128,416]{1,0:T(8,128)(2,1)S(1)} reduce(bf16[128,1,416]{2,1,0:T(2,128)(2,1)S(1)} %bitcast.62, bf16[]{:T(256)} %broadcast.191), dimensions={1}, to_apply=%bitcast.54.reduce_sub_computation | reduce | bytes 212994
  87.4 9.6 %all_to_all.5 = bf16[4,2,6656]{2,1,0:T(2,128)(2,1)S(1)} all-to-all(bf16[4,2,6656]{2,1,0:T(2,128)(2,1)S(1)} %reshape.287), channel_id=1, replica_groups=mesh['ha'=4,'wa'=16,'ba'=2] {'ha'}, dimensions={0} | all-to-all | bytes 212992 | tf_op jit(solution)/shard_map/all_to_all | solution.py:103
  97.3 0.8 copy.42
  (51 shorter events, 6.2 us)
Async XLA Ops:
  0.0 82.8 %copy-start = (bf16[96,16]{0,1:T(8,128)(2,1)S(1)}, bf16[96,16]{0,1:T(8,128)(2,1)}, u32[]{:S(2)}) copy-start(bf16[96,16]{0,1:T(8,128)(2,1)} %param.18) | copy-start | bytes 9220
  0.0 7.9 %copy-start.3 = (bf16[1,2,32,4992]{3,2,1,0:T(8,128)(2,1)S(1)}, bf16[1,2,32,4992]{3,2,1,0:T(8,128)(2,1)}, u32[]{:S(2)}) copy-start(bf16[1,2,32,4992]{3,2,1,0:T(8,128)(2,1)} %param.12) | copy-start | bytes 1916932
  4.8 4.4 %copy-start.7 = (f32[96]{0:T(128)S(1)}, f32[96]{0:T(128)}, u32[]{:S(2)}) copy-start(f32[96]{0:T(128)} %param.13) | copy-start | bytes 1156
  9.2 8.1 %copy-start.6 = (s32[1,1,1,64,1]{3,4,2,1,0:T(1,128)S(1)}, s32[1,1,1,64,1]{3,4,2,1,0:T(1,128)}, u32[]{:S(2)}) copy-start(s32[1,1,1,64,1]{3,4,2,1,0:T(1,128)} %param.21) | copy-start | bytes 772
  11.8 18.4 %copy-start.4 = (bf16[27,9216]{1,0:T(8,128)(2,1)S(1)}, bf16[27,9216]{1,0:T(8,128)(2,1)}, u32[]{:S(2)}) copy-start(bf16[27,9216]{1,0:T(8,128)(2,1)} %param.14) | copy-start | bytes 1492996
  12.6 6.2 %collective-permute-start = (bf16[1,6,1,52,96]{4,3,2,1,0:T(8,128)(2,1)}, bf16[1,6,1,52,96]{4,3,2,1,0:T(8,128)(2,1)S(1)}, u32[]{:S(2)}, u32[]{:S(2)}) collective-permute-start(bf16[1,6,1,52,96]{4,3,2,1,0:T(8,128)(2,1)} %get-tuple-element.7), channel_id=1, source_target_pairs={{0,32},{32,64},{64,96},{1,33},{33,65},{65,97},{2,34},{34,66},{66,9... | collective-permute-start | bytes 179720 | tf_op jit(solution)/shard_map/ppermute | solution.py:17
  15.9 6.6 %collective-permute-start.1 = (bf16[1,6,1,52,96]{4,3,2,1,0:T(8,128)(2,1)}, bf16[1,6,1,52,96]{4,3,2,1,0:T(8,128)(2,1)S(1)}, u32[]{:S(2)}, u32[]{:S(2)}) collective-permute-start(bf16[1,6,1,52,96]{4,3,2,1,0:T(8,128)(2,1)} %get-tuple-element.8), channel_id=1, source_target_pairs={{32,0},{64,32},{96,64},{33,1},{65,33},{97,65},{34,2},{66,34},{98,6... | collective-permute-start | bytes 179720 | tf_op jit(solution)/shard_map/ppermute | solution.py:18
  23.5 8.3 %collective-permute-start.2 = (bf16[1,6,34,1,96]{4,3,2,1,0:T(2,128)(2,1)}, bf16[1,6,34,1,96]{4,3,2,1,0:T(2,128)(2,1)}, u32[]{:S(2)}, u32[]{:S(2)}) collective-permute-start(bf16[1,6,34,1,96]{4,3,2,1,0:T(2,128)(2,1)} %get-tuple-element.5), channel_id=1, source_target_pairs={{0,2},{2,4},{4,6},{6,8},{8,10},{10,12},{12,14},{14,16},{16,18},{18... | collective-permute-start | bytes 117512 | tf_op jit(solution)/shard_map/ppermute | solution.py:17
  26.9 9.0 %collective-permute-start.3 = (bf16[1,6,34,1,96]{4,3,2,1,0:T(2,128)(2,1)}, bf16[1,6,34,1,96]{4,3,2,1,0:T(2,128)(2,1)}, u32[]{:S(2)}, u32[]{:S(2)}) collective-permute-start(bf16[1,6,34,1,96]{4,3,2,1,0:T(2,128)(2,1)} %get-tuple-element.6), channel_id=1, source_target_pairs={{2,0},{4,2},{6,4},{8,6},{10,8},{12,10},{14,12},{16,14},{18,16},{20... | collective-permute-start | bytes 117512 | tf_op jit(solution)/shard_map/ppermute | solution.py:18
  46.6 1.1 %copy-start.2 = (bf16[3,3,3,96,96]{4,3,2,1,0:T(8,128)(2,1)S(1)}, bf16[3,3,3,96,96]{4,3,2,1,0:T(8,128)(2,1)}, u32[]{:S(2)}) copy-start(bf16[3,3,3,96,96]{4,3,2,1,0:T(8,128)(2,1)} %reshape.254) | copy-start | bytes 1492996
  46.7 1.1 %copy-start.12 = (pred[8,7]{0,1:T(8,128)(4,1)S(1)}, pred[8,7]{0,1:T(8,128)(4,1)}, u32[]{:S(2)}) copy-start(pred[8,7]{0,1:T(8,128)(4,1)} %constant.34) | copy-start | bytes 172
  60.4 2.0 %copy-start.1 = (f32[1,4,32,52,96]{4,3,2,1,0:T(8,128)S(1)}, f32[1,4,32,52,96]{4,3,2,1,0:T(8,128)}, u32[]{:S(2)}) copy-start(f32[1,4,32,52,96]{4,3,2,1,0:T(8,128)} %reshape.274) | copy-start | bytes 7667716
  60.4 2.0 %copy-start.8 = (f32[96]{0:T(128)S(1)}, f32[96]{0:T(128)}, u32[]{:S(2)}) copy-start(f32[96]{0:T(128)} %param.15) | copy-start | bytes 1156
  62.4 3.4 %copy-start.9 = (s32[64]{0:T(128)S(1)}, s32[64]{0:T(128)}, u32[]{:S(2)}) copy-start(s32[64]{0:T(128)} %select_reduce_fusion) | copy-start | bytes 772
  62.4 10.2 %copy-start.5 = (bf16[9,9216]{1,0:T(8,128)(2,1)S(1)}, bf16[9,9216]{1,0:T(8,128)(2,1)}, u32[]{:S(2)}) copy-start(bf16[9,9216]{1,0:T(8,128)(2,1)} %param.16) | copy-start | bytes 497668
  64.6 6.1 %collective-permute-start.4 = (bf16[1,4,1,52,96]{4,3,2,1,0:T(8,128)(2,1)S(1)}, bf16[1,4,1,52,96]{4,3,2,1,0:T(8,128)(2,1)S(1)}, u32[]{:S(2)}, u32[]{:S(2)}) collective-permute-start(bf16[1,4,1,52,96]{4,3,2,1,0:T(8,128)(2,1)S(1)} %slice.30), channel_id=1, source_target_pairs={{32,0},{64,32},{96,64},{33,1},{65,33},{97,65},{34,2},{66,34},{98,6... | collective-permute-start | bytes 119816 | tf_op jit(solution)/shard_map/ppermute | solution.py:26
  70.7 8.3 %collective-permute-start.5 = (bf16[1,4,33,1,96]{4,3,2,1,0:T(2,128)(2,1)S(1)}, bf16[1,4,33,1,96]{4,3,2,1,0:T(2,128)(2,1)S(1)}, u32[]{:S(2)}, u32[]{:S(2)}) collective-permute-start(bf16[1,4,33,1,96]{4,3,2,1,0:T(2,128)(2,1)S(1)} %pad_maximum_fusion.6), channel_id=1, source_target_pairs={{2,0},{4,2},{6,4},{8,6},{10,8},{12,10},{14,12},{16,14},{18,16},{20... | collective-permute-start | bytes 76040 | tf_op jit(solution)/shard_map/ppermute | solution.py:26
  80.1 0.8 copy-start.10
  80.1 0.8 copy-start.13
  80.9 1.9 %copy-start.11 = (f32[16]{0:T(128)S(1)}, f32[16]{0:T(128)}, u32[]{:S(2)}) copy-start(f32[16]{0:T(128)} %param.19) | copy-start | bytes 196
where the time goes:
time: 98.7 us; the launch traced here: 98.1 us
  local copies, waits for them, and re-layouts  22.7 us (23%)
  other arithmetic  18.1 us (18%)
  waiting for transfers between devices  18.1 us (18%)
  matrix products  14.5 us (15%)
  starting transfers between devices  13.9 us (14%)
  blocking collectives  9.65 us (10%)
  between operations  1.05 us (1%)
    conv_general_dilated x1, matrix products, per_device(): lax.conv_general_dilated(padded, kernel, (1, 1, 1), 'VALID', dimension_nu...  12 us
    ppermute x2, waiting for transfers between devices, from_behind(): lax.ppermute(value, axis, [(source, source + steps) for source in range(i...  10.2 us
    all_to_all x1, blocking collectives, per_device(): lax.all_to_all(outgoing, 'ha', split_axis=1, concat_axis=1, tiled=True)  9.65 us
    ppermute x2, waiting for transfers between devices, with_halo(): after = lax.ppermute(initial, axis, down)  7.93 us
    ppermute x2, starting transfers between devices, with_halo(): before = lax.ppermute(last, axis, up)  6.86 us
    conv_general_dilated x5, local copies, waits for them, and re-layouts, per_device(): lax.conv_general_dilated(padded, kernel, (1, 1, 1), 'VALID', dimension_nu...  6.16 us
    reshape x1, local copies, waits for them, and re-layouts, per_device(): frames.astype(jnp.float32)  4.76 us
    concatenate x1, other arithmetic, with_halo(): array = jnp.concatenate([before, array, after], axis=dim)  4.28 us
  transfers between devices with their start and end apart: 6, of which 4 were waited for; matrix products, arithmetic and copies ran while one was open for 4% of the time, Pallas kernels for 0%

commit v1 on v0

v1 whole, which is shorter than its diff:
```python
import functools

import jax
import jax.numpy as jnp
import numpy as np
from jax import lax
from jax.experimental import pallas as pl
from jax.experimental.pallas import tpu as pltpu
from jax.sharding import PartitionSpec as P

EPS = 1e-06
C = 96
Z = 16
T = 4
TH = 32
TW = 52
OWN = 39
EXT = 42
FS = 48
KK = 27
QB = 8
KD = 1664
F32 = jnp.float32
BF16 = jnp.bfloat16


def lanes(tile, count=1):
    return pl.ds(pl.multiple_of(tile * 128, 128), count * 128)


def kernel(
    n_ha,
    n_wa,
    frames,
    cache,
    owners,
    valid,
    wa_w,
    wb_w,
    wd02,
    wd1,
    gain,
    cbias,
    lbias,
    out,
    ext,
    pack_top,
    pack_bot,
    above,
    below,
    act,
    xf,
    planes,
    ones,
    hp,
    hb,
    l32,
    x32,
    hp32,
    h32,
    vs,
    send,
    local_sem,
    send_sem,
    recv_sem,
    a2a_send,
    a2a_recv,
    self_sem,
):
    ha, wa = lax.axis_index("ha"), lax.axis_index("wa")
    up, down = lax.rem(ha + n_ha - 1, n_ha), lax.rem(ha + 1, n_ha)
    left, right = lax.rem(wa + n_wa - 1, n_wa), lax.rem(wa + 1, n_wa)

    load_cache = pltpu.make_async_copy(
        cache.at[0], ext.at[pl.ds(0, 2), :, pl.ds(0, OWN * 128)], local_sem.at[0]
    )
    load_frames = pltpu.make_async_copy(
        frames.at[0], ext.at[pl.ds(2, T), :, pl.ds(0, OWN * 128)], local_sem.at[1]
    )
    load_cache.start()
    load_frames.start()

    barrier = pltpu.get_barrier_semaphore()
    greeted = [
        {"ha": up, "wa": wa},
        {"ha": down, "wa": wa},
        {"ha": ha, "wa": left},
        {"ha": ha, "wa": right},
        {"ha": up, "wa": left},
        {"ha": up, "wa": right},
        {"ha": down, "wa": left},
        {"ha": down, "wa": right},
        {"ha": lax.rem(ha + 2, n_ha), "wa": wa},
    ]
    for device in greeted:
        pl.semaphore_signal(
            barrier, inc=1, device_id=device, device_id_type=pl.DeviceIdType.MESH
        )

    def remote(src, dst, index, device):
        return pltpu.make_async_remote_copy(
            src_ref=src,
            dst_ref=dst,
            send_sem=send_sem.at[index],
            recv_sem=recv_sem.at[index],
            device_id=device,
            device_id_type=pl.DeviceIdType.MESH,
        )

    load_cache.wait()
    load_frames.wait()

    sub = lax.broadcasted_iota(jnp.int32, (8, 384), 0)

    @pl.loop(0, OWN // 3)
    def _(g):
        win = lanes(3 * g, 3)
        tops = [ext[f, pl.ds(0, 16), win].astype(F32) for f in range(6)]
        bots = [ext[f, pl.ds(16, 16), win].astype(F32) for f in range(6)]
        lo = jnp.zeros((8, 384), F32)
        hi = jnp.zeros((8, 384), F32)
        for t in range(T):
            lo = jnp.where(sub == t, tops[2 + t][0:1], lo)
            lo = jnp.where(sub == 4 + t, tops[2 + t][1:2], lo)
        for t in range(2):
            hi = jnp.where(sub == t, tops[t][0:1], hi)
            hi = jnp.where(sub == 2 + t, tops[t][1:2], hi)
        pack_top[:, win] = jnp.concatenate([lo, hi], axis=0).astype(BF16)
        lo = jnp.zeros((8, 384), F32)
        for t in range(T):
            lo = jnp.where(sub == t, bots[2 + t][15:16], lo)
        for t in range(2):
            lo = jnp.where(sub == 4 + t, bots[t][15:16], lo)
        pack_bot[:, win] = jnp.concatenate([lo, jnp.zeros((8, 384), F32)], axis=0).astype(BF16)

    pl.semaphore_wait(barrier, len(greeted))

    own = pl.ds(0, OWN * 128)
    first, last = pl.ds(0, 256), pl.ds((OWN - 1) * 128, 128)
    from_right, from_left = pl.ds(OWN * 128, 256), pl.ds((OWN + 2) * 128, 128)
    row_copies = [
        remote(pack_top, below.at[:, own], 0, {"ha": up, "wa": wa}),
        remote(pack_bot, above.at[:, own], 1, {"ha": down, "wa": wa}),
        remote(pack_top.at[:, first], below.at[:, from_right], 2, {"ha": up, "wa": left}),
        remote(pack_top.at[:, last], below.at[:, from_left], 3, {"ha": up, "wa": right}),
        remote(pack_bot.at[:, first], above.at[:, from_right], 4, {"ha": down, "wa": left}),
        remote(pack_bot.at[:, last], above.at[:, from_left], 5, {"ha": down, "wa": right}),
    ]
    col_copies = [
        remote(
            frames.at[0, :, :, first],
            ext.at[pl.ds(2, T), :, from_right],
            6,
            {"ha": ha, "wa": left},
        ),
        remote(
            cache.at[0, :, :, first],
            ext.at[pl.ds(0, 2), :, from_right],
            7,
            {"ha": ha, "wa": left},
        ),
        remote(
            frames.at[0, :, :, last],
            ext.at[pl.ds(2, T), :, from_left],
            8,
            {"ha": ha, "wa": right},
        ),
        remote(
            cache.at[0, :, :, last],
            ext.at[pl.ds(0, 2), :, from_left],
            9,
            {"ha": ha, "wa": right},
        ),
    ]
    for copy in row_copies + col_copies:
        copy.start()

    def column_of(axis):
        index = lax.broadcasted_iota(jnp.int32, (384, 384), axis)
        return sum((index >= edge).astype(jnp.int32) for edge in (96, 192, 288))

    ones[...] = jnp.where(column_of(0) == column_of(1), 1.0, 0.0).astype(BF16)

    has_left = jnp.where(wa == 0, 0.0, 1.0).astype(F32)
    has_right = jnp.where(wa == n_wa - 1, 0.0, 1.0).astype(F32)
    has_above = jnp.where(ha == 0, 0.0, 1.0).astype(F32)
    has_below = jnp.where(ha == n_ha - 1, 0.0, 1.0).astype(F32)
    lane = lax.broadcasted_iota(jnp.int32, (1, 128), 1)

    def activate(x):
        squares = jnp.dot((x * x).astype(BF16), ones[...], preferred_element_type=F32)
        v = x * lax.rsqrt(squares * (1.0 / C) + EPS) * gain[...]
        return v / (1.0 + jnp.exp(-v))

    def halo_mask(x):
        return jnp.concatenate([x[:, :256] * has_right, x[:, 256:] * has_left], axis=1)

    def split_rows(tile, even, odd, even_at, odd_at):
        for f in range(6):
            rows = pl.ds(f * 16, 16)
            planes[even, tile + 1, rows] = act[tile, pl.ds(f * FS + even_at, 16, 2)].astype(BF16)
            planes[odd, tile + 1, rows] = act[tile, pl.ds(f * FS + odd_at, 16, 2)].astype(BF16)

    def group(g, edge):
        win = lanes(3 * g, 3)
        x = ext[pl.ds(2, T), :, win].reshape(T * TH, 384).astype(F32)
        earlier = ext[pl.ds(0, 2), :, win].reshape(2 * TH, 384).astype(F32)
        if edge:
            x, earlier = halo_mask(x), halo_mask(earlier)
        activated = activate(x)
        for j in range(3):
            cut = slice(128 * j, 128 * (j + 1))
            for f in range(6):
                source = earlier if f < 2 else activated
                at = (f if f < 2 else f - 2) * TH
                act[3 * g + j, pl.ds(f * FS + 8, TH)] = source[at : at + TH, cut]
            split_rows(3 * g + j, 1, 2, 8, 9)
        before = ext[pl.ds(2, T), :, lanes(jnp.maximum(3 * g - 1, 0))]
        before = pltpu.roll(before.reshape(T * TH, 128).astype(F32), 32, 1)
        for j in range(1 if edge else 3):
            here = pltpu.roll(x[:, 128 * j : 128 * (j + 1)], 32, 1)
            xf[3 * g + j + 1] = jnp.where(lane < 32, before, here)
            before = here

    @pl.loop(0, OWN // 3)
    def _(g):
        group(g, False)

    for copy in col_copies:
        copy.wait_recv()
    group(OWN // 3, True)
    for copy in row_copies:
        copy.wait_recv()

    def halo_group(g, edge):
        win = lanes(3 * g, 3)
        hi = below[:, win].astype(F32) * has_below
        lo = above[:, win].astype(F32) * has_above
        if edge:
            hi, lo = halo_mask(hi), halo_mask(lo)
        activated = activate(jnp.concatenate([hi[:8], lo[:8]], axis=0))
        for j in range(3):
            cut = slice(128 * j, 128 * (j + 1))
            tile = 3 * g + j
            act[tile, pl.ds(2 * FS + 40, T, FS)] = activated[0:4, cut]
            act[tile, pl.ds(2 * FS + 41, T, FS)] = activated[4:8, cut]
            act[tile, pl.ds(2 * FS + 7, T, FS)] = activated[8:12, cut]
            act[tile, pl.ds(40, 2, FS)] = hi[8:10, cut]
            act[tile, pl.ds(41, 2, FS)] = hi[10:12, cut]
            act[tile, pl.ds(7, 2, FS)] = lo[4:6, cut]
            split_rows(tile, 3, 0, 10, 7)
        before = below[:, lanes(jnp.maximum(3 * g - 1, 0))].astype(F32) * has_below
        before = pltpu.roll(before[:8], 32, 1)
        for j in range(1 if edge else 3):
            here = pltpu.roll(hi[:8, 128 * j : 128 * (j + 1)], 32, 1)
            x32[3 * g + j + 1] = jnp.where(lane < 32, before, here)
            before = here

    @pl.loop(0, OWN // 3)
    def _(g):
        halo_group(g, False)

    halo_group(OWN // 3, True)

    @pl.loop(0, 4)
    def _(plane):
        planes[plane, 0] = planes[plane, EXT]

        @pl.loop(0, 14)
        def _(i):
            later = planes[plane, 3 * i + 2].astype(F32)
            sooner = planes[plane, jnp.where(i == 0, 41, 3 * i - 1)].astype(F32)
            planes[plane, EXT + 1 + i] = jnp.where(lane < 64, later, sooner).astype(BF16)

    @pl.loop(0, 14)
    def _(i):
        for a in range(3):
            for r in range(3):
                rows = pl.ds(a * FS + 39 + r, T, FS)
                kk = (3 * a + r) * 3
                here = pl.ds(0, T)
                for j in range(3):
                    l32[0, i, kk + j, here] = act[3 * i + j, rows]
                later = act[3 * i + 1, rows]
                sooner = act[jnp.where(i == 0, 40, 3 * i - 2), rows]
                l32[1, i, kk, here] = jnp.where(lane < 64, later, sooner)
                l32[1, i, kk + 1, here] = act[jnp.where(i == 0, 41, 3 * i - 1), rows]
                l32[1, i, kk + 2, here] = act[3 * i, rows]

    def tile_a(k, j):
        return 3 * k + j + 1

    def tile_b(i, j):
        return EXT + 1 + i if j == 0 else 3 * i + j - 1

    def conv(parity, base, count, tile_of, weights):
        rows = []
        for w in range(count):
            pieces = []
            for a in range(3):
                for r in range(3):
                    for j in range(3):
                        pieces.append(
                            planes[r + parity, tile_of(base + w, j), pl.ds(a * 16, 64)]
                        )
            rows.append(jnp.concatenate(pieces, axis=1))
        return jnp.dot(
            jnp.concatenate(rows, axis=0), weights[...], preferred_element_type=F32
        )

    @pl.loop(0, 4)
    def _(step):
        parity, base = step // 2, (step % 2) * 6
        acc = conv(parity, base, 7, tile_a, wa_w)
        for w in range(7):
            k = base + w
            part = acc[64 * w : 64 * (w + 1)]
            x = xf[3 * k + 2, pl.ds(parity, 64, 2)]
            hb[parity, 3 * k + 2] = (x + part[:, :128] + cbias[1]).astype(BF16)
            hp[parity, k + 1] = part[:, 128:]

    cut_right = jnp.where((lane >= 32) & (wa == n_wa - 1), 0.0, 1.0).astype(F32)

    @pl.loop(0, 4)
    def _(step):
        parity, base = step // 2, (step % 2) * 7
        acc = conv(parity, base, 7, tile_b, wb_w)
        for w in range(7):
            i = base + w
            part = acc[64 * w : 64 * (w + 1)]
            x = xf[3 * i, pl.ds(parity, 64, 2)]
            hb[parity, 3 * i] = (x + part[:, :128] + hp[parity, i] + cbias[2]).astype(BF16)
            x = xf[3 * i + 1, pl.ds(parity, 64, 2)]
            h = x + part[:, 128:] + cbias[0]
            h = h * jnp.where(i == 13, cut_right, 1.0)
            hb[parity, 3 * i + 1] = h.astype(BF16)

    def conv32(side, weights):
        rows = []
        for w in range(14):
            rows.append(jnp.concatenate([l32[side, w, kk] for kk in range(KK)], axis=1))
        lhs = jnp.concatenate(rows, axis=0).astype(BF16)
        return jnp.dot(lhs, weights[...], preferred_element_type=F32)

    def put32(index, value):
        h32[index] = jnp.concatenate([value * has_below, jnp.zeros((8, 128), F32)], axis=0).astype(
            BF16
        )

    acc = conv32(0, wa_w)
    for k in range(13):
        part = acc[8 * k : 8 * (k + 1)]
        put32(3 * k + 2, x32[3 * k + 2] + part[:, :128] + cbias[1])
        hp32[k + 1] = part[:, 128:]
    acc = conv32(1, wb_w)
    for i in range(14):
        part = acc[8 * i : 8 * (i + 1)]
        if i:
            put32(3 * i, x32[3 * i] + part[:, :128] + hp32[i] + cbias[2])
        h = x32[3 * i + 1] + part[:, 128:] + cbias[0]
        put32(3 * i + 1, h * cut_right if i == 13 else h)

    def block(b, count):
        even = jnp.concatenate([hb[0, 12 * b + j + 1] for j in range(count)], axis=1)
        odd = jnp.concatenate([hb[1, 12 * b + j + 1] for j in range(count)], axis=1)
        extra = jnp.concatenate([h32[12 * b + j + 1] for j in range(count)], axis=1)
        return even, extra, odd

    blocks = [block(b, 13) for b in range(3)]
    uv = jnp.dot(
        jnp.concatenate([piece for b in blocks for piece in b[:2]], axis=0),
        wd02[...],
        preferred_element_type=F32,
    )
    u1 = jnp.dot(
        jnp.concatenate([b[2] for b in blocks], axis=0), wd1[...], preferred_element_type=F32
    )
    even, extra, odd = block(3, 4)
    uv_last = jnp.dot(
        jnp.concatenate([even, extra], axis=0), wd02[pl.ds(0, 512)], preferred_element_type=F32
    )
    u1_last = jnp.dot(odd, wd1[pl.ds(0, 512)], preferred_element_type=F32)

    latents = []
    for b in range(4):
        both = uv[80 * b : 80 * (b + 1)] if b < 3 else uv_last
        mid = u1[64 * b : 64 * (b + 1)] if b < 3 else u1_last
        for t in range(T):
            vs[t, pl.ds(0, 16)] = both[16 * t : 16 * (t + 1), 128:]
            vs[t, pl.ds(16, 1)] = both[64 + t : 65 + t, 128:]
        shifted = jnp.concatenate([vs[t, pl.ds(1, 16)] for t in range(T)], axis=0)
        latents.append(both[:64, :128] + mid + shifted)
    latent = jnp.concatenate(latents[:3] + [latents[3][:, :32]], axis=1) + lbias[...]
    frame_of = lax.broadcasted_iota(jnp.int32, (64, 1), 0)
    latent = jnp.where(frame_of < valid[0] * 16, latent, 0.0).astype(BF16)

    row = lax.broadcasted_iota(jnp.int32, (64, 64), 0)
    col = lax.broadcasted_iota(jnp.int32, (64, 64), 1)
    by_row = jnp.broadcast_to(owners[...], (64, 64))
    by_col = jnp.sum(jnp.where(row == col, by_row, 0), axis=0, keepdims=True)
    rank = jnp.sum(jnp.where((by_row == by_col) & (row < col), 1, 0), axis=0, keepdims=True)
    slot = by_col * 32 + rank
    slots = lax.broadcasted_iota(jnp.int32, (128, 64), 0)
    selector = jnp.where(slots == slot, 1.0, 0.0).astype(BF16)
    send[...] = jnp.dot(selector, latent, preferred_element_type=F32).astype(BF16)

    here = pl.ds(pl.multiple_of(ha * 32, 32), 32)
    keep = pltpu.make_async_copy(send.at[here], out.at[0, 0, 0, here], self_sem)
    copies = []
    for d in range(1, n_ha):
        target = lax.rem(ha + d, n_ha)
        copies.append(
            pltpu.make_async_remote_copy(
                src_ref=send.at[pl.ds(pl.multiple_of(target * 32, 32), 32)],
                dst_ref=out.at[0, 0, 0, here],
                send_sem=a2a_send.at[d - 1],
                recv_sem=a2a_recv.at[d - 1],
                device_id={"ha": target, "wa": wa},
                device_id_type=pl.DeviceIdType.MESH,
            )
        )
    for copy in copies:
        copy.start()
    keep.start()
    for copy in row_copies + col_copies:
        copy.wait_send()
    for copy in copies:
        copy.wait()
    keep.wait()


def conv_matrices(conv_weight):
    w = conv_weight.reshape(9, 3, C, C)
    zero = jnp.zeros((9, C, C), conv_weight.dtype)
    taps = [zero] + [w[:, s] for s in range(3)] + [zero]
    rows = [jnp.concatenate([taps[s + 1], taps[s]], axis=2) for s in range(4)]
    window = jnp.concatenate(rows, axis=1)
    first = jnp.pad(window, ((0, 0), (0, 0), (0, 64)))
    second = jnp.pad(jnp.roll(window, 64, axis=1), ((0, 0), (0, 0), (64, 0)))
    return first.reshape(KK * 128, 256), second.reshape(KK * 128, 256)


def down_matrices(down_weight, latent_weight):
    dw = down_weight.reshape(9, C, C)
    fused = jnp.einsum("kio,oz->kiz", dw, latent_weight, preferred_element_type=F32)
    fused = fused.astype(BF16).reshape(3, 3, C, Z)
    place = np.zeros((3, 2 * QB + 1, QB), np.float32)
    for s in range(3):
        for q in range(QB):
            place[s, 2 * q + s, q] = 1.0
    banded = jnp.einsum(
        "scq,rsiz->rciqz", jnp.asarray(place, BF16), fused, preferred_element_type=F32
    ).astype(BF16)
    banded = banded.reshape(3, (2 * QB + 1) * C, QB * Z)
    banded = jnp.pad(banded, ((0, 0), (KD - (2 * QB + 1) * C, 0), (0, 0)))
    return jnp.concatenate([banded[0], banded[2]], axis=1), banded[1]


def per_device(
    n_ha,
    n_wa,
    frames,
    cache,
    norm_gain,
    conv_weight,
    conv_bias,
    down_weight,
    down_bias,
    latent_weight,
    latent_bias,
    valid_frames,
    owners,
):
    wa_w, wb_w = conv_matrices(conv_weight)
    wd02, wd1 = down_matrices(down_weight, latent_weight)
    gain = jnp.tile(norm_gain, 4).reshape(1, 384)
    cbias = jnp.roll(jnp.tile(conv_bias, 4), 32).reshape(3, 1, 128)
    lbias = latent_bias + jnp.sum(down_bias[:, None] * latent_weight.astype(F32), axis=0)
    lbias = jnp.tile(lbias, TW // 2).reshape(1, TW // 2 * Z)
    vmem = pl.BlockSpec(memory_space=pltpu.VMEM)
    anyspace = pl.BlockSpec(memory_space=pl.ANY)
    return pl.pallas_call(
        functools.partial(kernel, n_ha, n_wa),
        out_shape=jax.ShapeDtypeStruct((1, 1, 1, 128, 416), BF16),
        in_specs=[anyspace, anyspace, vmem, pl.BlockSpec(memory_space=pltpu.SMEM)] + [vmem] * 7,
        out_specs=anyspace,
        scratch_shapes=[
            pltpu.VMEM((6, TH, EXT * 128), BF16),
            pltpu.VMEM((16, OWN * 128), BF16),
            pltpu.VMEM((16, OWN * 128), BF16),
            pltpu.VMEM((16, EXT * 128), BF16),
            pltpu.VMEM((16, EXT * 128), BF16),
            pltpu.VMEM((EXT, 6 * FS, 128), F32),
            pltpu.VMEM((41, T * TH, 128), F32),
            pltpu.VMEM((4, EXT + 15, 96, 128), BF16),
            pltpu.VMEM((384, 384), BF16),
            pltpu.VMEM((2, 14, 64, 128), F32),
            pltpu.VMEM((2, 41, 64, 128), BF16),
            pltpu.VMEM((2, 14, KK, 8, 128), F32),
            pltpu.VMEM((41, 8, 128), F32),
            pltpu.VMEM((14, 8, 128), F32),
            pltpu.VMEM((41, 16, 128), BF16),
            pltpu.VMEM((T, 24, 128), F32),
            pltpu.VMEM((128, 416), BF16),
            pltpu.SemaphoreType.DMA((2,)),
            pltpu.SemaphoreType.DMA((10,)),
            pltpu.SemaphoreType.DMA((10,)),
            pltpu.SemaphoreType.DMA((n_ha - 1,)),
            pltpu.SemaphoreType.DMA((n_ha - 1,)),
            pltpu.SemaphoreType.DMA,
        ],
        compiler_params=pltpu.CompilerParams(
            collective_id=0, has_side_effects=True, vmem_limit_bytes=56 * 2**20
        ),
        name="encoder_step",
    )(
        frames,
        cache,
        owners.reshape(64, 1),
        valid_frames,
        wa_w,
        wb_w,
        wd02,
        wd1,
        gain,
        cbias,
        lbias,
    )


def solution(mesh):
    in_specs = (
        P("ba", None, "ha", "wa"),
        P("ba", None, "ha", "wa"),
        P(),
        P(),
        P(),
        P(),
        P(),
        P(),
        P(),
        P("ba"),
        P("ba", "ha", "wa", None, None),
    )
    out_specs = P("ba", "ha", "wa", None, None)
    return jax.shard_map(
        functools.partial(per_device, mesh.shape["ha"], mesh.shape["wa"]),
        mesh=mesh,
        in_specs=in_specs,
        out_specs=out_specs,
        check_vma=False,
    )
```

time: 98.7 us -> 56.9 us (0.58)
  the two profiles are of different devices: /device:TPU:24 before, /device:TPU:0 now
where the time goes in v1:
time: 56.9 us; the launch traced here: 56.7 us
  Pallas kernels  35.1 us (62%)
  local copies, waits for them, and re-layouts  14.4 us (25%)
  other arithmetic  5.33 us (9%)
  matrix products  1.07 us (2%)
  between operations  0.82 us (1%)
    pallas_call x1, Pallas kernels, per_device(): pl.pallas_call(functools.partial(kernel, n_ha, n_wa), out_shape=jax.Shape...  35.1 us
    reshape x2, local copies, waits for them, and re-layouts, down_matrices(): banded = banded.reshape(3, (2 * QB + 1) * C, QB * Z)  4.44 us
    concatenate x1, other arithmetic, conv_matrices(): window = jnp.concatenate(rows, axis=1)  2.08 us
    concatenate x1, other arithmetic, conv_matrices(): second = jnp.pad(jnp.roll(window, 64, axis=1), ((0, 0), (0, 0), (64, 0)))  2.05 us
    reshape x1, local copies, waits for them, and re-layouts, conv_matrices(): w = conv_weight.reshape(9, 3, C, C)  1.71 us
    pallas_call x1, local copies, waits for them, and re-layouts, per_device(): pl.pallas_call(functools.partial(kernel, n_ha, n_wa), out_shape=jax.Shape...  1.66 us
    pad x1, local copies, waits for them, and re-layouts, conv_matrices(): first = jnp.pad(window, ((0, 0), (0, 0), (0, 64)))  1.54 us

profile of v1, /device:TPU:0, one launch (start us, length us, event | category | flops | bytes accessed | tf_op | source)
XLA Modules:
  0.0 56.7 jit_solution(15895537523655968999)
XLA Ops:
  0.0 1.7 %reshape.29 = bf16[9,3,96,96]{3,2,1,0:T(8,128)(2,1)S(1)} reshape(bf16[27,9216]{1,0:T(8,128)(2,1)} %param.15) | data formatting | bytes 995328 | tf_op jit(solution)/shard_map/reshape | solution.py:433
  1.8 0.2 concatenate.29
  2.0 2.1 %fusion.5 = bf16[9,384,192]{2,1,0:T(8,128)(2,1)S(1)} fusion(bf16[9,96,96]{2,1,0:T(8,128)(2,1)S(1)} %get-tuple-element.9, bf16[9,96,192]{2,1,0:T(8,128)(2,1)S(1)} %concatenate.29, bf16[9,96,96]{2,1,0:T(8,128)(2,1)S(1)} %get-tuple-element.8, bf16[9,96,96]{2,1,0:T(8,128)(2,1)S(1)} %get-tuple-element.10), kind=kLoop, calls=%fused_computation.8 | loop fusion | flops 9289728 | bytes 2156544 | tf_op jit(solution)/shard_map/concatenate | solution.py:437
  4.1 0.1 slice.48
  4.2 0.1 pad_slice_fusion.3
  4.3 2.0 %fusion.6 = bf16[9,384,256]{2,1,0:T(8,128)(2,1)} fusion(bf16[9,320,192]{2,1,0:T(8,128)(2,1)S(1)} %slice.48, bf16[9,64,192]{2,1,0:T(8,128)(2,1)S(1)} %pad_slice_fusion.3), kind=kLoop, calls=%fused_computation.9 | loop fusion | flops 6193152 | bytes 3096576 | tf_op jit(solution)/shard_map/jit(_roll_static)/concatenate | solution.py:439
  6.4 1.5 %pad.14 = bf16[9,384,256]{2,1,0:T(8,128)(2,1)} pad(bf16[9,384,192]{2,1,0:T(8,128)(2,1)S(1)} %fusion.5, bf16[]{:T(256)} %constant.3.clone.1), padding=0_0x0_0x0_64 | pad | bytes 3096578 | tf_op jit(solution)/shard_map/jit(_pad)/pad | solution.py:438
  7.9 0.0 copy-done
  7.9 0.2 reshape.32
  8.2 0.2 convolution_convert_fusion
  8.4 0.8 %convert_bitcast_fusion = bf16[3,17,96,8,16]{2,1,3,4,0:T(8,128)(2,1)S(1)} fusion(bf16[3,17,8,1,1]{1,0,2,4,3:T(4,128)(2,1)S(1)} %copy-done.2, bf16[3,3,96,16,1]{2,3,1,0,4:T(8,128)(2,1)S(1)} %bitcast.39), kind=kOutput, calls=%fused_computation.5 | convolution fusion | flops 4386816 | bytes 1281840 | tf_op jit(solution)/shard_map/scq,rsiz->rciqz/dot_general | solution.py:451
  9.3 0.6 %copy.24 = bf16[3,17,96,8,16]{2,1,4,3,0:T(8,128)(2,1)S(1)} copy(bf16[3,17,96,8,16]{2,1,3,4,0:T(8,128)(2,1)S(1)} %convert_bitcast_fusion) | data formatting | bytes 2506752 | tf_op jit(solution)/shard_map/convert_element_type | solution.py:453
  9.9 2.5 %reshape.34 = bf16[3,1632,128]{1,2,0:T(8,128)(2,1)} reshape(bf16[3,17,96,8,16]{2,1,4,3,0:T(8,128)(2,1)S(1)} %copy.24) | data formatting | bytes 2506752 | tf_op jit(solution)/shard_map/reshape | solution.py:454
  12.4 2.0 %copy.25 = bf16[3,1632,128]{2,1,0:T(8,128)(2,1)S(1)} copy(bf16[3,1632,128]{1,2,0:T(8,128)(2,1)} %reshape.34) | data formatting | bytes 2506752 | tf_op jit(solution)/shard_map/reshape | solution.py:454
  14.4 0.0 copy-start.4
  14.4 0.0 copy-start.3
  14.4 0.0 copy-start.5
  14.4 0.0 copy-start.7
  14.4 0.0 copy-start.6
  14.4 0.8 %fusion.9 = (bf16[1664,128]{1,0:T(8,128)(2,1)}, bf16[1664,128]{1,0:T(8,128)(2,1)S(1)}, bf16[1664,128]{1,0:T(8,128)(2,1)S(1)}) fusion(bf16[3,1632,128]{2,1,0:T(8,128)(2,1)S(1)} %copy.25), kind=kLoop, calls=%fused_computation.17 | loop fusion | bytes 2531328 | tf_op jit(solution)/shard_map/squeeze | solution.py:456
  15.3 1.0 %pad_maximum_fusion.wd02 = bf16[1664,256]{1,0:T(8,128)(2,1)} fusion(bf16[1664,128]{1,0:T(8,128)(2,1)S(1)} %get-tuple-element.6, bf16[1664,128]{1,0:T(8,128)(2,1)S(1)} %get-tuple-element.7), kind=kLoop, calls=%fused_computation.14 | loop fusion | flops 1703936 | bytes 1703936 | tf_op jit(solution)/shard_map/concatenate | solution.py:456
  16.3 0.0 copy-done.4
  16.3 0.1 tile.10
  16.3 0.1 slice.43
  16.4 0.1 pad_maximum_fusion.1
  16.5 0.6 %reshape.35.cbias = f32[3,1,128]{2,1,0:T(1,128)} reshape(f32[384]{0:T(512)S(1)} %pad_maximum_fusion.1) | data formatting | bytes 3072 | tf_op jit(solution)/shard_map/reshape | solution.py:477
  17.1 0.7 %copy.26.owners = s32[64,1]{1,0:T(8,128)} copy(s32[64,1]{0,1:T(1,128)S(1)} %bitcast.41) | data formatting | bytes 512 | tf_op jit(solution)/shard_map/reshape | solution.py:519
  17.8 0.1 multiply_reduce_fusion
  17.9 0.7 %reshape_tile.7.lbias = f32[1,416]{1,0:T(1,128)} reshape(f32[26,16]{1,0:T(8,128)S(1)} %tile.11) | data formatting | bytes 3328 | tf_op jit(solution)/shard_map/reshape;tile | solution.py:479
  18.6 0.7 %reshape_tile.6.gain = f32[1,384]{1,0:T(1,128)} reshape(f32[4,96]{1,0:T(4,128)S(1)} %tile.8) | data formatting | bytes 3072 | tf_op jit(solution)/shard_map/reshape;tile | solution.py:476
  19.9 35.1 %encoder_step.1 = bf16[1,1,1,128,416]{4,3,2,1,0:T(8,128)(2,1)} custom-call(bf16[1,4,32,4992]{3,2,1,0:T(8,128)(2,1)} %frames.1, bf16[1,2,32,4992]{3,2,1,0:T(8,128)(2,1)} %cache.1, s32[64,1]{1,0:T(8,128)} %copy.26.owners, s32[1]{0:T(128)S(6)} %copy.37.valid, bf16[3456,256]{1,0:T(8,128)(2,1)} %bitcast.38, bf16[3456,256]{1,0:T(8,128)(2,1)} %bitcast.37, ...), custom_call_target="tpu_custom_call" | custom-call | tf_op jit(solution)/shard_map/encoder_step/pallas_call | solution.py:482
  55.0 1.7 %copy.27 = bf16[1,1,1,128,416]{3,4,2,1,0:T(8,128)(2,1)} copy(bf16[1,1,1,128,416]{4,3,2,1,0:T(8,128)(2,1)} %encoder_step.1) | data formatting | bytes 212992 | tf_op jit(solution)/shard_map/encoder_step/pallas_call | solution.py:482
  (14 shorter events, 0.1 us)
Async XLA Ops:
  6.4 1.6 %copy-start = (bf16[9,9216]{1,0:T(8,128)(2,1)S(1)}, bf16[9,9216]{1,0:T(8,128)(2,1)}, u32[]{:S(2)}) copy-start(bf16[9,9216]{1,0:T(8,128)(2,1)} %param.17) | copy-start | bytes 497668
  6.4 1.8 %copy-start.1 = (bf16[96,16]{0,1:T(8,128)(2,1)S(1)}, bf16[96,16]{0,1:T(8,128)(2,1)}, u32[]{:S(2)}) copy-start(bf16[96,16]{0,1:T(8,128)(2,1)} %param.19) | copy-start | bytes 9220
  6.4 2.0 %copy-start.2 = (bf16[3,17,8,1,1]{1,0,2,4,3:T(4,128)(2,1)S(1)}, bf16[3,17,8,1,1]{1,0,2,4,3:T(4,128)(2,1)}, u32[]{:S(2)}) copy-start(bf16[3,17,8,1,1]{1,0,2,4,3:T(4,128)(2,1)} %constant.23) | copy-start | bytes 2452
  14.4 1.9 %copy-start.4 = (f32[96]{0:T(128)S(1)}, f32[96]{0:T(128)}, u32[]{:S(2)}) copy-start(f32[96]{0:T(128)} %param.16) | copy-start | bytes 1156
  14.4 2.7 %copy-start.3 = (s32[1,1,1,64,1]{3,4,2,1,0:T(1,128)S(1)}, s32[1,1,1,64,1]{3,4,2,1,0:T(1,128)}, u32[]{:S(2)}) copy-start(s32[1,1,1,64,1]{3,4,2,1,0:T(1,128)} %param.22) | copy-start | bytes 772
  14.4 3.4 %copy-start.5 = (f32[96]{0:T(128)S(1)}, f32[96]{0:T(128)}, u32[]{:S(2)}) copy-start(f32[96]{0:T(128)} %param.18) | copy-start | bytes 1156
  14.4 3.5 %copy-start.7 = (f32[16]{0:T(128)S(1)}, f32[16]{0:T(128)}, u32[]{:S(2)}) copy-start(f32[16]{0:T(128)} %param.20) | copy-start | bytes 196
  14.4 4.2 %copy-start.6 = (f32[96]{0:T(128)S(1)}, f32[96]{0:T(128)}, u32[]{:S(2)}) copy-start(f32[96]{0:T(128)} %param.14) | copy-start | bytes 1156

commit v2 on v1

--- a/solution.py
+++ b/solution.py
@@ -35,13 +35,13 @@
     cache,
     owners,
     valid,
-    wa_w,
-    wb_w,
-    wd02,
-    wd1,
-    gain,
-    cbias,
-    lbias,
+    norm_gain,
+    conv_weight,
+    conv_bias,
+    down_weight,
+    down_bias,
+    latent_weight,
+    latent_bias,
     out,
     ext,
     pack_top,
@@ -59,13 +59,20 @@
     hp32,
     h32,
     vs,
+    taps,
+    wa_w,
+    wb_w,
+    wd02,
+    wd1,
+    gain,
+    cbias,
     send,
+    received,
     local_sem,
     send_sem,
     recv_sem,
     a2a_send,
     a2a_recv,
-    self_sem,
 ):
     ha, wa = lax.axis_index("ha"), lax.axis_index("wa")
     up, down = lax.rem(ha + n_ha - 1, n_ha), lax.rem(ha + 1, n_ha)
@@ -175,6 +182,89 @@
     for copy in row_copies + col_copies:
         copy.start()
 
+    lane = lax.broadcasted_iota(jnp.int32, (1, 128), 1)
+
+    @pl.loop(0, C // 4)
+    def _(g):
+        win = lanes(3 * g, 3)
+        for weight, count, at in ((conv_weight, 27, 0), (down_weight, 9, 27)):
+            x = weight[:, win].astype(F32)
+            t0, t1, t2 = (x[:, 128 * j : 128 * (j + 1)] for j in range(3))
+            parts = [
+                t0,
+                jnp.where(lane < 32, pltpu.roll(t0, 32, 1), pltpu.roll(t1, 32, 1)),
+                jnp.where(lane < 64, pltpu.roll(t1, 64, 1), pltpu.roll(t2, 64, 1)),
+                pltpu.roll(t2, 96, 1),
+            ]
+            for u in range(4):
+                taps[pl.ds(at * C + 4 * g + u, count, C)] = jnp.where(lane < C, parts[u], 0.0)
+
+    @pl.loop(0, 9)
+    def _(n):
+        w = [taps[pl.ds((3 * n + s) * C, C)] for s in range(3)]
+        zero = jnp.zeros((C, 128), F32)
+        by96 = [zero] + [pltpu.roll(x, 96, 1) for x in w]
+        by64 = [pltpu.roll(x, 64, 1) for x in w] + [zero]
+        by32 = [zero] + [pltpu.roll(x, 32, 1) for x in w]
+        w = w + [zero]
+        for s in range(4):
+            rows = pl.ds(pl.multiple_of(n * 384 + s * 96, 32), C)
+            wa_w[rows, pl.ds(0, 128)] = jnp.where(lane < 96, w[s], by96[s]).astype(BF16)
+            wa_w[rows, pl.ds(128, 128)] = jnp.where(lane < 64, by96[s], 0.0).astype(BF16)
+            one = jnp.where(lane < 64, 0.0, by64[s]).astype(BF16)
+            two = jnp.where(lane < 32, by64[s], by32[s]).astype(BF16)
+            if s < 3:
+                rows = pl.ds(pl.multiple_of(n * 384 + s * 96 + 64, 32), C)
+                wb_w[rows, pl.ds(0, 128)] = one
+                wb_w[rows, pl.ds(128, 128)] = two
+            else:
+                rows = pl.ds(pl.multiple_of(n * 384 + 352, 32), 32)
+                wb_w[rows, pl.ds(0, 128)] = one[:32]
+                wb_w[rows, pl.ds(128, 128)] = two[:32]
+                rows = pl.ds(pl.multiple_of(n * 384, 32), 64)
+                wb_w[rows, pl.ds(0, 128)] = one[32:]
+                wb_w[rows, pl.ds(128, 128)] = two[32:]
+
+    by_z = jnp.concatenate([latent_weight[...]] * QB, axis=0)
+    by_column = (((1,), (1,)), ((), ()))
+    for t in range(9):
+        tap = taps[pl.ds((27 + t) * C, C)][:, :C].astype(BF16)
+        taps[pl.ds((27 + t) * C, C)] = lax.dot_general(
+            tap, by_z, by_column, preferred_element_type=F32
+        )
+    slot_of = sum((lane >= 16 * q).astype(jnp.int32) for q in range(1, QB))
+    for r in range(3):
+        target, at = ((wd02, 0), (wd1, 0), (wd02, 128))[r]
+        target[pl.ds(0, 32), pl.ds(at, 128)] = jnp.zeros((32, 128), BF16)
+
+        @pl.loop(0, 2 * QB + 1)
+        def _(col):
+            block = jnp.zeros((C, 128), F32)
+            for s in range(3):
+                fits = (2 * slot_of + s) == col
+                block = jnp.where(fits, taps[pl.ds((27 + 3 * r + s) * C, C)], block)
+            rows = pl.ds(pl.multiple_of(32 + C * col, 32), C)
+            target[rows, pl.ds(at, 128)] = block.astype(BF16)
+
+    rest = down_bias[...]
+    pieces = []
+    for _ in range(3):
+        piece = rest.astype(BF16)
+        pieces.append(piece.astype(F32))
+        rest = rest - pieces[-1]
+    pieces = jnp.concatenate(pieces + [jnp.zeros((13, C), F32)], axis=0).astype(BF16)
+    lbias = jnp.sum(
+        lax.dot_general(pieces, by_z, by_column, preferred_element_type=F32),
+        axis=0,
+        keepdims=True,
+    ) + jnp.concatenate([latent_bias[...]] * QB, axis=1)
+
+    gain[...] = jnp.concatenate([norm_gain[...]] * 4, axis=1)
+    bias = conv_bias[...]
+    bias = jnp.concatenate([bias[:, 64:]] + [bias] * 3 + [bias[:, :64]], axis=1)
+    for j in range(3):
+        cbias[j] = bias[:, 128 * j : 128 * (j + 1)]
+
     def column_of(axis):
         index = lax.broadcasted_iota(jnp.int32, (384, 384), axis)
         return sum((index >= edge).astype(jnp.int32) for edge in (96, 192, 288))
@@ -185,7 +275,6 @@
     has_right = jnp.where(wa == n_wa - 1, 0.0, 1.0).astype(F32)
     has_above = jnp.where(ha == 0, 0.0, 1.0).astype(F32)
     has_below = jnp.where(ha == n_ha - 1, 0.0, 1.0).astype(F32)
-    lane = lax.broadcasted_iota(jnp.int32, (1, 128), 1)
 
     def activate(x):
         squares = jnp.dot((x * x).astype(BF16), ones[...], preferred_element_type=F32)
@@ -389,30 +478,29 @@
             vs[t, pl.ds(0, 16)] = both[16 * t : 16 * (t + 1), 128:]
             vs[t, pl.ds(16, 1)] = both[64 + t : 65 + t, 128:]
         shifted = jnp.concatenate([vs[t, pl.ds(1, 16)] for t in range(T)], axis=0)
-        latents.append(both[:64, :128] + mid + shifted)
-    latent = jnp.concatenate(latents[:3] + [latents[3][:, :32]], axis=1) + lbias[...]
+        latents.append(both[:64, :128] + mid + shifted + lbias)
+    latent = jnp.concatenate(latents[:3] + [latents[3][:, :32]], axis=1)
     frame_of = lax.broadcasted_iota(jnp.int32, (64, 1), 0)
     latent = jnp.where(frame_of < valid[0] * 16, latent, 0.0).astype(BF16)
 
     row = lax.broadcasted_iota(jnp.int32, (64, 64), 0)
     col = lax.broadcasted_iota(jnp.int32, (64, 64), 1)
-    by_row = jnp.broadcast_to(owners[...], (64, 64))
-    by_col = jnp.sum(jnp.where(row == col, by_row, 0), axis=0, keepdims=True)
+    by_col = jnp.broadcast_to(owners[...], (64, 64))
+    by_row = jnp.sum(jnp.where(row == col, by_col, 0), axis=1, keepdims=True)
     rank = jnp.sum(jnp.where((by_row == by_col) & (row < col), 1, 0), axis=0, keepdims=True)
-    slot = by_col * 32 + rank
+    slot = owners[...] * 32 + rank
     slots = lax.broadcasted_iota(jnp.int32, (128, 64), 0)
     selector = jnp.where(slots == slot, 1.0, 0.0).astype(BF16)
     send[...] = jnp.dot(selector, latent, preferred_element_type=F32).astype(BF16)
 
     here = pl.ds(pl.multiple_of(ha * 32, 32), 32)
-    keep = pltpu.make_async_copy(send.at[here], out.at[0, 0, 0, here], self_sem)
     copies = []
     for d in range(1, n_ha):
         target = lax.rem(ha + d, n_ha)
         copies.append(
             pltpu.make_async_remote_copy(
                 src_ref=send.at[pl.ds(pl.multiple_of(target * 32, 32), 32)],
-                dst_ref=out.at[0, 0, 0, here],
+                dst_ref=received.at[here],
                 send_sem=a2a_send.at[d - 1],
                 recv_sem=a2a_recv.at[d - 1],
                 device_id={"ha": target, "wa": wa},
@@ -421,39 +509,13 @@
         )
     for copy in copies:
         copy.start()
-    keep.start()
+    received[here] = send[here]
     for copy in row_copies + col_copies:
         copy.wait_send()
     for copy in copies:
         copy.wait()
-    keep.wait()
-
-
-def conv_matrices(conv_weight):
-    w = conv_weight.reshape(9, 3, C, C)
-    zero = jnp.zeros((9, C, C), conv_weight.dtype)
-    taps = [zero] + [w[:, s] for s in range(3)] + [zero]
-    rows = [jnp.concatenate([taps[s + 1], taps[s]], axis=2) for s in range(4)]
-    window = jnp.concatenate(rows, axis=1)
-    first = jnp.pad(window, ((0, 0), (0, 0), (0, 64)))
-    second = jnp.pad(jnp.roll(window, 64, axis=1), ((0, 0), (0, 0), (64, 0)))
-    return first.reshape(KK * 128, 256), second.reshape(KK * 128, 256)
-
-
-def down_matrices(down_weight, latent_weight):
-    dw = down_weight.reshape(9, C, C)
-    fused = jnp.einsum("kio,oz->kiz", dw, latent_weight, preferred_element_type=F32)
-    fused = fused.astype(BF16).reshape(3, 3, C, Z)
-    place = np.zeros((3, 2 * QB + 1, QB), np.float32)
-    for s in range(3):
-        for q in range(QB):
-            place[s, 2 * q + s, q] = 1.0
-    banded = jnp.einsum(
-        "scq,rsiz->rciqz", jnp.asarray(place, BF16), fused, preferred_element_type=F32
-    ).astype(BF16)
-    banded = banded.reshape(3, (2 * QB + 1) * C, QB * Z)
-    banded = jnp.pad(banded, ((0, 0), (KD - (2 * QB + 1) * C, 0), (0, 0)))
-    return jnp.concatenate([banded[0], banded[2]], axis=1), banded[1]
+    full = jnp.concatenate([received[...].astype(F32), jnp.zeros((128, 96), F32)], axis=1)
+    out[0, 0, 0] = full.T[:416].astype(BF16)
 
 
 def per_device(
@@ -471,19 +533,13 @@
     valid_frames,
     owners,
 ):
-    wa_w, wb_w = conv_matrices(conv_weight)
-    wd02, wd1 = down_matrices(down_weight, latent_weight)
-    gain = jnp.tile(norm_gain, 4).reshape(1, 384)
-    cbias = jnp.roll(jnp.tile(conv_bias, 4), 32).reshape(3, 1, 128)
-    lbias = latent_bias + jnp.sum(down_bias[:, None] * latent_weight.astype(F32), axis=0)
-    lbias = jnp.tile(lbias, TW // 2).reshape(1, TW // 2 * Z)
     vmem = pl.BlockSpec(memory_space=pltpu.VMEM)
     anyspace = pl.BlockSpec(memory_space=pl.ANY)
-    return pl.pallas_call(
+    routed = pl.pallas_call(
         functools.partial(kernel, n_ha, n_wa),
-        out_shape=jax.ShapeDtypeStruct((1, 1, 1, 128, 416), BF16),
+        out_shape=jax.ShapeDtypeStruct((1, 1, 1, 416, 128), BF16),
         in_specs=[anyspace, anyspace, vmem, pl.BlockSpec(memory_space=pltpu.SMEM)] + [vmem] * 7,
-        out_specs=anyspace,
+        out_specs=vmem,
         scratch_shapes=[
             pltpu.VMEM((6, TH, EXT * 128), BF16),
             pltpu.VMEM((16, OWN * 128), BF16),
@@ -501,13 +557,20 @@
             pltpu.VMEM((14, 8, 128), F32),
             pltpu.VMEM((41, 16, 128), BF16),
             pltpu.VMEM((T, 24, 128), F32),
+            pltpu.VMEM((36 * C, 128), F32),
+            pltpu.VMEM((KK * 128, 256), BF16),
+            pltpu.VMEM((KK * 128, 256), BF16),
+            pltpu.VMEM((KD, 256), BF16),
+            pltpu.VMEM((KD, 128), BF16),
+            pltpu.VMEM((1, 384), F32),
+            pltpu.VMEM((3, 1, 128), F32),
+            pltpu.VMEM((128, 416), BF16),
             pltpu.VMEM((128, 416), BF16),
             pltpu.SemaphoreType.DMA((2,)),
             pltpu.SemaphoreType.DMA((10,)),
             pltpu.SemaphoreType.DMA((10,)),
             pltpu.SemaphoreType.DMA((n_ha - 1,)),
             pltpu.SemaphoreType.DMA((n_ha - 1,)),
-            pltpu.SemaphoreType.DMA,
         ],
         compiler_params=pltpu.CompilerParams(
             collective_id=0, has_side_effects=True, vmem_limit_bytes=56 * 2**20
@@ -516,16 +579,17 @@
     )(
         frames,
         cache,
-        owners.reshape(64, 1),
+        owners.reshape(1, 64),
         valid_frames,
-        wa_w,
-        wb_w,
-        wd02,
-        wd1,
-        gain,
-        cbias,
-        lbias,
-    )
+        norm_gain.reshape(1, C),
+        conv_weight,
+        conv_bias.reshape(1, C),
+        down_weight,
+        down_bias.reshape(1, C),
+        latent_weight.T,
+        latent_bias.reshape(1, Z),
+    )
+    return jnp.swapaxes(routed, 3, 4)
 
 
 def solution(mesh):

time: 56.9 us -> 40.4 us (0.71)
  local copies, waits for them, and re-layouts: 14.4 us -> 1.55 us
  other arithmetic: 5.33 us -> 0 us
  Pallas kernels: 35.1 us -> 38 us
  matrix products: 1.07 us -> 0 us
    reshape x6 -> x0, local copies, waits for them, and re-layouts: 7.69 us -> none  [the longest x2 4.44 us: down_matrices(): banded = banded.reshape(3, (2 * QB + 1) * C, QB * Z)]
    concatenate x4 -> x0, other arithmetic: 5.21 us -> none  [the longest x1 2.08 us: conv_matrices(): window = jnp.concatenate(rows, axis=1)]
    pallas_call x1, Pallas kernels: 35.1 us -> 38 us  [per_device(): pl.pallas_call(functools.partial(kernel, n_ha, n_wa), out_shape=jax.Shape...]
    pallas_call x1 -> x0, local copies, waits for them, and re-layouts: 1.66 us -> none  [per_device(): pl.pallas_call(functools.partial(kernel, n_ha, n_wa), out_shape=jax.Shape...]
    pad x1 -> x0, local copies, waits for them, and re-layouts: 1.54 us -> none  [conv_matrices(): first = jnp.pad(window, ((0, 0), (0, 0), (0, 64)))]
    unnamed x16 -> x1, local copies, waits for them, and re-layouts: 0.04 us -> 1.55 us
    another operation x6 -> x0, local copies, waits for them, and re-layouts: 1.41 us -> none  [the longest x2 0.66 us: per_device(): gain = jnp.tile(norm_gain, 4).reshape(1, 384)]
    dot_general x2 -> x0, matrix products: 1.07 us -> none  [the longest x1 0.84 us: down_matrices(): jnp.einsum('scq,rsiz->rciqz', jnp.asarray(place, BF16), fused, preferred_...]
where the time goes in v2:
time: 40.4 us; the launch traced here: 40.2 us
  Pallas kernels  38 us (94%)
  local copies, waits for them, and re-layouts  1.55 us (4%)
  between operations  0.66 us (2%)
    pallas_call x1, Pallas kernels, per_device(): pl.pallas_call(functools.partial(kernel, n_ha, n_wa), out_shape=jax.Shape...  38 us
    unnamed x1, local copies, waits for them, and re-layouts  1.55 us

profile of v2, /device:TPU:0, one launch (start us, length us, event | category | flops | bytes accessed | tf_op | source)
XLA Modules:
  0.0 40.2 jit_solution(13044961013699877634)
XLA Ops:
  0.7 38.0 %encoder_step.1 = bf16[1,1,1,416,128]{4,3,2,1,0:T(8,128)(2,1)} custom-call(bf16[1,4,32,4992]{3,2,1,0:T(8,128)(2,1)} %frames.1, bf16[1,2,32,4992]{3,2,1,0:T(8,128)(2,1)} %cache.1, s32[1,64]{1,0:T(1,128)} %bitcast.9, s32[1]{0:T(128)S(6)} %copy.13.valid, f32[1,96]{1,0:T(1,128)} %bitcast.10, bf16[27,9216]{1,0:T(8,128)(2,1)} %conv_weight.1, f32[1,96]{1,0:T(1,128)} %bitcast.11, ...), custom_call_target="tpu_custom_call" | custom-call | tf_op jit(solution)/shard_map/encoder_step/pallas_call | solution.py:538
  38.7 1.5 %copy.14 = bf16[1,1,1,128,416]{3,4,2,1,0:T(8,128)(2,1)} copy(bf16[1,1,1,128,416]{3,4,2,1,0:T(8,128)(2,1)} %bitcast.7) | data formatting | bytes 212992

commit v3 on v2

v3 whole, which is shorter than its diff:
```python
import functools

import jax
import jax.numpy as jnp
import numpy as np
from jax import lax
from jax.experimental import pallas as pl
from jax.experimental.pallas import tpu as pltpu
from jax.sharding import PartitionSpec as P

EPS = 1e-06
C = 96
Z = 16
T = 4
TH = 32
TW = 52
OWN = 39
EXT = 42
FS = 48
KK = 27
QB = 8
F32 = jnp.float32
BF16 = jnp.bfloat16


def lanes(tile, count=1):
    return pl.ds(pl.multiple_of(tile * 128, 128), count * 128)


def kernel(
    n_ha,
    n_wa,
    frames,
    cache,
    owners,
    valid,
    norm_gain,
    conv_weight,
    conv_bias,
    down_weight,
    down_bias,
    latent_weight,
    latent_bias,
    out,
    ext,
    pack_top,
    pack_bot,
    above,
    below,
    act,
    xf,
    planes,
    ones,
    middle,
    hp,
    hb,
    l32,
    x32,
    hp32,
    h32,
    vs,
    conv_taps,
    down_taps,
    taps,
    wa_w,
    wb_w,
    down_w,
    gain,
    cbias,
    lbias,
    send,
    received,
    local_sem,
    send_sem,
    recv_sem,
    a2a_send,
    a2a_recv,
):
    ha, wa = lax.axis_index("ha"), lax.axis_index("wa")
    up, down = lax.rem(ha + n_ha - 1, n_ha), lax.rem(ha + 1, n_ha)
    left, right = lax.rem(wa + n_wa - 1, n_wa), lax.rem(wa + 1, n_wa)

    load_cache = pltpu.make_async_copy(
        cache.at[0], ext.at[pl.ds(0, 2), :, pl.ds(0, OWN * 128)], local_sem.at[0]
    )
    load_frames = pltpu.make_async_copy(
        frames.at[0], ext.at[pl.ds(2, T), :, pl.ds(0, OWN * 128)], local_sem.at[1]
    )
    load_conv = pltpu.make_async_copy(conv_weight, conv_taps, local_sem.at[2])
    load_down = pltpu.make_async_copy(down_weight, down_taps, local_sem.at[3])
    loads = [load_cache, load_frames, load_conv, load_down]
    for load in loads:
        load.start()

    barrier = pltpu.get_barrier_semaphore()
    greeted = [
        {"ha": up, "wa": wa},
        {"ha": down, "wa": wa},
        {"ha": ha, "wa": left},
        {"ha": ha, "wa": right},
        {"ha": up, "wa": left},
        {"ha": up, "wa": right},
        {"ha": down, "wa": left},
        {"ha": down, "wa": right},
        {"ha": lax.rem(ha + 2, n_ha), "wa": wa},
    ]
    for device in greeted:
        pl.semaphore_signal(
            barrier, inc=1, device_id=device, device_id_type=pl.DeviceIdType.MESH
        )

    def remote(src, dst, index, device):
        return pltpu.make_async_remote_copy(
            src_ref=src,
            dst_ref=dst,
            send_sem=send_sem.at[index],
            recv_sem=recv_sem.at[index],
            device_id=device,
            device_id_type=pl.DeviceIdType.MESH,
        )

    load_cache.wait()
    load_frames.wait()

    sub = lax.broadcasted_iota(jnp.int32, (8, 384), 0)

    @pl.loop(0, OWN // 3)
    def _(g):
        win = lanes(3 * g, 3)
        tops = [ext[f, pl.ds(0, 16), win].astype(F32) for f in range(6)]
        bots = [ext[f, pl.ds(16, 16), win].astype(F32) for f in range(6)]
        lo = jnp.zeros((8, 384), F32)
        hi = jnp.zeros((8, 384), F32)
        for t in range(T):
            lo = jnp.where(sub == t, tops[2 + t][0:1], lo)
            lo = jnp.where(sub == 4 + t, tops[2 + t][1:2], lo)
        for t in range(2):
            hi = jnp.where(sub == t, tops[t][0:1], hi)
            hi = jnp.where(sub == 2 + t, tops[t][1:2], hi)
        pack_top[:, win] = jnp.concatenate([lo, hi], axis=0).astype(BF16)
        lo = jnp.zeros((8, 384), F32)
        for t in range(T):
            lo = jnp.where(sub == t, bots[2 + t][15:16], lo)
        for t in range(2):
            lo = jnp.where(sub == 4 + t, bots[t][15:16], lo)
        pack_bot[:, win] = jnp.concatenate([lo, jnp.zeros((8, 384), F32)], axis=0).astype(BF16)

    pl.semaphore_wait(barrier, len(greeted))

    own = pl.ds(0, OWN * 128)
    first, last = pl.ds(0, 256), pl.ds((OWN - 1) * 128, 128)
    from_right, from_left = pl.ds(OWN * 128, 256), pl.ds((OWN + 2) * 128, 128)
    row_copies = [
        remote(pack_top, below.at[:, own], 0, {"ha": up, "wa": wa}),
        remote(pack_bot, above.at[:, own], 1, {"ha": down, "wa": wa}),
        remote(pack_top.at[:, first], below.at[:, from_right], 2, {"ha": up, "wa": left}),
        remote(pack_top.at[:, last], below.at[:, from_left], 3, {"ha": up, "wa": right}),
        remote(pack_bot.at[:, first], above.at[:, from_right], 4, {"ha": down, "wa": left}),
        remote(pack_bot.at[:, last], above.at[:, from_left], 5, {"ha": down, "wa": right}),
    ]
    col_copies = [
        remote(
            frames.at[0, :, :, first],
            ext.at[pl.ds(2, T), :, from_right],
            6,
            {"ha": ha, "wa": left},
        ),
        remote(
            cache.at[0, :, :, first],
            ext.at[pl.ds(0, 2), :, from_right],
            7,
            {"ha": ha, "wa": left},
        ),
        remote(
            frames.at[0, :, :, last],
            ext.at[pl.ds(2, T), :, from_left],
            8,
            {"ha": ha, "wa": right},
        ),
        remote(
            cache.at[0, :, :, last],
            ext.at[pl.ds(0, 2), :, from_left],
            9,
            {"ha": ha, "wa": right},
        ),
    ]
    for copy in row_copies + col_copies:
        copy.start()

    lane = lax.broadcasted_iota(jnp.int32, (1, 128), 1)

    gain[...] = jnp.concatenate([norm_gain[...]] * 4, axis=1) * (0.5 * C**0.5)

    def column_of(axis):
        index = lax.broadcasted_iota(jnp.int32, (384, 384), axis)
        return sum((index >= edge).astype(jnp.int32) for edge in (96, 192, 288))

    ones[...] = jnp.where(column_of(0) == column_of(1), 1.0, 0.0).astype(BF16)

    has_left = jnp.where(wa == 0, 0.0, 1.0).astype(F32)
    has_right = jnp.where(wa == n_wa - 1, 0.0, 1.0).astype(F32)
    has_above = jnp.where(ha == 0, 0.0, 1.0).astype(F32)
    has_below = jnp.where(ha == n_ha - 1, 0.0, 1.0).astype(F32)

    def activate(x):
        squares = jnp.dot((x * x).astype(BF16), ones[...], preferred_element_type=F32)
        u = x * lax.rsqrt(squares + C * EPS) * gain[...]
        return u + u * jnp.tanh(u)

    def halo_mask(x):
        return jnp.concatenate([x[:, :256] * has_right, x[:, 256:] * has_left], axis=1)

    def groups(gs, edge):
        xs, earlier = [], []
        for g in gs:
            win = lanes(3 * g, 3)
            x = ext[pl.ds(2, T), :, win].reshape(T * TH, 384).astype(F32)
            old = ext[pl.ds(0, 2), :, win].reshape(2 * TH, 384).astype(F32)
            if edge and g == 13:
                x, old = halo_mask(x), halo_mask(old)
            xs.append(x)
            earlier.append(old)
        activated = activate(jnp.concatenate(xs, axis=0))
        for n, g in enumerate(gs):
            before = ext[pl.ds(2, T), :, lanes(jnp.maximum(3 * g - 1, 0))]
            before = pltpu.roll(before.reshape(T * TH, 128).astype(F32), 32, 1)
            for j in range(1 if edge and g == 13 else 3):
                here = pltpu.roll(xs[n][:, 128 * j : 128 * (j + 1)], 32, 1)
                xf[3 * g + j + 1] = jnp.where(lane < 32, before, here)
                before = here
            for j in range(3):
                part = slice(128 * j, 128 * (j + 1))
                tile = 3 * g + j
                for f in range(6):
                    if f < 2:
                        value = earlier[n][f * TH : (f + 1) * TH, part]
                    else:
                        at = n * T * TH + (f - 2) * TH
                        value = activated[at : at + TH, part]
                    act[tile, pl.ds(f * FS + 8, TH)] = value
                for f in range(6):
                    d1 = act[tile, pl.ds(f * FS + 8, 16, 2)]
                    d2 = act[tile, pl.ds(f * FS + 9, 16, 2)]
                    planes[1, tile + 1, pl.ds(f * 16, 16)] = (d1 + d2).astype(BF16)
                    planes[2, tile + 1, pl.ds(f * 16, 16)] = (d2 - d1).astype(BF16)

    @pl.loop(0, 4)
    def _(n):
        groups([3 * n, 3 * n + 1, 3 * n + 2], False)

    load_conv.wait()
    load_down.wait()

    @pl.loop(0, C // 4)
    def _(g):
        win = lanes(3 * g, 3)
        for weight, count, at in ((conv_taps, 27, 0), (down_taps, 9, 27)):
            x = weight[:, win].astype(F32)
            t0, t1, t2 = (x[:, 128 * j : 128 * (j + 1)] for j in range(3))
            parts = [
                t0,
                jnp.where(lane < 32, pltpu.roll(t0, 32, 1), pltpu.roll(t1, 32, 1)),
                jnp.where(lane < 64, pltpu.roll(t1, 64, 1), pltpu.roll(t2, 64, 1)),
                pltpu.roll(t2, 96, 1),
            ]
            for u in range(4):
                taps[pl.ds(at * C + 4 * g + u, count, C)] = jnp.where(lane < C, parts[u], 0.0)

    @pl.loop(0, 3)
    def _(a):
        for m in range(4):
            w = []
            for s in range(3):
                g0, g1, g2 = (taps[pl.ds((9 * a + 3 * r + s) * C, C)] for r in range(3))
                if m == 0:
                    w.append(g0)
                elif m == 1:
                    w.append(0.5 * (g0 + g2 + g1))
                elif m == 2:
                    w.append(0.5 * (g0 + g2 - g1))
                else:
                    w.append(g2)
            zero = jnp.zeros((C, 128), F32)
            by96 = [zero] + [pltpu.roll(x, 96, 1) for x in w]
            by64 = [pltpu.roll(x, 64, 1) for x in w] + [zero]
            by32 = [zero] + [pltpu.roll(x, 32, 1) for x in w]
            w = w + [zero]
            at = m * 1152 + a * 384
            for s in range(4):
                rows = pl.ds(pl.multiple_of(at + s * 96, 32), C)
                wa_w[rows, pl.ds(0, 128)] = jnp.where(lane < 96, w[s], by96[s]).astype(BF16)
                wa_w[rows, pl.ds(128, 128)] = jnp.where(lane < 64, by96[s], 0.0).astype(BF16)
                one = jnp.where(lane < 64, 0.0, by64[s]).astype(BF16)
                two = jnp.where(lane < 32, by64[s], by32[s]).astype(BF16)
                if s < 3:
                    rows = pl.ds(pl.multiple_of(at + s * 96 + 64, 32), C)
                    wb_w[rows, pl.ds(0, 128)] = one
                    wb_w[rows, pl.ds(128, 128)] = two
                else:
                    rows = pl.ds(pl.multiple_of(at + 352, 32), 32)
                    wb_w[rows, pl.ds(0, 128)] = one[:32]
                    wb_w[rows, pl.ds(128, 128)] = two[:32]
                    rows = pl.ds(pl.multiple_of(at, 32), 64)
                    wb_w[rows, pl.ds(0, 128)] = one[32:]
                    wb_w[rows, pl.ds(128, 128)] = two[32:]

    by_z = jnp.concatenate([latent_weight[...]] * QB, axis=0)
    by_column = (((1,), (1,)), ((), ()))
    fused = lax.dot_general(
        taps[pl.ds(27 * C, 9 * C)][:, :C].astype(BF16),
        by_z,
        by_column,
        preferred_element_type=F32,
    )
    down_w[...] = jnp.zeros((1024, 128), BF16)
    for r in range(3):
        first = (0, 0, 2)[r]
        for col in range(5):
            block = jnp.zeros((C, 128), F32)
            for s in range(3):
                q = col - s
                if q in (0, 2):
                    tap = fused[(3 * r + s) * C : (3 * r + s + 1) * C]
                    place = first + q // 2
                    block = jnp.where((lane >= 16 * place) & (lane < 16 * (place + 1)), tap, block)
            rows = pl.ds((512 if r == 1 else 0) + 32 + C * col, C)
            if r == 2:
                block = block + down_w[rows].astype(F32)
            down_w[rows] = block.astype(BF16)

    rest = down_bias[...]
    pieces = []
    for _ in range(3):
        piece = rest.astype(BF16)
        pieces.append(piece.astype(F32))
        rest = rest - pieces[-1]
    pieces = jnp.concatenate(pieces + [jnp.zeros((13, C), F32)], axis=0).astype(BF16)
    lbias_row = jnp.sum(
        lax.dot_general(pieces, by_z, by_column, preferred_element_type=F32),
        axis=0,
        keepdims=True,
    ) + jnp.concatenate([latent_bias[...]] * QB, axis=1)

    lbias[...] = lbias_row
    bias = conv_bias[...]
    bias = jnp.concatenate([bias[:, 64:]] + [bias] * 3 + [bias[:, :64]], axis=1)
    for j in range(3):
        cbias[j] = bias[:, 128 * j : 128 * (j + 1)]

    for copy in col_copies:
        copy.wait_recv()
    groups([12, 13], True)
    for copy in row_copies:
        copy.wait_recv()

    @pl.loop(0, 2)
    def _(half):
        his, los = [], []
        for n in range(7):
            g = 7 * half + n
            win = lanes(3 * g, 3)
            hi = below[:, win].astype(F32) * has_below
            lo = above[:, win].astype(F32) * has_above
            if n == 6:
                right_on = jnp.where(half == 1, has_right, 1.0)
                left_on = jnp.where(half == 1, has_left, 1.0)
                hi, lo = (
                    jnp.concatenate([x[:, :256] * right_on, x[:, 256:] * left_on], axis=1)
                    for x in (hi, lo)
                )
            his.append(hi)
            los.append(lo)
        activated = activate(
            jnp.concatenate([x[:8] for pair in zip(his, los) for x in pair], axis=0)
        )
        before = below[:, lanes(jnp.maximum(21 * half - 1, 0))].astype(F32) * has_below
        before = pltpu.roll(before[:8], 32, 1)
        for n in range(7):
            for j in range(3):
                part = slice(128 * j, 128 * (j + 1))
                tile = 21 * half + 3 * n + j
                new = activated[16 * n : 16 * (n + 1), part]
                act[tile, pl.ds(2 * FS + 40, T, FS)] = new[0:4]
                act[tile, pl.ds(2 * FS + 41, T, FS)] = new[4:8]
                act[tile, pl.ds(2 * FS + 7, T, FS)] = new[8:12]
                act[tile, pl.ds(40, 2, FS)] = his[n][8:10, part]
                act[tile, pl.ds(41, 2, FS)] = his[n][10:12, part]
                act[tile, pl.ds(7, 2, FS)] = los[n][4:6, part]
                here = pltpu.roll(his[n][:8, part], 32, 1)
                x32[tile + 1] = jnp.where(lane < 32, before, here)
                before = here

    @pl.loop(0, EXT // 3)
    def _(g):
        for j in range(3):
            tile = 3 * g + j
            for f in range(6):
                d0, d1, d2, d3 = (act[tile, pl.ds(f * FS + 7 + r, 16, 2)] for r in range(4))
                planes[0, tile + 1, pl.ds(f * 16, 16)] = (d0 - d2).astype(BF16)
                planes[3, tile + 1, pl.ds(f * 16, 16)] = (d1 - d3).astype(BF16)

            for a in range(3):
                d0, d1, d2 = (act[tile, pl.ds(a * FS + 39 + r, T, FS)] for r in range(3))
                l32[tile, a, pl.ds(0, T)] = d0 - d2
                l32[tile, 3 + a, pl.ds(0, T)] = d1 + d2
                l32[tile, 6 + a, pl.ds(0, T)] = d2 - d1

    @pl.loop(0, 4)
    def _(plane):
        planes[plane, 0] = planes[plane, EXT]
        for i in range(14):
            later = planes[plane, 3 * i + 2]
            sooner = planes[plane, 41 if i == 0 else 3 * i - 1]
            planes[plane, EXT + 1 + i] = jnp.where(lane < 64, later, sooner)

    for i in range(14):
        sooner = 40 if i == 0 else 3 * i - 2
        for n in range(9):
            l32[EXT + i, n] = jnp.where(lane < 64, l32[3 * i + 1, n], l32[sooner, n])

    def tile_a(k, j):
        return 3 * k + j + 1

    def tile_b(i, j):
        return EXT + 1 + i if j == 0 else 3 * i + j - 1

    def conv(base, count, tile_of, weights):
        def product(m):
            rows = []
            for w in range(count):
                pieces = [
                    planes[m, tile_of(base + w, j), pl.ds(a * 16, 64)]
                    for a in range(3)
                    for j in range(3)
                ]
                rows.append(jnp.concatenate(pieces, axis=1))
            return jnp.dot(
                jnp.concatenate(rows, axis=0),
                weights[pl.ds(m * 1152, 1152)],
                preferred_element_type=F32,
            )

        middle[0] = product(1)
        middle[1] = product(2)
        even = product(0) + (middle[0] + middle[1])
        return even, (middle[0] - middle[1]) - product(3)

    @pl.loop(0, 2)
    def _(step):
        base = step * 6
        both = conv(base, 7, tile_a, wa_w)
        for parity in range(2):
            for w in range(7):
                k = base + w
                part = both[parity][64 * w : 64 * (w + 1)]
                x = xf[3 * k + 2, pl.ds(parity, 64, 2)]
                hb[parity, 3 * k + 2] = (x + part[:, :128] + cbias[1]).astype(BF16)
                hp[parity, k + 1] = part[:, 128:]

    cut_right = jnp.where((lane >= 32) & (wa == n_wa - 1), 0.0, 1.0).astype(F32)

    @pl.loop(0, 2)
    def _(step):
        base = step * 7
        both = conv(base, 7, tile_b, wb_w)
        for parity in range(2):
            for w in range(7):
                i = base + w
                part = both[parity][64 * w : 64 * (w + 1)]
                x = xf[3 * i, pl.ds(parity, 64, 2)]
                hb[parity, 3 * i] = (x + part[:, :128] + hp[parity, i] + cbias[2]).astype(BF16)
                x = xf[3 * i + 1, pl.ds(parity, 64, 2)]
                h = x + part[:, 128:] + cbias[0]
                if w == 6:
                    h = h * jnp.where(i == 13, cut_right, 1.0)
                hb[parity, 3 * i + 1] = h.astype(BF16)

    def tile32_a(k, j):
        return 3 * k + j

    def tile32_b(i, j):
        return EXT + i if j == 0 else (41 if i == 0 and j == 1 else 3 * i + j - 2)

    def conv32(tile_of, weights):
        rows = []
        for w in range(14):
            pieces = [l32[tile_of(w, j), n] for n in range(9) for j in range(3)]
            rows.append(jnp.concatenate(pieces, axis=1))
        lhs = jnp.concatenate(rows, axis=0).astype(BF16)
        return jnp.dot(lhs, weights[pl.ds(0, KK * 128)], preferred_element_type=F32)

    acc = conv32(tile32_a, wa_w)
    for k in range(13):
        part = acc[8 * k : 8 * (k + 1)]
        h32[3 * k + 2] = (x32[3 * k + 2] + part[:, :128] + cbias[1]) * has_below
        hp32[k + 1] = part[:, 128:]
    acc = conv32(tile32_b, wb_w)
    for i in range(14):
        part = acc[8 * i : 8 * (i + 1)]
        if i:
            h = x32[3 * i] + part[:, :128] + hp32[i] + cbias[2]
            h32[3 * i] = h * has_below
        h = (x32[3 * i + 1] + part[:, 128:] + cbias[0]) * has_below
        h32[3 * i + 1] = h * cut_right if i == 13 else h

    rows = []
    for k in range(13):
        pieces = [hb[parity, 3 * k + j + 1] for parity in range(2) for j in range(4)]
        rows.append(jnp.concatenate(pieces, axis=1))
    main = jnp.dot(jnp.concatenate(rows, axis=0), down_w[...], preferred_element_type=F32)
    rows = [
        jnp.concatenate([h32[3 * min(k, 12) + j + 1] for j in range(4)], axis=1) for k in range(14)
    ]
    extra = jnp.dot(
        jnp.concatenate(rows, axis=0).astype(BF16),
        down_w[pl.ds(0, 512)],
        preferred_element_type=F32,
    )
    blocks = []
    for b in range(4):
        here = jnp.zeros((64, 128), F32)
        over = jnp.zeros((64, 128), F32)
        over32 = jnp.zeros((8, 128), F32)
        for j in range(4 if b < 3 else 1):
            k = 4 * b + j
            fits = (lane >= 32 * j) & (lane < 32 * (j + 1))
            part = main[64 * k : 64 * (k + 1)]
            turned = pltpu.roll(part, 32 * j, 1) if j else part
            here = jnp.where(fits, turned, here)
            turned = pltpu.roll(part, (32 * j + 96) % 128, 1) if j != 1 else part
            over = jnp.where(fits, turned, over)
            part = extra[8 * k : 8 * (k + 1)]
            turned = pltpu.roll(part, (32 * j + 96) % 128, 1) if j != 1 else part
            over32 = jnp.where(fits, turned, over32)
        for t in range(T):
            vs[t, pl.ds(0, 16)] = over[16 * t : 16 * (t + 1)]
            vs[t, pl.ds(16, 1)] = over32[t : t + 1]
        shifted = jnp.concatenate([vs[t, pl.ds(1, 16)] for t in range(T)], axis=0)
        blocks.append(here + shifted + lbias[...])
    latent = jnp.concatenate(blocks[:3] + [blocks[3][:, :32]], axis=1)
    frame_of = lax.broadcasted_iota(jnp.int32, (64, 1), 0)
    latent = jnp.where(frame_of < valid[0] * 16, latent, 0.0).astype(BF16)

    row = lax.broadcasted_iota(jnp.int32, (64, 64), 0)
    col = lax.broadcasted_iota(jnp.int32, (64, 64), 1)
    by_col = jnp.broadcast_to(owners[...], (64, 64))
    by_row = jnp.sum(jnp.where(row == col, by_col, 0), axis=1, keepdims=True)
    rank = jnp.sum(jnp.where((by_row == by_col) & (row < col), 1, 0), axis=0, keepdims=True)
    slot = owners[...] * 32 + rank
    slots = lax.broadcasted_iota(jnp.int32, (128, 64), 0)
    selector = jnp.where(slots == slot, 1.0, 0.0).astype(BF16)
    send[...] = jnp.dot(selector, latent, preferred_element_type=F32).astype(BF16)

    here = pl.ds(pl.multiple_of(ha * 32, 32), 32)
    copies = []
    for d in range(1, n_ha):
        target = lax.rem(ha + d, n_ha)
        copies.append(
            pltpu.make_async_remote_copy(
                src_ref=send.at[pl.ds(pl.multiple_of(target * 32, 32), 32)],
                dst_ref=received.at[here],
                send_sem=a2a_send.at[d - 1],
                recv_sem=a2a_recv.at[d - 1],
                device_id={"ha": target, "wa": wa},
                device_id_type=pl.DeviceIdType.MESH,
            )
        )
    for copy in copies:
        copy.start()
    received[here] = send[here]
    for copy in row_copies + col_copies:
        copy.wait_send()
    for copy in copies:
        copy.wait()
    full = jnp.concatenate([received[...].astype(F32), jnp.zeros((128, 96), F32)], axis=1)
    out[0, 0, 0] = full.T[:416].astype(BF16)


def per_device(
    n_ha,
    n_wa,
    frames,
    cache,
    norm_gain,
    conv_weight,
    conv_bias,
    down_weight,
    down_bias,
    latent_weight,
    latent_bias,
    valid_frames,
    owners,
):
    vmem = pl.BlockSpec(memory_space=pltpu.VMEM)
    hbm = pl.BlockSpec(memory_space=pltpu.HBM)
    routed = pl.pallas_call(
        functools.partial(kernel, n_ha, n_wa),
        out_shape=jax.ShapeDtypeStruct((1, 1, 1, 416, 128), BF16),
        in_specs=[hbm, hbm, vmem, pl.BlockSpec(memory_space=pltpu.SMEM), vmem, hbm, vmem, hbm]
        + [vmem] * 3,
        out_specs=vmem,
        scratch_shapes=[
            pltpu.VMEM((6, TH, EXT * 128), BF16),
            pltpu.VMEM((16, OWN * 128), BF16),
            pltpu.VMEM((16, OWN * 128), BF16),
            pltpu.VMEM((16, EXT * 128), BF16),
            pltpu.VMEM((16, EXT * 128), BF16),
            pltpu.VMEM((EXT, 6 * FS, 128), F32),
            pltpu.VMEM((41, T * TH, 128), F32),
            pltpu.VMEM((4, EXT + 15, 96, 128), BF16),
            pltpu.VMEM((384, 384), BF16),
            pltpu.VMEM((2, 448, 256), F32),
            pltpu.VMEM((2, 14, 64, 128), F32),
            pltpu.VMEM((2, 41, 64, 128), BF16),
            pltpu.VMEM((EXT + 14, 9, 8, 128), F32),
            pltpu.VMEM((EXT + 1, 8, 128), F32),
            pltpu.VMEM((14, 8, 128), F32),
            pltpu.VMEM((41, 8, 128), F32),
            pltpu.VMEM((T, 24, 128), F32),
            pltpu.VMEM((27, C * C), BF16),
            pltpu.VMEM((9, C * C), BF16),
            pltpu.VMEM((36 * C, 128), F32),
            pltpu.VMEM((4608, 256), BF16),
            pltpu.VMEM((4608, 256), BF16),
            pltpu.VMEM((1024, 128), BF16),
            pltpu.VMEM((1, 384), F32),
            pltpu.VMEM((3, 1, 128), F32),
            pltpu.VMEM((1, 128), F32),
            pltpu.VMEM((128, 416), BF16),
            pltpu.VMEM((128, 416), BF16),
            pltpu.SemaphoreType.DMA((4,)),
            pltpu.SemaphoreType.DMA((10,)),
            pltpu.SemaphoreType.DMA((10,)),
            pltpu.SemaphoreType.DMA((n_ha - 1,)),
            pltpu.SemaphoreType.DMA((n_ha - 1,)),
        ],
        compiler_params=pltpu.CompilerParams(
            collective_id=0, has_side_effects=True, vmem_limit_bytes=56 * 2**20
        ),
        name="encoder_step",
    )(
        frames,
        cache,
        owners.reshape(1, 64),
        valid_frames,
        norm_gain.reshape(1, C),
        conv_weight,
        conv_bias.reshape(1, C),
        down_weight,
        down_bias.reshape(1, C),
        latent_weight.T,
        latent_bias.reshape(1, Z),
    )
    return jnp.swapaxes(routed, 3, 4)


def solution(mesh):
    in_specs = (
        P("ba", None, "ha", "wa"),
        P("ba", None, "ha", "wa"),
        P(),
        P(),
        P(),
        P(),
        P(),
        P(),
        P(),
        P("ba"),
        P("ba", "ha", "wa", None, None),
    )
    out_specs = P("ba", "ha", "wa", None, None)
    return jax.shard_map(
        functools.partial(per_device, mesh.shape["ha"], mesh.shape["wa"]),
        mesh=mesh,
        in_specs=in_specs,
        out_specs=out_specs,
        check_vma=False,
    )
```

time: 40.4 us -> 32.5 us (0.80)
  Pallas kernels: 38 us -> 30.1 us
    pallas_call x1, Pallas kernels: 38 us -> 30.1 us  [per_device(): pl.pallas_call(functools.partial(kernel, n_ha, n_wa), out_shape=jax.Shape...]
where the time goes in v3:
time: 32.5 us; the launch traced here: 32.3 us
  Pallas kernels  30.1 us (93%)
  local copies, waits for them, and re-layouts  1.55 us (5%)
  between operations  0.66 us (2%)
    pallas_call x1, Pallas kernels, per_device(): pl.pallas_call(functools.partial(kernel, n_ha, n_wa), out_shape=jax.Shape...  30.1 us
    unnamed x1, local copies, waits for them, and re-layouts  1.55 us

profile of v3, /device:TPU:0, one launch (start us, length us, event | category | flops | bytes accessed | tf_op | source)
XLA Modules:
  0.0 32.3 jit_solution(4439724977283450148)
XLA Ops:
  0.7 30.1 %encoder_step.1 = bf16[1,1,1,416,128]{4,3,2,1,0:T(8,128)(2,1)} custom-call(bf16[1,4,32,4992]{3,2,1,0:T(8,128)(2,1)} %frames.1, bf16[1,2,32,4992]{3,2,1,0:T(8,128)(2,1)} %cache.1, s32[1,64]{1,0:T(1,128)} %bitcast.9, s32[1]{0:T(128)S(6)} %copy.13.valid, f32[1,96]{1,0:T(1,128)} %bitcast.10, bf16[27,9216]{1,0:T(8,128)(2,1)} %conv_weight.1, f32[1,96]{1,0:T(1,128)} %bitcast.11, ...), custom_call_target="tpu_custom_call" | custom-call | tf_op jit(solution)/shard_map/encoder_step/pallas_call | solution.py:596
  30.7 1.5 %copy.14 = bf16[1,1,1,128,416]{3,4,2,1,0:T(8,128)(2,1)} copy(bf16[1,1,1,128,416]{3,4,2,1,0:T(8,128)(2,1)} %bitcast.7) | data formatting | bytes 212992

commit v4 on v3

--- a/solution.py
+++ b/solution.py
@@ -49,7 +49,8 @@
     below,
     act,
     xf,
-    planes,
+    inner,
+    outer,
     ones,
     middle,
     hp,
@@ -124,7 +125,7 @@
 
     sub = lax.broadcasted_iota(jnp.int32, (8, 384), 0)
 
-    @pl.loop(0, OWN // 3)
+    @pl.loop(0, OWN // 3, unroll=True)
     def _(g):
         win = lanes(3 * g, 3)
         tops = [ext[f, pl.ds(0, 16), win].astype(F32) for f in range(6)]
@@ -191,67 +192,10 @@
 
     gain[...] = jnp.concatenate([norm_gain[...]] * 4, axis=1) * (0.5 * C**0.5)
 
-    def column_of(axis):
-        index = lax.broadcasted_iota(jnp.int32, (384, 384), axis)
-        return sum((index >= edge).astype(jnp.int32) for edge in (96, 192, 288))
-
-    ones[...] = jnp.where(column_of(0) == column_of(1), 1.0, 0.0).astype(BF16)
-
-    has_left = jnp.where(wa == 0, 0.0, 1.0).astype(F32)
-    has_right = jnp.where(wa == n_wa - 1, 0.0, 1.0).astype(F32)
-    has_above = jnp.where(ha == 0, 0.0, 1.0).astype(F32)
-    has_below = jnp.where(ha == n_ha - 1, 0.0, 1.0).astype(F32)
-
-    def activate(x):
-        squares = jnp.dot((x * x).astype(BF16), ones[...], preferred_element_type=F32)
-        u = x * lax.rsqrt(squares + C * EPS) * gain[...]
-        return u + u * jnp.tanh(u)
-
-    def halo_mask(x):
-        return jnp.concatenate([x[:, :256] * has_right, x[:, 256:] * has_left], axis=1)
-
-    def groups(gs, edge):
-        xs, earlier = [], []
-        for g in gs:
-            win = lanes(3 * g, 3)
-            x = ext[pl.ds(2, T), :, win].reshape(T * TH, 384).astype(F32)
-            old = ext[pl.ds(0, 2), :, win].reshape(2 * TH, 384).astype(F32)
-            if edge and g == 13:
-                x, old = halo_mask(x), halo_mask(old)
-            xs.append(x)
-            earlier.append(old)
-        activated = activate(jnp.concatenate(xs, axis=0))
-        for n, g in enumerate(gs):
-            before = ext[pl.ds(2, T), :, lanes(jnp.maximum(3 * g - 1, 0))]
-            before = pltpu.roll(before.reshape(T * TH, 128).astype(F32), 32, 1)
-            for j in range(1 if edge and g == 13 else 3):
-                here = pltpu.roll(xs[n][:, 128 * j : 128 * (j + 1)], 32, 1)
-                xf[3 * g + j + 1] = jnp.where(lane < 32, before, here)
-                before = here
-            for j in range(3):
-                part = slice(128 * j, 128 * (j + 1))
-                tile = 3 * g + j
-                for f in range(6):
-                    if f < 2:
-                        value = earlier[n][f * TH : (f + 1) * TH, part]
-                    else:
-                        at = n * T * TH + (f - 2) * TH
-                        value = activated[at : at + TH, part]
-                    act[tile, pl.ds(f * FS + 8, TH)] = value
-                for f in range(6):
-                    d1 = act[tile, pl.ds(f * FS + 8, 16, 2)]
-                    d2 = act[tile, pl.ds(f * FS + 9, 16, 2)]
-                    planes[1, tile + 1, pl.ds(f * 16, 16)] = (d1 + d2).astype(BF16)
-                    planes[2, tile + 1, pl.ds(f * 16, 16)] = (d2 - d1).astype(BF16)
-
-    @pl.loop(0, 4)
-    def _(n):
-        groups([3 * n, 3 * n + 1, 3 * n + 2], False)
-
     load_conv.wait()
     load_down.wait()
 
-    @pl.loop(0, C // 4)
+    @pl.loop(0, C // 4, unroll=4)
     def _(g):
         win = lanes(3 * g, 3)
         for weight, count, at in ((conv_taps, 27, 0), (down_taps, 9, 27)):
@@ -347,6 +291,63 @@
     for j in range(3):
         cbias[j] = bias[:, 128 * j : 128 * (j + 1)]
 
+    def column_of(axis):
+        index = lax.broadcasted_iota(jnp.int32, (384, 384), axis)
+        return sum((index >= edge).astype(jnp.int32) for edge in (96, 192, 288))
+
+    ones[...] = jnp.where(column_of(0) == column_of(1), 1.0, 0.0).astype(BF16)
+
+    has_left = jnp.where(wa == 0, 0.0, 1.0).astype(F32)
+    has_right = jnp.where(wa == n_wa - 1, 0.0, 1.0).astype(F32)
+    has_above = jnp.where(ha == 0, 0.0, 1.0).astype(F32)
+    has_below = jnp.where(ha == n_ha - 1, 0.0, 1.0).astype(F32)
+
+    def activate(x):
+        squares = jnp.dot((x * x).astype(BF16), ones[...], preferred_element_type=F32)
+        u = x * lax.rsqrt(squares + C * EPS) * gain[...]
+        return u + u * jnp.tanh(u)
+
+    def halo_mask(x):
+        return jnp.concatenate([x[:, :256] * has_right, x[:, 256:] * has_left], axis=1)
+
+    def groups(gs, edge):
+        xs, earlier = [], []
+        for g in gs:
+            win = lanes(3 * g, 3)
+            x = ext[pl.ds(2, T), :, win].reshape(T * TH, 384).astype(F32)
+            old = ext[pl.ds(0, 2), :, win].reshape(2 * TH, 384).astype(F32)
+            if edge and g == 13:
+                x, old = halo_mask(x), halo_mask(old)
+            xs.append(x)
+            earlier.append(old)
+        activated = activate(jnp.concatenate(xs, axis=0))
+        for n, g in enumerate(gs):
+            before = ext[pl.ds(2, T), :, lanes(jnp.maximum(3 * g - 1, 0))]
+            before = pltpu.roll(before.reshape(T * TH, 128).astype(F32), 32, 1)
+            for j in range(1 if edge and g == 13 else 3):
+                here = pltpu.roll(xs[n][:, 128 * j : 128 * (j + 1)], 32, 1)
+                xf[3 * g + j + 1] = jnp.where(lane < 32, before, here)
+                before = here
+            for j in range(3):
+                part = slice(128 * j, 128 * (j + 1))
+                tile = 3 * g + j
+                for f in range(6):
+                    if f < 2:
+                        value = earlier[n][f * TH : (f + 1) * TH, part]
+                    else:
+                        at = n * T * TH + (f - 2) * TH
+                        value = activated[at : at + TH, part]
+                    act[tile, pl.ds(f * FS + 8, TH)] = value
+                for f in range(6):
+                    d1 = act[tile, pl.ds(f * FS + 8, 16, 2)]
+                    d2 = act[tile, pl.ds(f * FS + 9, 16, 2)]
+                    inner[0, tile + 1, pl.ds(f * 16, 16)] = (d1 + d2).astype(BF16)
+                    inner[1, tile + 1, pl.ds(f * 16, 16)] = (d2 - d1).astype(BF16)
+
+    @pl.loop(0, 4)
+    def _(n):
+        groups([3 * n, 3 * n + 1, 3 * n + 2], False)
+
     for copy in col_copies:
         copy.wait_recv()
     groups([12, 13], True)
@@ -390,65 +391,70 @@
                 x32[tile + 1] = jnp.where(lane < 32, before, here)
                 before = here
 
-    @pl.loop(0, EXT // 3)
-    def _(g):
-        for j in range(3):
-            tile = 3 * g + j
-            for f in range(6):
-                d0, d1, d2, d3 = (act[tile, pl.ds(f * FS + 7 + r, 16, 2)] for r in range(4))
-                planes[0, tile + 1, pl.ds(f * 16, 16)] = (d0 - d2).astype(BF16)
-                planes[3, tile + 1, pl.ds(f * 16, 16)] = (d1 - d3).astype(BF16)
-
-            for a in range(3):
-                d0, d1, d2 = (act[tile, pl.ds(a * FS + 39 + r, T, FS)] for r in range(3))
-                l32[tile, a, pl.ds(0, T)] = d0 - d2
-                l32[tile, 3 + a, pl.ds(0, T)] = d1 + d2
-                l32[tile, 6 + a, pl.ds(0, T)] = d2 - d1
-
-    @pl.loop(0, 4)
-    def _(plane):
-        planes[plane, 0] = planes[plane, EXT]
-        for i in range(14):
-            later = planes[plane, 3 * i + 2]
-            sooner = planes[plane, 41 if i == 0 else 3 * i - 1]
-            planes[plane, EXT + 1 + i] = jnp.where(lane < 64, later, sooner)
-
-    for i in range(14):
-        sooner = 40 if i == 0 else 3 * i - 2
-        for n in range(9):
-            l32[EXT + i, n] = jnp.where(lane < 64, l32[3 * i + 1, n], l32[sooner, n])
-
     def tile_a(k, j):
         return 3 * k + j + 1
 
     def tile_b(i, j):
         return EXT + 1 + i if j == 0 else 3 * i + j - 1
 
-    def conv(base, count, tile_of, weights):
-        def product(m):
-            rows = []
-            for w in range(count):
-                pieces = [
-                    planes[m, tile_of(base + w, j), pl.ds(a * 16, 64)]
-                    for a in range(3)
-                    for j in range(3)
-                ]
-                rows.append(jnp.concatenate(pieces, axis=1))
-            return jnp.dot(
-                jnp.concatenate(rows, axis=0),
-                weights[pl.ds(m * 1152, 1152)],
-                preferred_element_type=F32,
-            )
-
-        middle[0] = product(1)
-        middle[1] = product(2)
-        even = product(0) + (middle[0] + middle[1])
-        return even, (middle[0] - middle[1]) - product(3)
+    def join(planes):
+        @pl.loop(0, 2)
+        def _(m):
+            planes[m, 0] = planes[m, EXT]
+            for i in range(14):
+                later = planes[m, 3 * i + 2]
+                sooner = planes[m, 41 if i == 0 else 3 * i - 1]
+                planes[m, EXT + 1 + i] = jnp.where(lane < 64, later, sooner)
+
+    def product(planes, m, at, base, tile_of, weights):
+        rows = []
+        for w in range(7):
+            pieces = [
+                planes[m, tile_of(base + w, j), pl.ds(a * 16, 64)]
+                for a in range(3)
+                for j in range(3)
+            ]
+            rows.append(jnp.concatenate(pieces, axis=1))
+        return jnp.dot(
+            jnp.concatenate(rows, axis=0),
+            weights[pl.ds(at * 1152, 1152)],
+            preferred_element_type=F32,
+        )
+
+    def outer_planes(tile):
+        for f in range(6):
+            d0, d1, d2, d3 = (act[tile, pl.ds(f * FS + 7 + r, 16, 2)] for r in range(4))
+            outer[0, tile + 1, pl.ds(f * 16, 16)] = (d0 - d2).astype(BF16)
+            outer[1, tile + 1, pl.ds(f * 16, 16)] = (d1 - d3).astype(BF16)
+
+        for a in range(3):
+            d0, d1, d2 = (act[tile, pl.ds(a * FS + 39 + r, T, FS)] for r in range(3))
+            l32[tile, a, pl.ds(0, T)] = d0 - d2
+            l32[tile, 3 + a, pl.ds(0, T)] = d1 + d2
+            l32[tile, 6 + a, pl.ds(0, T)] = d2 - d1
+
+    join(inner)
+
+    @pl.loop(0, 2)
+    def _(step):
+        for n in range(21):
+            outer_planes(21 * step + n)
+        for m in range(2):
+            middle[step, 0, m] = product(inner, m, 1 + m, 6 * step, tile_a, wa_w)
+            middle[step, 1, m] = product(inner, m, 1 + m, 7 * step, tile_b, wb_w)
+
+    join(outer)
+    cut_right = jnp.where((lane >= 32) & (wa == n_wa - 1), 0.0, 1.0).astype(F32)
+
+    def both_rows(step, side, base, tile_of, weights):
+        one, two = middle[step, side, 0], middle[step, side, 1]
+        even = product(outer, 0, 0, base, tile_of, weights) + (one + two)
+        return even, (one - two) - product(outer, 1, 3, base, tile_of, weights)
 
     @pl.loop(0, 2)
     def _(step):
         base = step * 6
-        both = conv(base, 7, tile_a, wa_w)
+        both = both_rows(step, 0, base, tile_a, wa_w)
         for parity in range(2):
             for w in range(7):
                 k = base + w
@@ -456,13 +462,8 @@
                 x = xf[3 * k + 2, pl.ds(parity, 64, 2)]
                 hb[parity, 3 * k + 2] = (x + part[:, :128] + cbias[1]).astype(BF16)
                 hp[parity, k + 1] = part[:, 128:]
-
-    cut_right = jnp.where((lane >= 32) & (wa == n_wa - 1), 0.0, 1.0).astype(F32)
-
-    @pl.loop(0, 2)
-    def _(step):
         base = step * 7
-        both = conv(base, 7, tile_b, wb_w)
+        both = both_rows(step, 1, base, tile_b, wb_w)
         for parity in range(2):
             for w in range(7):
                 i = base + w
@@ -474,6 +475,11 @@
                 if w == 6:
                     h = h * jnp.where(i == 13, cut_right, 1.0)
                 hb[parity, 3 * i + 1] = h.astype(BF16)
+
+    for i in range(14):
+        sooner = 40 if i == 0 else 3 * i - 2
+        for n in range(9):
+            l32[EXT + i, n] = jnp.where(lane < 64, l32[3 * i + 1, n], l32[sooner, n])
 
     def tile32_a(k, j):
         return 3 * k + j
@@ -607,9 +613,10 @@
             pltpu.VMEM((16, EXT * 128), BF16),
             pltpu.VMEM((EXT, 6 * FS, 128), F32),
             pltpu.VMEM((41, T * TH, 128), F32),
-            pltpu.VMEM((4, EXT + 15, 96, 128), BF16),
+            pltpu.VMEM((2, EXT + 15, 96, 128), BF16),
+            pltpu.VMEM((2, EXT + 15, 96, 128), BF16),
             pltpu.VMEM((384, 384), BF16),
-            pltpu.VMEM((2, 448, 256), F32),
+            pltpu.VMEM((2, 2, 2, 448, 256), F32),
             pltpu.VMEM((2, 14, 64, 128), F32),
             pltpu.VMEM((2, 41, 64, 128), BF16),
             pltpu.VMEM((EXT + 14, 9, 8, 128), F32),

time: 32.5 us -> 31.3 us (0.963)
  Pallas kernels: 30.1 us -> 28.9 us
    pallas_call x1, Pallas kernels: 30.1 us -> 28.9 us  [per_device(): pl.pallas_call(functools.partial(kernel, n_ha, n_wa), out_shape=jax.Shape...]
where the time goes in v4:
time: 31.3 us; the launch traced here: 31.1 us
  Pallas kernels  28.9 us (92%)
  local copies, waits for them, and re-layouts  1.55 us (5%)
  between operations  0.66 us (2%)
    pallas_call x1, Pallas kernels, per_device(): pl.pallas_call(functools.partial(kernel, n_ha, n_wa), out_shape=jax.Shape...  28.9 us
    unnamed x1, local copies, waits for them, and re-layouts  1.55 us

profile of v4, /device:TPU:0, one launch (start us, length us, event | category | flops | bytes accessed | tf_op | source)
XLA Modules:
  0.0 31.1 jit_solution(10700668736568117545)
XLA Ops:
  0.7 28.9 %encoder_step.1 = bf16[1,1,1,416,128]{4,3,2,1,0:T(8,128)(2,1)} custom-call(bf16[1,4,32,4992]{3,2,1,0:T(8,128)(2,1)} %frames.1, bf16[1,2,32,4992]{3,2,1,0:T(8,128)(2,1)} %cache.1, s32[1,64]{1,0:T(1,128)} %bitcast.9, s32[1]{0:T(128)S(6)} %copy.13.valid, f32[1,96]{1,0:T(1,128)} %bitcast.10, bf16[27,9216]{1,0:T(8,128)(2,1)} %conv_weight.1, f32[1,96]{1,0:T(1,128)} %bitcast.11, ...), custom_call_target="tpu_custom_call" | custom-call | tf_op jit(solution)/shard_map/encoder_step/pallas_call | solution.py:602
  29.6 1.5 %copy.14 = bf16[1,1,1,128,416]{3,4,2,1,0:T(8,128)(2,1)} copy(bf16[1,1,1,128,416]{3,4,2,1,0:T(8,128)(2,1)} %bitcast.7) | data formatting | bytes 212992

commit v5 on v4

--- a/solution.py
+++ b/solution.py
@@ -16,7 +16,6 @@
 TW = 52
 OWN = 39
 EXT = 42
-FS = 48
 KK = 27
 QB = 8
 F32 = jnp.float32
@@ -41,16 +40,16 @@
     down_bias,
     latent_weight,
     latent_bias,
+    mixer,
     out,
     ext,
     pack_top,
     pack_bot,
     above,
     below,
-    act,
+    stacked,
     xf,
-    inner,
-    outer,
+    planes,
     ones,
     middle,
     hp,
@@ -62,6 +61,8 @@
     vs,
     conv_taps,
     down_taps,
+    swap_conv,
+    swap_down,
     taps,
     wa_w,
     wb_w,
@@ -195,20 +196,49 @@
     load_conv.wait()
     load_down.wait()
 
-    @pl.loop(0, C // 4, unroll=4)
-    def _(g):
-        win = lanes(3 * g, 3)
-        for weight, count, at in ((conv_taps, 27, 0), (down_taps, 9, 27)):
-            x = weight[:, win].astype(F32)
-            t0, t1, t2 = (x[:, 128 * j : 128 * (j + 1)] for j in range(3))
-            parts = [
-                t0,
-                jnp.where(lane < 32, pltpu.roll(t0, 32, 1), pltpu.roll(t1, 32, 1)),
-                jnp.where(lane < 64, pltpu.roll(t1, 64, 1), pltpu.roll(t2, 64, 1)),
-                pltpu.roll(t2, 96, 1),
-            ]
-            for u in range(4):
-                taps[pl.ds(at * C + 4 * g + u, count, C)] = jnp.where(lane < C, parts[u], 0.0)
+    def swap(taps_log, count_log):
+        row = lax.broadcasted_iota(jnp.int32, (256, 256), 0)
+        col = lax.broadcasted_iota(jnp.int32, (256, 256), 1)
+        source = ((row & ((1 << count_log) - 1)) << taps_log) + (row >> count_log)
+        return jnp.where(col == source, 1.0, 0.0).astype(BF16)
+
+    swap_conv[...] = swap(5, 3)
+    swap_down[...] = swap(4, 4)
+
+    def channels(weight, count, rows, tile):
+        x = weight[:, lanes(tile, 3)].astype(F32)
+        x = jnp.concatenate([x, jnp.zeros((rows - count, 384), F32)], axis=0)
+        t0, t1, t2 = (x[:, 128 * j : 128 * (j + 1)] for j in range(3))
+        parts = [
+            t0,
+            jnp.where(lane < 32, pltpu.roll(t0, 32, 1), pltpu.roll(t1, 32, 1)),
+            jnp.where(lane < 64, pltpu.roll(t1, 64, 1), pltpu.roll(t2, 64, 1)),
+            pltpu.roll(t2, 96, 1),
+        ]
+        return [jnp.where(lane < C, part, 0.0) for part in parts]
+
+    @pl.loop(0, 6)
+    def _(n):
+        parts = [x for g in range(4) for x in channels(conv_taps, 27, 32, 12 * n + 3 * g)]
+        pair = [jnp.concatenate(parts[8 * b : 8 * (b + 1)], axis=0) for b in range(2)]
+        swapped = jnp.dot(
+            swap_conv[...],
+            jnp.concatenate(pair, axis=1).astype(BF16),
+            preferred_element_type=F32,
+        )
+        for tap in range(27):
+            for b in range(2):
+                at = pl.multiple_of(tap * C + 16 * n + 8 * b, 8)
+                taps[pl.ds(at, 8)] = swapped[8 * tap : 8 * (tap + 1), 128 * b : 128 * (b + 1)]
+        parts = [x for g in range(4) for x in channels(down_taps, 9, 16, 12 * n + 3 * g)]
+        swapped = jnp.dot(
+            swap_down[...],
+            jnp.concatenate(parts, axis=0).astype(BF16),
+            preferred_element_type=F32,
+        )
+        for tap in range(9):
+            at = pl.multiple_of((27 + tap) * C + 16 * n, 8)
+            taps[pl.ds(at, 16)] = swapped[16 * tap : 16 * (tap + 1)]
 
     @pl.loop(0, 3)
     def _(a):
@@ -311,16 +341,17 @@
         return jnp.concatenate([x[:, :256] * has_right, x[:, 256:] * has_left], axis=1)
 
     def groups(gs, edge):
-        xs, earlier = [], []
+        xs = []
         for g in gs:
             win = lanes(3 * g, 3)
             x = ext[pl.ds(2, T), :, win].reshape(T * TH, 384).astype(F32)
-            old = ext[pl.ds(0, 2), :, win].reshape(2 * TH, 384).astype(F32)
+            old = ext[pl.ds(0, 2), :, win].reshape(2 * TH, 384)
             if edge and g == 13:
-                x, old = halo_mask(x), halo_mask(old)
+                x, old = halo_mask(x), halo_mask(old.astype(F32)).astype(BF16)
             xs.append(x)
-            earlier.append(old)
-        activated = activate(jnp.concatenate(xs, axis=0))
+            for j in range(3):
+                stacked[3 * g + j, pl.ds(0, 2 * TH)] = old[:, 128 * j : 128 * (j + 1)]
+        activated = activate(jnp.concatenate(xs, axis=0)).astype(BF16)
         for n, g in enumerate(gs):
             before = ext[pl.ds(2, T), :, lanes(jnp.maximum(3 * g - 1, 0))]
             before = pltpu.roll(before.reshape(T * TH, 128).astype(F32), 32, 1)
@@ -329,20 +360,9 @@
                 xf[3 * g + j + 1] = jnp.where(lane < 32, before, here)
                 before = here
             for j in range(3):
-                part = slice(128 * j, 128 * (j + 1))
-                tile = 3 * g + j
-                for f in range(6):
-                    if f < 2:
-                        value = earlier[n][f * TH : (f + 1) * TH, part]
-                    else:
-                        at = n * T * TH + (f - 2) * TH
-                        value = activated[at : at + TH, part]
-                    act[tile, pl.ds(f * FS + 8, TH)] = value
-                for f in range(6):
-                    d1 = act[tile, pl.ds(f * FS + 8, 16, 2)]
-                    d2 = act[tile, pl.ds(f * FS + 9, 16, 2)]
-                    inner[0, tile + 1, pl.ds(f * 16, 16)] = (d1 + d2).astype(BF16)
-                    inner[1, tile + 1, pl.ds(f * 16, 16)] = (d2 - d1).astype(BF16)
+                stacked[3 * g + j, pl.ds(2 * TH, T * TH)] = activated[
+                    n * T * TH : (n + 1) * T * TH, 128 * j : 128 * (j + 1)
+                ]
 
     @pl.loop(0, 4)
     def _(n):
@@ -381,12 +401,11 @@
                 part = slice(128 * j, 128 * (j + 1))
                 tile = 21 * half + 3 * n + j
                 new = activated[16 * n : 16 * (n + 1), part]
-                act[tile, pl.ds(2 * FS + 40, T, FS)] = new[0:4]
-                act[tile, pl.ds(2 * FS + 41, T, FS)] = new[4:8]
-                act[tile, pl.ds(2 * FS + 7, T, FS)] = new[8:12]
-                act[tile, pl.ds(40, 2, FS)] = his[n][8:10, part]
-                act[tile, pl.ds(41, 2, FS)] = his[n][10:12, part]
-                act[tile, pl.ds(7, 2, FS)] = los[n][4:6, part]
+                low = jnp.concatenate([new[:8], his[n][8:, part]], axis=0)
+                stacked[tile, pl.ds(6 * TH, 16)] = low.astype(BF16)
+                high = jnp.where(sub[:, :128] < 4, new[8:], los[n][:8, part])
+                high = jnp.concatenate([high, jnp.zeros((8, 128), F32)], axis=0)
+                stacked[tile, pl.ds(6 * TH + 16, 16)] = high.astype(BF16)
                 here = pltpu.roll(his[n][:8, part], 32, 1)
                 x32[tile + 1] = jnp.where(lane < 32, before, here)
                 before = here
@@ -397,8 +416,8 @@
     def tile_b(i, j):
         return EXT + 1 + i if j == 0 else 3 * i + j - 1
 
-    def join(planes):
-        @pl.loop(0, 2)
+    def join():
+        @pl.loop(0, 4)
         def _(m):
             planes[m, 0] = planes[m, EXT]
             for i in range(14):
@@ -406,7 +425,7 @@
                 sooner = planes[m, 41 if i == 0 else 3 * i - 1]
                 planes[m, EXT + 1 + i] = jnp.where(lane < 64, later, sooner)
 
-    def product(planes, m, at, base, tile_of, weights):
+    def product(m, base, tile_of, weights):
         rows = []
         for w in range(7):
             pieces = [
@@ -417,44 +436,34 @@
             rows.append(jnp.concatenate(pieces, axis=1))
         return jnp.dot(
             jnp.concatenate(rows, axis=0),
-            weights[pl.ds(at * 1152, 1152)],
+            weights[pl.ds(m * 1152, 1152)],
             preferred_element_type=F32,
         )
 
-    def outer_planes(tile):
-        for f in range(6):
-            d0, d1, d2, d3 = (act[tile, pl.ds(f * FS + 7 + r, 16, 2)] for r in range(4))
-            outer[0, tile + 1, pl.ds(f * 16, 16)] = (d0 - d2).astype(BF16)
-            outer[1, tile + 1, pl.ds(f * 16, 16)] = (d1 - d3).astype(BF16)
-
-        for a in range(3):
-            d0, d1, d2 = (act[tile, pl.ds(a * FS + 39 + r, T, FS)] for r in range(3))
-            l32[tile, a, pl.ds(0, T)] = d0 - d2
-            l32[tile, 3 + a, pl.ds(0, T)] = d1 + d2
-            l32[tile, 6 + a, pl.ds(0, T)] = d2 - d1
-
-    join(inner)
-
-    @pl.loop(0, 2)
-    def _(step):
-        for n in range(21):
-            outer_planes(21 * step + n)
-        for m in range(2):
-            middle[step, 0, m] = product(inner, m, 1 + m, 6 * step, tile_a, wa_w)
-            middle[step, 1, m] = product(inner, m, 1 + m, 7 * step, tile_b, wb_w)
-
-    join(outer)
+    @pl.loop(0, EXT // 2)
+    def _(q):
+        both = jnp.concatenate([stacked[2 * q], stacked[2 * q + 1]], axis=1)
+        rows = jnp.dot(mixer[...], both, preferred_element_type=F32)
+        for h in range(2):
+            part = rows[:, 128 * h : 128 * (h + 1)]
+            for m in range(4):
+                planes[m, 2 * q + h + 1] = part[96 * m : 96 * (m + 1)].astype(BF16)
+            l32[2 * q + h] = part[384:].reshape(9, 8, 128)
+
+    join()
     cut_right = jnp.where((lane >= 32) & (wa == n_wa - 1), 0.0, 1.0).astype(F32)
 
-    def both_rows(step, side, base, tile_of, weights):
-        one, two = middle[step, side, 0], middle[step, side, 1]
-        even = product(outer, 0, 0, base, tile_of, weights) + (one + two)
-        return even, (one - two) - product(outer, 1, 3, base, tile_of, weights)
+    def both_rows(side, base, tile_of, weights):
+        middle[side, 0] = product(1, base, tile_of, weights)
+        middle[side, 1] = product(2, base, tile_of, weights)
+        one, two = middle[side, 0], middle[side, 1]
+        even = product(0, base, tile_of, weights) + (one + two)
+        return even, (one - two) - product(3, base, tile_of, weights)
 
     @pl.loop(0, 2)
     def _(step):
         base = step * 6
-        both = both_rows(step, 0, base, tile_a, wa_w)
+        both = both_rows(0, base, tile_a, wa_w)
         for parity in range(2):
             for w in range(7):
                 k = base + w
@@ -463,7 +472,7 @@
                 hb[parity, 3 * k + 2] = (x + part[:, :128] + cbias[1]).astype(BF16)
                 hp[parity, k + 1] = part[:, 128:]
         base = step * 7
-        both = both_rows(step, 1, base, tile_b, wb_w)
+        both = both_rows(1, base, tile_b, wb_w)
         for parity in range(2):
             for w in range(7):
                 i = base + w
@@ -582,6 +591,36 @@
     out[0, 0, 0] = full.T[:416].astype(BF16)
 
 
+def row_mixer():
+    def at(f, h):
+        if 0 <= h < TH:
+            return f * TH + h
+        if h < 0:
+            return 6 * TH + 16 + (4 + f if f < 2 else f - 2)
+        return 6 * TH + (8 + 2 * (h - TH) + f if f < 2 else 4 * (h - TH) + f - 2)
+
+    def terms(m, h):
+        d = [h - 1, h, h + 1, h + 2]
+        return ((d[0], 1, d[2], -1), (d[1], 1, d[2], 1), (d[2], 1, d[1], -1), (d[1], 1, d[3], -1))[m]
+
+    mixer = np.zeros((384 + 72, 6 * TH + 32), np.float32)
+
+    def put(row, f, m, h):
+        one, sign, two, other = terms(m, h)
+        mixer[row, at(f, one)] += sign
+        mixer[row, at(f, two)] += other
+
+    for m in range(4):
+        for f in range(6):
+            for p in range(16):
+                put(96 * m + 16 * f + p, f, m, 2 * p)
+    for m in range(3):
+        for a in range(3):
+            for t in range(T):
+                put(384 + 8 * (3 * m + a) + t, a + t, m, TH)
+    return mixer
+
+
 def per_device(
     n_ha,
     n_wa,
@@ -603,7 +642,7 @@
         functools.partial(kernel, n_ha, n_wa),
         out_shape=jax.ShapeDtypeStruct((1, 1, 1, 416, 128), BF16),
         in_specs=[hbm, hbm, vmem, pl.BlockSpec(memory_space=pltpu.SMEM), vmem, hbm, vmem, hbm]
-        + [vmem] * 3,
+        + [vmem] * 4,
         out_specs=vmem,
         scratch_shapes=[
             pltpu.VMEM((6, TH, EXT * 128), BF16),
@@ -611,12 +650,11 @@
             pltpu.VMEM((16, OWN * 128), BF16),
             pltpu.VMEM((16, EXT * 128), BF16),
             pltpu.VMEM((16, EXT * 128), BF16),
-            pltpu.VMEM((EXT, 6 * FS, 128), F32),
+            pltpu.VMEM((EXT, 6 * TH + 32, 128), BF16),
             pltpu.VMEM((41, T * TH, 128), F32),
-            pltpu.VMEM((2, EXT + 15, 96, 128), BF16),
-            pltpu.VMEM((2, EXT + 15, 96, 128), BF16),
+            pltpu.VMEM((4, EXT + 15, 96, 128), BF16),
             pltpu.VMEM((384, 384), BF16),
-            pltpu.VMEM((2, 2, 2, 448, 256), F32),
+            pltpu.VMEM((2, 2, 448, 256), F32),
             pltpu.VMEM((2, 14, 64, 128), F32),
             pltpu.VMEM((2, 41, 64, 128), BF16),
             pltpu.VMEM((EXT + 14, 9, 8, 128), F32),
@@ -626,6 +664,8 @@
             pltpu.VMEM((T, 24, 128), F32),
             pltpu.VMEM((27, C * C), BF16),
             pltpu.VMEM((9, C * C), BF16),
+            pltpu.VMEM((256, 256), BF16),
+            pltpu.VMEM((256, 256), BF16),
             pltpu.VMEM((36 * C, 128), F32),
             pltpu.VMEM((4608, 256), BF16),
             pltpu.VMEM((4608, 256), BF16),
@@ -642,7 +682,7 @@
             pltpu.SemaphoreType.DMA((n_ha - 1,)),
         ],
         compiler_params=pltpu.CompilerParams(
-            collective_id=0, has_side_effects=True, vmem_limit_bytes=56 * 2**20
+            collective_id=0, has_side_effects=True, vmem_limit_bytes=54784 * 2**10
         ),
         name="encoder_step",
     )(
@@ -657,6 +697,7 @@
         down_bias.reshape(1, C),
         latent_weight.T,
         latent_bias.reshape(1, Z),
+        jnp.asarray(row_mixer(), BF16),
     )
     return jnp.swapaxes(routed, 3, 4)
 

time: 31.3 us -> 37.6 us (1.20)
  local copies, waits for them, and re-layouts: 1.55 us -> 5.54 us
  Pallas kernels: 28.9 us -> 31.1 us
    unnamed x1 -> x15, local copies, waits for them, and re-layouts: 1.55 us -> 5.54 us
    pallas_call x1, Pallas kernels: 28.9 us -> 31.1 us  [per_device(): pl.pallas_call(functools.partial(kernel, n_ha, n_wa), out_shape=jax.Shape...]
where the time goes in v5:
time: 37.6 us; the launch traced here: 37.3 us
  Pallas kernels  31.1 us (83%)
  local copies, waits for them, and re-layouts  5.54 us (15%)
  between operations  0.67 us (2%)
    pallas_call x1, Pallas kernels, per_device(): pl.pallas_call(functools.partial(kernel, n_ha, n_wa), out_shape=jax.Shape...  31.1 us
    unnamed x15, local copies, waits for them, and re-layouts  5.54 us

profile of v5, /device:TPU:0, one launch (start us, length us, event | category | flops | bytes accessed | tf_op | source)
XLA Modules:
  0.0 37.3 jit_solution(3556774328634024560)
XLA Ops:
  0.7 0.0 copy-start
  0.7 0.9 %copy-done = bf16[456,224]{1,0:T(8,128)(2,1)S(1)} copy-done((bf16[456,224]{1,0:T(8,128)(2,1)S(1)}, bf16[456,224]{1,0:T(8,128)(2,1)}, u32[]{:S(2)}) %copy-start) | copy-done | bytes 204312
  1.6 0.0 copy-start.1
  1.6 0.7 %copy-done.1 = bf16[96,16]{0,1:T(8,128)(2,1)S(1)} copy-done((bf16[96,16]{0,1:T(8,128)(2,1)S(1)}, bf16[96,16]{0,1:T(8,128)(2,1)}, u32[]{:S(2)}) %copy-start.1) | copy-done | bytes 3096
  2.3 0.0 copy-start.2
  2.3 0.7 %copy-done.2 = s32[1,1,1,64,1]{3,4,2,1,0:T(1,128)S(1)} copy-done((s32[1,1,1,64,1]{3,4,2,1,0:T(1,128)S(1)}, s32[1,1,1,64,1]{3,4,2,1,0:T(1,128)}, u32[]{:S(2)}) %copy-start.2) | copy-done | bytes 280
  2.9 0.0 copy-start.3
  2.9 0.7 %copy-done.3 = f32[96]{0:T(128)S(1)} copy-done((f32[96]{0:T(128)S(1)}, f32[96]{0:T(128)}, u32[]{:S(2)}) %copy-start.3) | copy-done | bytes 408
  3.6 0.0 copy-start.4
  3.6 0.7 %copy-done.4 = f32[96]{0:T(128)S(1)} copy-done((f32[96]{0:T(128)S(1)}, f32[96]{0:T(128)}, u32[]{:S(2)}) %copy-start.4) | copy-done | bytes 408
  4.3 0.0 copy-start.5
  4.3 0.7 %copy-done.5 = f32[96]{0:T(128)S(1)} copy-done((f32[96]{0:T(128)S(1)}, f32[96]{0:T(128)}, u32[]{:S(2)}) %copy-start.5) | copy-done | bytes 408
  4.9 0.0 copy-start.6
  4.9 0.7 %copy-done.6 = f32[16]{0:T(128)S(1)} copy-done((f32[16]{0:T(128)S(1)}, f32[16]{0:T(128)}, u32[]{:S(2)}) %copy-start.6) | copy-done | bytes 88
  5.6 31.1 %encoder_step.1 = bf16[1,1,1,416,128]{4,3,2,1,0:T(8,128)(2,1)S(1)} custom-call(bf16[1,4,32,4992]{3,2,1,0:T(8,128)(2,1)} %frames.1, bf16[1,2,32,4992]{3,2,1,0:T(8,128)(2,1)} %cache.1, s32[1,64]{1,0:T(1,128)S(1)} %bitcast.9, s32[1]{0:T(128)S(6)} %copy.14.valid, f32[1,96]{1,0:T(1,128)S(1)} %bitcast.10, bf16[27,9216]{1,0:T(8,128)(2,1)} %conv_weight.1, ...), custom_call_target="tpu_custom_call" | custom-call | tf_op jit(solution)/shard_map/encoder_step/pallas_call | solution.py:641
  36.7 0.6 %copy.15 = bf16[1,1,1,128,416]{3,4,2,1,0:T(8,128)(2,1)} copy(bf16[1,1,1,128,416]{3,4,2,1,0:T(8,128)(2,1)S(1)} %bitcast.7) | data formatting | bytes 212992
Async XLA Ops:
  0.7 0.9 %copy-start = (bf16[456,224]{1,0:T(8,128)(2,1)S(1)}, bf16[456,224]{1,0:T(8,128)(2,1)}, u32[]{:S(2)}) copy-start(bf16[456,224]{1,0:T(8,128)(2,1)} %constant.2.clone.mixer) | copy-start | bytes 612868
  1.6 0.7 %copy-start.1 = (bf16[96,16]{0,1:T(8,128)(2,1)S(1)}, bf16[96,16]{0,1:T(8,128)(2,1)}, u32[]{:S(2)}) copy-start(bf16[96,16]{0,1:T(8,128)(2,1)} %param.19) | copy-start | bytes 9220
  2.3 0.7 %copy-start.2 = (s32[1,1,1,64,1]{3,4,2,1,0:T(1,128)S(1)}, s32[1,1,1,64,1]{3,4,2,1,0:T(1,128)}, u32[]{:S(2)}) copy-start(s32[1,1,1,64,1]{3,4,2,1,0:T(1,128)} %param.22) | copy-start | bytes 772
  2.9 0.7 %copy-start.3 = (f32[96]{0:T(128)S(1)}, f32[96]{0:T(128)}, u32[]{:S(2)}) copy-start(f32[96]{0:T(128)} %param.14) | copy-start | bytes 1156
  3.6 0.7 %copy-start.4 = (f32[96]{0:T(128)S(1)}, f32[96]{0:T(128)}, u32[]{:S(2)}) copy-start(f32[96]{0:T(128)} %param.16) | copy-start | bytes 1156
  4.3 0.7 %copy-start.5 = (f32[96]{0:T(128)S(1)}, f32[96]{0:T(128)}, u32[]{:S(2)}) copy-start(f32[96]{0:T(128)} %param.18) | copy-start | bytes 1156
  4.9 0.7 %copy-start.6 = (f32[16]{0:T(128)S(1)}, f32[16]{0:T(128)}, u32[]{:S(2)}) copy-start(f32[16]{0:T(128)} %param.20) | copy-start | bytes 196

commit v6 on v4

--- a/solution.py
+++ b/solution.py
@@ -32,16 +32,23 @@
     n_wa,
     frames,
     cache,
+    owners_in,
+    valid,
+    norm_gain_in,
+    conv_weight,
+    conv_bias_in,
+    down_weight,
+    down_bias_in,
+    latent_weight_in,
+    latent_bias_in,
+    out,
     owners,
-    valid,
     norm_gain,
-    conv_weight,
     conv_bias,
-    down_weight,
     down_bias,
     latent_weight,
     latent_bias,
-    out,
+    selector,
     ext,
     pack_top,
     pack_bot,
@@ -70,7 +77,6 @@
     cbias,
     lbias,
     send,
-    received,
     local_sem,
     send_sem,
     recv_sem,
@@ -81,16 +87,31 @@
     up, down = lax.rem(ha + n_ha - 1, n_ha), lax.rem(ha + 1, n_ha)
     left, right = lax.rem(wa + n_wa - 1, n_wa), lax.rem(wa + 1, n_wa)
 
-    load_cache = pltpu.make_async_copy(
-        cache.at[0], ext.at[pl.ds(0, 2), :, pl.ds(0, OWN * 128)], local_sem.at[0]
-    )
-    load_frames = pltpu.make_async_copy(
-        frames.at[0], ext.at[pl.ds(2, T), :, pl.ds(0, OWN * 128)], local_sem.at[1]
-    )
-    load_conv = pltpu.make_async_copy(conv_weight, conv_taps, local_sem.at[2])
-    load_down = pltpu.make_async_copy(down_weight, down_taps, local_sem.at[3])
-    loads = [load_cache, load_frames, load_conv, load_down]
-    for load in loads:
+    own = pl.ds(0, OWN * 128)
+    loads = [
+        pltpu.make_async_copy(frames.at[0, t], ext.at[2 + t, :, own], local_sem.at[t])
+        for t in range(T)
+    ]
+    loads += [
+        pltpu.make_async_copy(cache.at[0, t], ext.at[t, :, own], local_sem.at[T + t])
+        for t in range(2)
+    ]
+    small = [
+        pltpu.make_async_copy(source, target, local_sem.at[8 + n])
+        for n, (source, target) in enumerate(
+            (
+                (owners_in, owners),
+                (norm_gain_in, norm_gain),
+                (conv_bias_in, conv_bias),
+                (down_bias_in, down_bias),
+                (latent_weight_in, latent_weight),
+                (latent_bias_in, latent_bias),
+            )
+        )
+    ]
+    load_conv = pltpu.make_async_copy(conv_weight, conv_taps, local_sem.at[6])
+    load_down = pltpu.make_async_copy(down_weight, down_taps, local_sem.at[7])
+    for load in loads + small + [load_conv, load_down]:
         load.start()
 
     barrier = pltpu.get_barrier_semaphore()
@@ -120,8 +141,46 @@
             device_id_type=pl.DeviceIdType.MESH,
         )
 
-    load_cache.wait()
-    load_frames.wait()
+    def column_of(axis):
+        index = lax.broadcasted_iota(jnp.int32, (384, 384), axis)
+        return sum((index >= edge).astype(jnp.int32) for edge in (96, 192, 288))
+
+    ones[...] = jnp.where(column_of(0) == column_of(1), 1.0, 0.0).astype(BF16)
+
+    for load in small:
+        load.wait()
+    by_column = (((1,), (1,)), ((), ()))
+    by_z = jnp.concatenate([latent_weight[...]] * QB, axis=0)
+    rest = down_bias[...]
+    pieces = []
+    for _ in range(3):
+        piece = rest.astype(BF16)
+        pieces.append(piece.astype(F32))
+        rest = rest - pieces[-1]
+    pieces = jnp.concatenate(pieces + [jnp.zeros((13, C), F32)], axis=0).astype(BF16)
+    lbias_row = jnp.sum(
+        lax.dot_general(pieces, by_z, by_column, preferred_element_type=F32),
+        axis=0,
+        keepdims=True,
+    ) + jnp.concatenate([latent_bias[...]] * QB, axis=1)
+
+    lbias[...] = lbias_row
+    bias = conv_bias[...]
+    bias = jnp.concatenate([bias[:, 64:]] + [bias] * 3 + [bias[:, :64]], axis=1)
+    for j in range(3):
+        cbias[j] = bias[:, 128 * j : 128 * (j + 1)]
+
+    gain[...] = jnp.concatenate([norm_gain[...]] * 4, axis=1) * (0.5 * C**0.5)
+    row = lax.broadcasted_iota(jnp.int32, (64, 64), 0)
+    col = lax.broadcasted_iota(jnp.int32, (64, 64), 1)
+    by_col = jnp.broadcast_to(owners[...], (64, 64))
+    by_row = jnp.sum(jnp.where(row == col, by_col, 0), axis=1, keepdims=True)
+    rank = jnp.sum(jnp.where((by_row == by_col) & (row < col), 1, 0), axis=0, keepdims=True)
+    slot = owners[...] * 32 + rank
+    slots = lax.broadcasted_iota(jnp.int32, (128, 64), 0)
+    selector[...] = jnp.where(slots == slot, 1.0, 0.0).astype(BF16)
+    for load in loads:
+        load.wait()
 
     sub = lax.broadcasted_iota(jnp.int32, (8, 384), 0)
 
@@ -148,7 +207,6 @@
 
     pl.semaphore_wait(barrier, len(greeted))
 
-    own = pl.ds(0, OWN * 128)
     first, last = pl.ds(0, 256), pl.ds((OWN - 1) * 128, 128)
     from_right, from_left = pl.ds(OWN * 128, 256), pl.ds((OWN + 2) * 128, 128)
     row_copies = [
@@ -190,7 +248,6 @@
 
     lane = lax.broadcasted_iota(jnp.int32, (1, 128), 1)
 
-    gain[...] = jnp.concatenate([norm_gain[...]] * 4, axis=1) * (0.5 * C**0.5)
 
     load_conv.wait()
     load_down.wait()
@@ -248,8 +305,6 @@
                     wb_w[rows, pl.ds(0, 128)] = one[32:]
                     wb_w[rows, pl.ds(128, 128)] = two[32:]
 
-    by_z = jnp.concatenate([latent_weight[...]] * QB, axis=0)
-    by_column = (((1,), (1,)), ((), ()))
     fused = lax.dot_general(
         taps[pl.ds(27 * C, 9 * C)][:, :C].astype(BF16),
         by_z,
@@ -271,31 +326,6 @@
             if r == 2:
                 block = block + down_w[rows].astype(F32)
             down_w[rows] = block.astype(BF16)
-
-    rest = down_bias[...]
-    pieces = []
-    for _ in range(3):
-        piece = rest.astype(BF16)
-        pieces.append(piece.astype(F32))
-        rest = rest - pieces[-1]
-    pieces = jnp.concatenate(pieces + [jnp.zeros((13, C), F32)], axis=0).astype(BF16)
-    lbias_row = jnp.sum(
-        lax.dot_general(pieces, by_z, by_column, preferred_element_type=F32),
-        axis=0,
-        keepdims=True,
-    ) + jnp.concatenate([latent_bias[...]] * QB, axis=1)
-
-    lbias[...] = lbias_row
-    bias = conv_bias[...]
-    bias = jnp.concatenate([bias[:, 64:]] + [bias] * 3 + [bias[:, :64]], axis=1)
-    for j in range(3):
-        cbias[j] = bias[:, 128 * j : 128 * (j + 1)]
-
-    def column_of(axis):
-        index = lax.broadcasted_iota(jnp.int32, (384, 384), axis)
-        return sum((index >= edge).astype(jnp.int32) for edge in (96, 192, 288))
-
-    ones[...] = jnp.where(column_of(0) == column_of(1), 1.0, 0.0).astype(BF16)
 
     has_left = jnp.where(wa == 0, 0.0, 1.0).astype(F32)
     has_right = jnp.where(wa == n_wa - 1, 0.0, 1.0).astype(F32)
@@ -344,8 +374,7 @@
                     inner[0, tile + 1, pl.ds(f * 16, 16)] = (d1 + d2).astype(BF16)
                     inner[1, tile + 1, pl.ds(f * 16, 16)] = (d2 - d1).astype(BF16)
 
-    @pl.loop(0, 4)
-    def _(n):
+    for n in range(4):
         groups([3 * n, 3 * n + 1, 3 * n + 2], False)
 
     for copy in col_copies:
@@ -435,8 +464,7 @@
 
     join(inner)
 
-    @pl.loop(0, 2)
-    def _(step):
+    for step in range(2):
         for n in range(21):
             outer_planes(21 * step + n)
         for m in range(2):
@@ -451,8 +479,7 @@
         even = product(outer, 0, 0, base, tile_of, weights) + (one + two)
         return even, (one - two) - product(outer, 1, 3, base, tile_of, weights)
 
-    @pl.loop(0, 2)
-    def _(step):
+    for step in range(2):
         base = step * 6
         both = both_rows(step, 0, base, tile_a, wa_w)
         for parity in range(2):
@@ -473,7 +500,7 @@
                 x = xf[3 * i + 1, pl.ds(parity, 64, 2)]
                 h = x + part[:, 128:] + cbias[0]
                 if w == 6:
-                    h = h * jnp.where(i == 13, cut_right, 1.0)
+                    h = h * cut_right if i == 13 else h
                 hb[parity, 3 * i + 1] = h.astype(BF16)
 
     for i in range(14):
@@ -547,24 +574,17 @@
     frame_of = lax.broadcasted_iota(jnp.int32, (64, 1), 0)
     latent = jnp.where(frame_of < valid[0] * 16, latent, 0.0).astype(BF16)
 
-    row = lax.broadcasted_iota(jnp.int32, (64, 64), 0)
-    col = lax.broadcasted_iota(jnp.int32, (64, 64), 1)
-    by_col = jnp.broadcast_to(owners[...], (64, 64))
-    by_row = jnp.sum(jnp.where(row == col, by_col, 0), axis=1, keepdims=True)
-    rank = jnp.sum(jnp.where((by_row == by_col) & (row < col), 1, 0), axis=0, keepdims=True)
-    slot = owners[...] * 32 + rank
-    slots = lax.broadcasted_iota(jnp.int32, (128, 64), 0)
-    selector = jnp.where(slots == slot, 1.0, 0.0).astype(BF16)
-    send[...] = jnp.dot(selector, latent, preferred_element_type=F32).astype(BF16)
+    send[...] = jnp.dot(selector[...], latent, preferred_element_type=F32).astype(BF16)
 
     here = pl.ds(pl.multiple_of(ha * 32, 32), 32)
+    keep = pltpu.make_async_copy(send.at[here], out.at[0, 0, 0, here], local_sem.at[0])
     copies = []
     for d in range(1, n_ha):
         target = lax.rem(ha + d, n_ha)
         copies.append(
             pltpu.make_async_remote_copy(
                 src_ref=send.at[pl.ds(pl.multiple_of(target * 32, 32), 32)],
-                dst_ref=received.at[here],
+                dst_ref=out.at[0, 0, 0, here],
                 send_sem=a2a_send.at[d - 1],
                 recv_sem=a2a_recv.at[d - 1],
                 device_id={"ha": target, "wa": wa},
@@ -573,13 +593,12 @@
         )
     for copy in copies:
         copy.start()
-    received[here] = send[here]
+    keep.start()
     for copy in row_copies + col_copies:
         copy.wait_send()
     for copy in copies:
         copy.wait()
-    full = jnp.concatenate([received[...].astype(F32), jnp.zeros((128, 96), F32)], axis=1)
-    out[0, 0, 0] = full.T[:416].astype(BF16)
+    keep.wait()
 
 
 def per_device(
@@ -597,15 +616,20 @@
     valid_frames,
     owners,
 ):
-    vmem = pl.BlockSpec(memory_space=pltpu.VMEM)
     hbm = pl.BlockSpec(memory_space=pltpu.HBM)
-    routed = pl.pallas_call(
+    return pl.pallas_call(
         functools.partial(kernel, n_ha, n_wa),
-        out_shape=jax.ShapeDtypeStruct((1, 1, 1, 416, 128), BF16),
-        in_specs=[hbm, hbm, vmem, pl.BlockSpec(memory_space=pltpu.SMEM), vmem, hbm, vmem, hbm]
-        + [vmem] * 3,
-        out_specs=vmem,
+        out_shape=jax.ShapeDtypeStruct((1, 1, 1, 128, 416), BF16),
+        in_specs=[hbm, hbm, hbm, pl.BlockSpec(memory_space=pltpu.SMEM)] + [hbm] * 7,
+        out_specs=hbm,
         scratch_shapes=[
+            pltpu.VMEM((1, 64), jnp.int32),
+            pltpu.VMEM((1, C), F32),
+            pltpu.VMEM((1, C), F32),
+            pltpu.VMEM((1, C), F32),
+            pltpu.VMEM((Z, C), BF16),
+            pltpu.VMEM((1, Z), F32),
+            pltpu.VMEM((128, 64), BF16),
             pltpu.VMEM((6, TH, EXT * 128), BF16),
             pltpu.VMEM((16, OWN * 128), BF16),
             pltpu.VMEM((16, OWN * 128), BF16),
@@ -634,8 +658,7 @@
             pltpu.VMEM((3, 1, 128), F32),
             pltpu.VMEM((1, 128), F32),
             pltpu.VMEM((128, 416), BF16),
-            pltpu.VMEM((128, 416), BF16),
-            pltpu.SemaphoreType.DMA((4,)),
+            pltpu.SemaphoreType.DMA((14,)),
             pltpu.SemaphoreType.DMA((10,)),
             pltpu.SemaphoreType.DMA((10,)),
             pltpu.SemaphoreType.DMA((n_ha - 1,)),
@@ -658,7 +681,6 @@
         latent_weight.T,
         latent_bias.reshape(1, Z),
     )
-    return jnp.swapaxes(routed, 3, 4)
 
 
 def solution(mesh):

time: 31.3 us -> 29.5 us (0.942)
  Pallas kernels: 28.9 us -> 27 us
    pallas_call x1, Pallas kernels: 28.9 us -> 27 us  [per_device(): pl.pallas_call(functools.partial(kernel, n_ha, n_wa), out_shape=jax.Shape...]
    pallas_call x0 -> x1, local copies, waits for them, and re-layouts: none -> 1.66 us  [per_device(): pl.pallas_call(functools.partial(kernel, n_ha, n_wa), out_shape=jax.Shape...]
    unnamed x1 -> x0, local copies, waits for them, and re-layouts: 1.55 us -> none
where the time goes in v6:
time: 29.5 us; the launch traced here: 29.3 us
  Pallas kernels  27 us (92%)
  local copies, waits for them, and re-layouts  1.66 us (6%)
  between operations  0.66 us (2%)
    pallas_call x1, Pallas kernels, per_device(): pl.pallas_call(functools.partial(kernel, n_ha, n_wa), out_shape=jax.Shape...  27 us
    pallas_call x1, local copies, waits for them, and re-layouts, per_device(): pl.pallas_call(functools.partial(kernel, n_ha, n_wa), out_shape=jax.Shape...  1.66 us

profile of v6, /device:TPU:0, one launch (start us, length us, event | category | flops | bytes accessed | tf_op | source)
XLA Modules:
  0.0 29.3 jit_solution(12405143703667829614)
XLA Ops:
  0.7 27.0 %encoder_step.1 = bf16[1,1,1,128,416]{4,3,2,1,0:T(8,128)(2,1)} custom-call(bf16[1,4,32,4992]{3,2,1,0:T(8,128)(2,1)} %frames.1, bf16[1,2,32,4992]{3,2,1,0:T(8,128)(2,1)} %cache.1, s32[1,64]{1,0:T(1,128)} %bitcast.7, s32[1]{0:T(128)S(6)} %copy.13.valid, f32[1,96]{1,0:T(1,128)} %bitcast.8, bf16[27,9216]{1,0:T(8,128)(2,1)} %conv_weight.1, f32[1,96]{1,0:T(1,128)} %bitcast.9, ...), custom_call_target="tpu_custom_call" | custom-call | tf_op jit(solution)/shard_map/encoder_step/pallas_call | solution.py:620
  27.7 1.7 %copy.12 = bf16[1,1,1,128,416]{3,4,2,1,0:T(8,128)(2,1)} copy(bf16[1,1,1,128,416]{4,3,2,1,0:T(8,128)(2,1)} %encoder_step.1) | data formatting | bytes 212992 | tf_op jit(solution)/shard_map/encoder_step/pallas_call | solution.py:620

commit v7 on v6

--- a/solution.py
+++ b/solution.py
@@ -59,8 +59,9 @@
     inner,
     outer,
     ones,
-    middle,
-    hp,
+    squares,
+    sums,
+    prod,
     hb,
     l32,
     x32,
@@ -269,41 +270,31 @@
 
     @pl.loop(0, 3)
     def _(a):
-        for m in range(4):
-            w = []
-            for s in range(3):
-                g0, g1, g2 = (taps[pl.ds((9 * a + 3 * r + s) * C, C)] for r in range(3))
+        for c in range(0, C, 16):
+            g = [
+                [taps[pl.ds((9 * a + 3 * r + s) * C + c, 16)] for s in range(3)] for r in range(3)
+            ]
+            for m in range(4):
                 if m == 0:
-                    w.append(g0)
-                elif m == 1:
-                    w.append(0.5 * (g0 + g2 + g1))
-                elif m == 2:
-                    w.append(0.5 * (g0 + g2 - g1))
+                    w = g[0]
+                elif m == 3:
+                    w = g[2]
                 else:
-                    w.append(g2)
-            zero = jnp.zeros((C, 128), F32)
-            by96 = [zero] + [pltpu.roll(x, 96, 1) for x in w]
-            by64 = [pltpu.roll(x, 64, 1) for x in w] + [zero]
-            by32 = [zero] + [pltpu.roll(x, 32, 1) for x in w]
-            w = w + [zero]
-            at = m * 1152 + a * 384
-            for s in range(4):
-                rows = pl.ds(pl.multiple_of(at + s * 96, 32), C)
-                wa_w[rows, pl.ds(0, 128)] = jnp.where(lane < 96, w[s], by96[s]).astype(BF16)
-                wa_w[rows, pl.ds(128, 128)] = jnp.where(lane < 64, by96[s], 0.0).astype(BF16)
-                one = jnp.where(lane < 64, 0.0, by64[s]).astype(BF16)
-                two = jnp.where(lane < 32, by64[s], by32[s]).astype(BF16)
-                if s < 3:
-                    rows = pl.ds(pl.multiple_of(at + s * 96 + 64, 32), C)
-                    wb_w[rows, pl.ds(0, 128)] = one
-                    wb_w[rows, pl.ds(128, 128)] = two
-                else:
-                    rows = pl.ds(pl.multiple_of(at + 352, 32), 32)
-                    wb_w[rows, pl.ds(0, 128)] = one[:32]
-                    wb_w[rows, pl.ds(128, 128)] = two[:32]
-                    rows = pl.ds(pl.multiple_of(at, 32), 64)
-                    wb_w[rows, pl.ds(0, 128)] = one[32:]
-                    wb_w[rows, pl.ds(128, 128)] = two[32:]
+                    sign = 1.0 if m == 1 else -1.0
+                    w = [0.5 * (g[0][s] + g[2][s] + sign * g[1][s]) for s in range(3)]
+                zero = jnp.zeros((16, 128), F32)
+                by96 = [zero] + [pltpu.roll(x, 96, 1) for x in w]
+                by64 = [pltpu.roll(x, 64, 1) for x in w] + [zero]
+                by32 = [zero] + [pltpu.roll(x, 32, 1) for x in w]
+                w = list(w) + [zero]
+                at = m * 1152 + a * 384
+                for s in range(4):
+                    rows = pl.ds(pl.multiple_of(at + s * 96 + c, 16), 16)
+                    wa_w[rows, pl.ds(0, 128)] = jnp.where(lane < 96, w[s], by96[s]).astype(BF16)
+                    wa_w[rows, pl.ds(128, 128)] = jnp.where(lane < 64, by96[s], 0.0).astype(BF16)
+                    rows = pl.ds(pl.multiple_of(at + (s * 96 + c + 64) % 384, 16), 16)
+                    wb_w[rows, pl.ds(0, 128)] = jnp.where(lane < 64, 0.0, by64[s]).astype(BF16)
+                    wb_w[rows, pl.ds(128, 128)] = jnp.where(lane < 32, by64[s], by32[s]).astype(BF16)
 
     fused = lax.dot_general(
         taps[pl.ds(27 * C, 9 * C)][:, :C].astype(BF16),
@@ -337,38 +328,40 @@
         u = x * lax.rsqrt(squares + C * EPS) * gain[...]
         return u + u * jnp.tanh(u)
 
-    def halo_mask(x):
-        return jnp.concatenate([x[:, :256] * has_right, x[:, 256:] * has_left], axis=1)
+    def piece(g, f, j, edge):
+        x = ext[f, :, lanes(3 * g + j)].astype(F32)
+        if edge and g == 13:
+            x = x * (has_right if j < 2 else has_left)
+        return x
 
     def groups(gs, edge):
-        xs, earlier = [], []
         for g in gs:
-            win = lanes(3 * g, 3)
-            x = ext[pl.ds(2, T), :, win].reshape(T * TH, 384).astype(F32)
-            old = ext[pl.ds(0, 2), :, win].reshape(2 * TH, 384).astype(F32)
-            if edge and g == 13:
-                x, old = halo_mask(x), halo_mask(old)
-            xs.append(x)
-            earlier.append(old)
-        activated = activate(jnp.concatenate(xs, axis=0))
-        for n, g in enumerate(gs):
-            before = ext[pl.ds(2, T), :, lanes(jnp.maximum(3 * g - 1, 0))]
-            before = pltpu.roll(before.reshape(T * TH, 128).astype(F32), 32, 1)
-            for j in range(1 if edge and g == 13 else 3):
-                here = pltpu.roll(xs[n][:, 128 * j : 128 * (j + 1)], 32, 1)
-                xf[3 * g + j + 1] = jnp.where(lane < 32, before, here)
-                before = here
-            for j in range(3):
-                part = slice(128 * j, 128 * (j + 1))
-                tile = 3 * g + j
-                for f in range(6):
-                    if f < 2:
-                        value = earlier[n][f * TH : (f + 1) * TH, part]
-                    else:
-                        at = n * T * TH + (f - 2) * TH
-                        value = activated[at : at + TH, part]
-                    act[tile, pl.ds(f * FS + 8, TH)] = value
-                for f in range(6):
+            for f in range(T):
+                for j in range(3):
+                    x = piece(g, 2 + f, j, edge)
+                    squares[g, pl.ds(f * TH, TH), pl.ds(128 * j, 128)] = (x * x).astype(BF16)
+        sums[pl.ds(gs[0], len(gs))] = jnp.dot(
+            squares[pl.ds(gs[0], len(gs))].reshape(len(gs) * T * TH, 384),
+            ones[...],
+            preferred_element_type=F32,
+        ).reshape(len(gs), T * TH, 384)
+        for g in gs:
+            for f in range(6):
+                rows = pl.ds((f - 2) * TH, TH)
+                if f >= 2:
+                    before = pltpu.roll(piece(max(g - 1, 0), f, 2, edge), 32, 1)
+                for j in range(3):
+                    tile = 3 * g + j
+                    x = piece(g, f, j, edge)
+                    if f >= 2:
+                        if tile < 40:
+                            here = pltpu.roll(x, 32, 1)
+                            xf[tile + 1, rows] = jnp.where(lane < 32, before, here)
+                            before = here
+                        total = sums[g, rows, pl.ds(128 * j, 128)]
+                        u = x * lax.rsqrt(total + C * EPS) * gain[:, 128 * j : 128 * (j + 1)]
+                        x = u + u * jnp.tanh(u)
+                    act[tile, pl.ds(f * FS + 8, TH)] = x
                     d1 = act[tile, pl.ds(f * FS + 8, 16, 2)]
                     d2 = act[tile, pl.ds(f * FS + 9, 16, 2)]
                     inner[0, tile + 1, pl.ds(f * 16, 16)] = (d1 + d2).astype(BF16)
@@ -467,41 +460,41 @@
     for step in range(2):
         for n in range(21):
             outer_planes(21 * step + n)
+        rows = pl.ds(448 * step, 448)
         for m in range(2):
-            middle[step, 0, m] = product(inner, m, 1 + m, 6 * step, tile_a, wa_w)
-            middle[step, 1, m] = product(inner, m, 1 + m, 7 * step, tile_b, wb_w)
+            prod[0, 1 + m, rows] = product(inner, m, 1 + m, 6 * step, tile_a, wa_w)
+            prod[1, 1 + m, rows] = product(inner, m, 1 + m, 7 * step, tile_b, wb_w)
 
     join(outer)
     cut_right = jnp.where((lane >= 32) & (wa == n_wa - 1), 0.0, 1.0).astype(F32)
 
-    def both_rows(step, side, base, tile_of, weights):
-        one, two = middle[step, side, 0], middle[step, side, 1]
-        even = product(outer, 0, 0, base, tile_of, weights) + (one + two)
-        return even, (one - two) - product(outer, 1, 3, base, tile_of, weights)
-
     for step in range(2):
-        base = step * 6
-        both = both_rows(step, 0, base, tile_a, wa_w)
-        for parity in range(2):
-            for w in range(7):
-                k = base + w
-                part = both[parity][64 * w : 64 * (w + 1)]
-                x = xf[3 * k + 2, pl.ds(parity, 64, 2)]
-                hb[parity, 3 * k + 2] = (x + part[:, :128] + cbias[1]).astype(BF16)
-                hp[parity, k + 1] = part[:, 128:]
-        base = step * 7
-        both = both_rows(step, 1, base, tile_b, wb_w)
-        for parity in range(2):
-            for w in range(7):
-                i = base + w
-                part = both[parity][64 * w : 64 * (w + 1)]
-                x = xf[3 * i, pl.ds(parity, 64, 2)]
-                hb[parity, 3 * i] = (x + part[:, :128] + hp[parity, i] + cbias[2]).astype(BF16)
-                x = xf[3 * i + 1, pl.ds(parity, 64, 2)]
-                h = x + part[:, 128:] + cbias[0]
-                if w == 6:
-                    h = h * cut_right if i == 13 else h
-                hb[parity, 3 * i + 1] = h.astype(BF16)
+        rows = pl.ds(448 * step, 448)
+        for m in range(2):
+            prod[0, 3 * m, rows] = product(outer, m, 3 * m, 6 * step, tile_a, wa_w)
+            prod[1, 3 * m, rows] = product(outer, m, 3 * m, 7 * step, tile_b, wb_w)
+
+        def both_rows(side, window, half, at):
+            row = 64 * window + (64 if side == 0 and window > 6 else 0) + at
+            cut = (pl.ds(row, 32), pl.ds(128 * half, 128))
+            p0, p1, p2, p3 = (prod[(side, m) + cut] for m in range(4))
+            return p0 + (p1 + p2), (p1 - p2) - p3
+
+        def put(tile, at, values, mask=None):
+            for parity in range(2):
+                x = xf[tile + 1, pl.ds(2 * at + parity, 32, 2)]
+                h = x + values[parity] + cbias[tile % 3]
+                h = h if mask is None else h * mask
+                hb[parity, tile + 1, pl.ds(at, 32)] = h.astype(BF16)
+
+        for at in range(0, 64, 32):
+            for k in range(7 * step, 7 + 6 * step):
+                put(3 * k + 1, at, both_rows(0, k, 0, at))
+            for i in range(7 * step, 7 * step + 7):
+                if i:
+                    one, two = both_rows(0, i - 1, 1, at), both_rows(1, i, 0, at)
+                    put(3 * i - 1, at, (one[0] + two[0], one[1] + two[1]))
+                put(3 * i, at, both_rows(1, i, 1, at), cut_right if i == 13 else None)
 
     for i in range(14):
         sooner = 40 if i == 0 else 3 * i - 2
@@ -640,8 +633,9 @@
             pltpu.VMEM((2, EXT + 15, 96, 128), BF16),
             pltpu.VMEM((2, EXT + 15, 96, 128), BF16),
             pltpu.VMEM((384, 384), BF16),
-            pltpu.VMEM((2, 2, 2, 448, 256), F32),
-            pltpu.VMEM((2, 14, 64, 128), F32),
+            pltpu.VMEM((14, T * TH, 384), BF16),
+            pltpu.VMEM((14, T * TH, 384), F32),
+            pltpu.VMEM((2, 4, 896, 256), F32),
             pltpu.VMEM((2, 41, 64, 128), BF16),
             pltpu.VMEM((EXT + 14, 9, 8, 128), F32),
             pltpu.VMEM((EXT + 1, 8, 128), F32),

time: 29.5 us -> 29.4 us (level)
  no operation moved by 1% of the time
where the time goes in v7:
time: 29.4 us; the launch traced here: 29.3 us
  Pallas kernels  27 us (92%)
  local copies, waits for them, and re-layouts  1.66 us (6%)
  between operations  0.66 us (2%)
    pallas_call x1, Pallas kernels, per_device(): pl.pallas_call(functools.partial(kernel, n_ha, n_wa), out_shape=jax.Shape...  27 us
    pallas_call x1, local copies, waits for them, and re-layouts, per_device(): pl.pallas_call(functools.partial(kernel, n_ha, n_wa), out_shape=jax.Shape...  1.66 us

profile of v7, /device:TPU:0, one launch (start us, length us, event | category | flops | bytes accessed | tf_op | source)
XLA Modules:
  0.0 29.3 jit_solution(7257078611722141543)
XLA Ops:
  0.7 27.0 %encoder_step.1 = bf16[1,1,1,128,416]{4,3,2,1,0:T(8,128)(2,1)} custom-call(bf16[1,4,32,4992]{3,2,1,0:T(8,128)(2,1)} %frames.1, bf16[1,2,32,4992]{3,2,1,0:T(8,128)(2,1)} %cache.1, s32[1,64]{1,0:T(1,128)} %bitcast.7, s32[1]{0:T(128)S(6)} %copy.13.valid, f32[1,96]{1,0:T(1,128)} %bitcast.8, bf16[27,9216]{1,0:T(8,128)(2,1)} %conv_weight.1, f32[1,96]{1,0:T(1,128)} %bitcast.9, ...), custom_call_target="tpu_custom_call" | custom-call | tf_op jit(solution)/shard_map/encoder_step/pallas_call | solution.py:613
  27.6 1.7 %copy.12 = bf16[1,1,1,128,416]{3,4,2,1,0:T(8,128)(2,1)} copy(bf16[1,1,1,128,416]{4,3,2,1,0:T(8,128)(2,1)} %encoder_step.1) | data formatting | bytes 212992 | tf_op jit(solution)/shard_map/encoder_step/pallas_call | solution.py:613

commit v8 on v7

--- a/solution.py
+++ b/solution.py
@@ -14,6 +14,8 @@
 T = 4
 TH = 32
 TW = 52
+TOP_TILES = 30
+BOTTOM_TILES = 20
 OWN = 39
 EXT = 42
 FS = 48
@@ -52,8 +54,12 @@
     ext,
     pack_top,
     pack_bot,
+    corner_top,
+    corner_bot,
     above,
+    above_side,
     below,
+    below_side,
     act,
     xf,
     inner,
@@ -142,82 +148,8 @@
             device_id_type=pl.DeviceIdType.MESH,
         )
 
-    def column_of(axis):
-        index = lax.broadcasted_iota(jnp.int32, (384, 384), axis)
-        return sum((index >= edge).astype(jnp.int32) for edge in (96, 192, 288))
-
-    ones[...] = jnp.where(column_of(0) == column_of(1), 1.0, 0.0).astype(BF16)
-
-    for load in small:
-        load.wait()
-    by_column = (((1,), (1,)), ((), ()))
-    by_z = jnp.concatenate([latent_weight[...]] * QB, axis=0)
-    rest = down_bias[...]
-    pieces = []
-    for _ in range(3):
-        piece = rest.astype(BF16)
-        pieces.append(piece.astype(F32))
-        rest = rest - pieces[-1]
-    pieces = jnp.concatenate(pieces + [jnp.zeros((13, C), F32)], axis=0).astype(BF16)
-    lbias_row = jnp.sum(
-        lax.dot_general(pieces, by_z, by_column, preferred_element_type=F32),
-        axis=0,
-        keepdims=True,
-    ) + jnp.concatenate([latent_bias[...]] * QB, axis=1)
-
-    lbias[...] = lbias_row
-    bias = conv_bias[...]
-    bias = jnp.concatenate([bias[:, 64:]] + [bias] * 3 + [bias[:, :64]], axis=1)
-    for j in range(3):
-        cbias[j] = bias[:, 128 * j : 128 * (j + 1)]
-
-    gain[...] = jnp.concatenate([norm_gain[...]] * 4, axis=1) * (0.5 * C**0.5)
-    row = lax.broadcasted_iota(jnp.int32, (64, 64), 0)
-    col = lax.broadcasted_iota(jnp.int32, (64, 64), 1)
-    by_col = jnp.broadcast_to(owners[...], (64, 64))
-    by_row = jnp.sum(jnp.where(row == col, by_col, 0), axis=1, keepdims=True)
-    rank = jnp.sum(jnp.where((by_row == by_col) & (row < col), 1, 0), axis=0, keepdims=True)
-    slot = owners[...] * 32 + rank
-    slots = lax.broadcasted_iota(jnp.int32, (128, 64), 0)
-    selector[...] = jnp.where(slots == slot, 1.0, 0.0).astype(BF16)
-    for load in loads:
-        load.wait()
-
-    sub = lax.broadcasted_iota(jnp.int32, (8, 384), 0)
-
-    @pl.loop(0, OWN // 3, unroll=True)
-    def _(g):
-        win = lanes(3 * g, 3)
-        tops = [ext[f, pl.ds(0, 16), win].astype(F32) for f in range(6)]
-        bots = [ext[f, pl.ds(16, 16), win].astype(F32) for f in range(6)]
-        lo = jnp.zeros((8, 384), F32)
-        hi = jnp.zeros((8, 384), F32)
-        for t in range(T):
-            lo = jnp.where(sub == t, tops[2 + t][0:1], lo)
-            lo = jnp.where(sub == 4 + t, tops[2 + t][1:2], lo)
-        for t in range(2):
-            hi = jnp.where(sub == t, tops[t][0:1], hi)
-            hi = jnp.where(sub == 2 + t, tops[t][1:2], hi)
-        pack_top[:, win] = jnp.concatenate([lo, hi], axis=0).astype(BF16)
-        lo = jnp.zeros((8, 384), F32)
-        for t in range(T):
-            lo = jnp.where(sub == t, bots[2 + t][15:16], lo)
-        for t in range(2):
-            lo = jnp.where(sub == 4 + t, bots[t][15:16], lo)
-        pack_bot[:, win] = jnp.concatenate([lo, jnp.zeros((8, 384), F32)], axis=0).astype(BF16)
-
-    pl.semaphore_wait(barrier, len(greeted))
-
     first, last = pl.ds(0, 256), pl.ds((OWN - 1) * 128, 128)
     from_right, from_left = pl.ds(OWN * 128, 256), pl.ds((OWN + 2) * 128, 128)
-    row_copies = [
-        remote(pack_top, below.at[:, own], 0, {"ha": up, "wa": wa}),
-        remote(pack_bot, above.at[:, own], 1, {"ha": down, "wa": wa}),
-        remote(pack_top.at[:, first], below.at[:, from_right], 2, {"ha": up, "wa": left}),
-        remote(pack_top.at[:, last], below.at[:, from_left], 3, {"ha": up, "wa": right}),
-        remote(pack_bot.at[:, first], above.at[:, from_right], 4, {"ha": down, "wa": left}),
-        remote(pack_bot.at[:, last], above.at[:, from_left], 5, {"ha": down, "wa": right}),
-    ]
     col_copies = [
         remote(
             frames.at[0, :, :, first],
@@ -244,10 +176,115 @@
             {"ha": ha, "wa": right},
         ),
     ]
-    for copy in row_copies + col_copies:
+    pl.semaphore_wait(barrier, len(greeted))
+    for copy in col_copies:
         copy.start()
+    for load in loads:
+        load.wait()
+
+    sub = lax.broadcasted_iota(jnp.int32, (8, 128), 0)
+
+    def top_rows(tile):
+        tops = [ext[f, pl.ds(0, 16), pl.ds(tile * 128, 128)].astype(F32)[:8] for f in range(6)]
+        lo = jnp.zeros((8, 128), F32)
+        hi = jnp.zeros((8, 128), F32)
+        for t in range(T):
+            lo = jnp.where(sub == t, tops[2 + t][0:1], lo)
+            lo = jnp.where(sub == 4 + t, tops[2 + t][1:2], lo)
+        for t in range(2):
+            hi = jnp.where(sub == t, tops[t][0:1], hi)
+            hi = jnp.where(sub == 2 + t, tops[t][1:2], hi)
+        return lo, hi
+
+    def bottom_rows(tile):
+        bots = [ext[f, pl.ds(16, 16), pl.ds(tile * 128, 128)].astype(F32)[8:] for f in range(6)]
+        lo = jnp.zeros((8, 128), F32)
+        for t in range(T):
+            lo = jnp.where(sub == t, bots[2 + t][7:8], lo)
+        for t in range(2):
+            lo = jnp.where(sub == 4 + t, bots[t][7:8], lo)
+        return lo
+
+    def put_pack(target, tile, lo, hi):
+        target[:, pl.ds(tile * 128, 128)] = jnp.concatenate([lo, hi], axis=0).astype(BF16)
+
+    above_us, below_us = {"ha": up, "wa": wa}, {"ha": down, "wa": wa}
+    half = TOP_TILES // 2 * 128
+    row_copies = []
+
+    def send_rows(copy):
+        copy.start()
+        row_copies.append(copy)
+
+    spread = TOP_TILES // 3
+    for tile in range(TOP_TILES):
+        lo, hi = top_rows(tile) if tile < TOP_TILES - 1 else (jnp.zeros((8, 128), F32),) * 2
+        far_lo, far_hi = top_rows(TOP_TILES - 1 + tile % spread)
+        far = (pltpu.roll(far_lo, 4, 0), far_lo, pltpu.roll(far_hi, 4, 0))[tile // spread]
+        put_pack(pack_top, tile, lo, jnp.where(sub < 4, hi, far))
+        if tile == TOP_TILES // 2 - 1:
+            cut = pl.ds(0, half)
+            send_rows(remote(pack_top.at[:, cut], below.at[:, cut], 0, above_us))
+    cut = pl.ds(half, half)
+    send_rows(remote(pack_top.at[:, cut], below.at[:, cut], 10, above_us))
+    for tile in range(BOTTOM_TILES):
+        far = tile + BOTTOM_TILES
+        hi = bottom_rows(far) if far < OWN else jnp.zeros((8, 128), F32)
+        put_pack(pack_bot, tile, bottom_rows(tile), hi)
+    send_rows(remote(pack_bot, above, 1, below_us))
+    for n, tile in enumerate((0, 1, OWN - 1)):
+        put_pack(corner_top, n, *top_rows(tile))
+        put_pack(corner_bot, n, bottom_rows(tile), jnp.zeros((8, 128), F32))
+    one, two = pl.ds(0, 256), pl.ds(256, 128)
+    for source, target, index, to in (
+        (corner_top, below_side, 2, up),
+        (corner_bot, above_side, 4, down),
+    ):
+        for n, (cut, side) in enumerate(((one, left), (two, right))):
+            send_rows(
+                remote(source.at[:, cut], target.at[:, cut], index + n, {"ha": to, "wa": side})
+            )
 
     lane = lax.broadcasted_iota(jnp.int32, (1, 128), 1)
+
+    def column_of(axis):
+        index = lax.broadcasted_iota(jnp.int32, (384, 384), axis)
+        return sum((index >= edge).astype(jnp.int32) for edge in (96, 192, 288))
+
+    ones[...] = jnp.where(column_of(0) == column_of(1), 1.0, 0.0).astype(BF16)
+
+    for load in small:
+        load.wait()
+    by_column = (((1,), (1,)), ((), ()))
+    by_z = jnp.concatenate([latent_weight[...]] * QB, axis=0)
+    rest = down_bias[...]
+    pieces = []
+    for _ in range(3):
+        piece = rest.astype(BF16)
+        pieces.append(piece.astype(F32))
+        rest = rest - pieces[-1]
+    pieces = jnp.concatenate(pieces + [jnp.zeros((13, C), F32)], axis=0).astype(BF16)
+    lbias_row = jnp.sum(
+        lax.dot_general(pieces, by_z, by_column, preferred_element_type=F32),
+        axis=0,
+        keepdims=True,
+    ) + jnp.concatenate([latent_bias[...]] * QB, axis=1)
+
+    lbias[...] = lbias_row
+    bias = conv_bias[...]
+    bias = jnp.concatenate([bias[:, 64:]] + [bias] * 3 + [bias[:, :64]], axis=1)
+    for j in range(3):
+        cbias[j] = bias[:, 128 * j : 128 * (j + 1)]
+
+    gain[...] = jnp.concatenate([norm_gain[...]] * 4, axis=1) * (0.5 * C**0.5)
+    row = lax.broadcasted_iota(jnp.int32, (64, 64), 0)
+    col = lax.broadcasted_iota(jnp.int32, (64, 64), 1)
+    by_col = jnp.broadcast_to(owners[...], (64, 64))
+    by_row = jnp.sum(jnp.where(row == col, by_col, 0), axis=1, keepdims=True)
+    rank = jnp.sum(jnp.where((by_row == by_col) & (row < col), 1, 0), axis=0, keepdims=True)
+    slot = owners[...] * 32 + rank
+    slots = lax.broadcasted_iota(jnp.int32, (128, 64), 0)
+    selector[...] = jnp.where(slots == slot, 1.0, 0.0).astype(BF16)
 
 
     load_conv.wait()
@@ -376,42 +413,51 @@
     for copy in row_copies:
         copy.wait_recv()
 
-    @pl.loop(0, 2)
-    def _(half):
-        his, los = [], []
-        for n in range(7):
-            g = 7 * half + n
-            win = lanes(3 * g, 3)
-            hi = below[:, win].astype(F32) * has_below
-            lo = above[:, win].astype(F32) * has_above
-            if n == 6:
-                right_on = jnp.where(half == 1, has_right, 1.0)
-                left_on = jnp.where(half == 1, has_left, 1.0)
-                hi, lo = (
-                    jnp.concatenate([x[:, :256] * right_on, x[:, 256:] * left_on], axis=1)
-                    for x in (hi, lo)
-                )
-            his.append(hi)
-            los.append(lo)
+    def halo_rows(tile):
+        if tile >= OWN:
+            cut = pl.ds((tile - OWN) * 128, 128)
+            hi, lo = below_side[:, cut].astype(F32), above_side[:, cut].astype(F32)[:8]
+            mask = has_right if tile < OWN + 2 else has_left
+            return hi * (has_below * mask), lo * (has_above * mask)
+        if tile < TOP_TILES - 1:
+            hi = below[:, pl.ds(tile * 128, 128)].astype(F32)
+        else:
+            far = [
+                below[:, pl.ds((spread * n + tile - TOP_TILES + 1) * 128, 128)].astype(F32)[8:]
+                for n in range(3)
+            ]
+            hi = jnp.concatenate(
+                [jnp.where(sub < 4, pltpu.roll(far[0], 4, 0), far[1]), pltpu.roll(far[2], 4, 0)],
+                axis=0,
+            )
+        lo = above[:, pl.ds(tile % BOTTOM_TILES * 128, 128)].astype(F32)
+        lo = lo[:8] if tile < BOTTOM_TILES else lo[8:]
+        return hi * has_below, lo * has_above
+
+    for part in range(2):
+        tiles = range(21 * part, 21 * (part + 1))
+        rows = [halo_rows(tile) for tile in tiles]
+        stacked = [jnp.concatenate([hi[:8], lo], axis=0) for hi, lo in rows]
         activated = activate(
-            jnp.concatenate([x[:8] for pair in zip(his, los) for x in pair], axis=0)
+            jnp.concatenate(
+                [jnp.concatenate(stacked[3 * n : 3 * n + 3], axis=1) for n in range(7)], axis=0
+            )
         )
-        before = below[:, lanes(jnp.maximum(21 * half - 1, 0))].astype(F32) * has_below
-        before = pltpu.roll(before[:8], 32, 1)
-        for n in range(7):
-            for j in range(3):
-                part = slice(128 * j, 128 * (j + 1))
-                tile = 21 * half + 3 * n + j
-                new = activated[16 * n : 16 * (n + 1), part]
-                act[tile, pl.ds(2 * FS + 40, T, FS)] = new[0:4]
-                act[tile, pl.ds(2 * FS + 41, T, FS)] = new[4:8]
-                act[tile, pl.ds(2 * FS + 7, T, FS)] = new[8:12]
-                act[tile, pl.ds(40, 2, FS)] = his[n][8:10, part]
-                act[tile, pl.ds(41, 2, FS)] = his[n][10:12, part]
-                act[tile, pl.ds(7, 2, FS)] = los[n][4:6, part]
-                here = pltpu.roll(his[n][:8, part], 32, 1)
-                x32[tile + 1] = jnp.where(lane < 32, before, here)
-                before = here
+        before = halo_rows(max(21 * part - 1, 0))[0][:8]
+        before = pltpu.roll(before, 32, 1)
+        for n, tile in enumerate(tiles):
+            hi, lo = rows[n]
+            cut = slice(128 * (n % 3), 128 * (n % 3 + 1))
+            new = activated[16 * (n // 3) : 16 * (n // 3 + 1), cut]
+            act[tile, pl.ds(2 * FS + 40, T, FS)] = new[0:4]
+            act[tile, pl.ds(2 * FS + 41, T, FS)] = new[4:8]
+            act[tile, pl.ds(2 * FS + 7, T, FS)] = new[8:12]
+            act[tile, pl.ds(40, 2, FS)] = hi[8:10]
+            act[tile, pl.ds(41, 2, FS)] = hi[10:12]
+            act[tile, pl.ds(7, 2, FS)] = lo[4:6]
+            here = pltpu.roll(hi[:8], 32, 1)
+            x32[tile + 1] = jnp.where(lane < 32, before, here)
+            before = here
 
     def tile_a(k, j):
         return 3 * k + j + 1
@@ -624,10 +670,14 @@
             pltpu.VMEM((1, Z), F32),
             pltpu.VMEM((128, 64), BF16),
             pltpu.VMEM((6, TH, EXT * 128), BF16),
-            pltpu.VMEM((16, OWN * 128), BF16),
-            pltpu.VMEM((16, OWN * 128), BF16),
-            pltpu.VMEM((16, EXT * 128), BF16),
-            pltpu.VMEM((16, EXT * 128), BF16),
+            pltpu.VMEM((16, TOP_TILES * 128), BF16),
+            pltpu.VMEM((16, BOTTOM_TILES * 128), BF16),
+            pltpu.VMEM((16, 384), BF16),
+            pltpu.VMEM((16, 384), BF16),
+            pltpu.VMEM((16, BOTTOM_TILES * 128), BF16),
+            pltpu.VMEM((16, 384), BF16),
+            pltpu.VMEM((16, TOP_TILES * 128), BF16),
+            pltpu.VMEM((16, 384), BF16),
             pltpu.VMEM((EXT, 6 * FS, 128), F32),
             pltpu.VMEM((41, T * TH, 128), F32),
             pltpu.VMEM((2, EXT + 15, 96, 128), BF16),
@@ -653,8 +703,8 @@
             pltpu.VMEM((1, 128), F32),
             pltpu.VMEM((128, 416), BF16),
             pltpu.SemaphoreType.DMA((14,)),
-            pltpu.SemaphoreType.DMA((10,)),
-            pltpu.SemaphoreType.DMA((10,)),
+            pltpu.SemaphoreType.DMA((11,)),
+            pltpu.SemaphoreType.DMA((11,)),
             pltpu.SemaphoreType.DMA((n_ha - 1,)),
             pltpu.SemaphoreType.DMA((n_ha - 1,)),
         ],

time: 29.4 us -> 29.1 us (0.990)
  Pallas kernels: 27 us -> 26.6 us
    pallas_call x1, Pallas kernels: 27 us -> 26.6 us  [per_device(): pl.pallas_call(functools.partial(kernel, n_ha, n_wa), out_shape=jax.Shape...]
where the time goes in v8:
time: 29.1 us; the launch traced here: 28.9 us
  Pallas kernels  26.6 us (91%)
  local copies, waits for them, and re-layouts  1.66 us (6%)
  between operations  0.66 us (2%)
    pallas_call x1, Pallas kernels, per_device(): pl.pallas_call(functools.partial(kernel, n_ha, n_wa), out_shape=jax.Shape...  26.6 us
    pallas_call x1, local copies, waits for them, and re-layouts, per_device(): pl.pallas_call(functools.partial(kernel, n_ha, n_wa), out_shape=jax.Shape...  1.66 us

profile of v8, /device:TPU:0, one launch (start us, length us, event | category | flops | bytes accessed | tf_op | source)
XLA Modules:
  0.0 28.9 jit_solution(7116651088314706140)
XLA Ops:
  0.7 26.6 %encoder_step.1 = bf16[1,1,1,128,416]{4,3,2,1,0:T(8,128)(2,1)} custom-call(bf16[1,4,32,4992]{3,2,1,0:T(8,128)(2,1)} %frames.1, bf16[1,2,32,4992]{3,2,1,0:T(8,128)(2,1)} %cache.1, s32[1,64]{1,0:T(1,128)} %bitcast.7, s32[1]{0:T(128)S(6)} %copy.13.valid, f32[1,96]{1,0:T(1,128)} %bitcast.8, bf16[27,9216]{1,0:T(8,128)(2,1)} %conv_weight.1, f32[1,96]{1,0:T(1,128)} %bitcast.9, ...), custom_call_target="tpu_custom_call" | custom-call | tf_op jit(solution)/shard_map/encoder_step/pallas_call | solution.py:659
  27.3 1.7 %copy.12 = bf16[1,1,1,128,416]{3,4,2,1,0:T(8,128)(2,1)} copy(bf16[1,1,1,128,416]{4,3,2,1,0:T(8,128)(2,1)} %encoder_step.1) | data formatting | bytes 212992 | tf_op jit(solution)/shard_map/encoder_step/pallas_call | solution.py:659

commit v9 on v8

--- a/solution.py
+++ b/solution.py
@@ -179,6 +179,48 @@
     pl.semaphore_wait(barrier, len(greeted))
     for copy in col_copies:
         copy.start()
+    lane = lax.broadcasted_iota(jnp.int32, (1, 128), 1)
+
+    def column_of(axis):
+        index = lax.broadcasted_iota(jnp.int32, (384, 384), axis)
+        return sum((index >= edge).astype(jnp.int32) for edge in (96, 192, 288))
+
+    ones[...] = jnp.where(column_of(0) == column_of(1), 1.0, 0.0).astype(BF16)
+
+    for load in small:
+        load.wait()
+    by_column = (((1,), (1,)), ((), ()))
+    by_z = jnp.concatenate([latent_weight[...]] * QB, axis=0)
+    rest = down_bias[...]
+    pieces = []
+    for _ in range(3):
+        piece = rest.astype(BF16)
+        pieces.append(piece.astype(F32))
+        rest = rest - pieces[-1]
+    pieces = jnp.concatenate(pieces + [jnp.zeros((13, C), F32)], axis=0).astype(BF16)
+    lbias_row = jnp.sum(
+        lax.dot_general(pieces, by_z, by_column, preferred_element_type=F32),
+        axis=0,
+        keepdims=True,
+    ) + jnp.concatenate([latent_bias[...]] * QB, axis=1)
+
+    lbias[...] = lbias_row
+    bias = conv_bias[...]
+    bias = jnp.concatenate([bias[:, 64:]] + [bias] * 3 + [bias[:, :64]], axis=1)
+    for j in range(3):
+        cbias[j] = bias[:, 128 * j : 128 * (j + 1)]
+
+    gain[...] = jnp.concatenate([norm_gain[...]] * 4, axis=1) * (0.5 * C**0.5)
+    row = lax.broadcasted_iota(jnp.int32, (64, 64), 0)
+    col = lax.broadcasted_iota(jnp.int32, (64, 64), 1)
+    by_col = jnp.broadcast_to(owners[...], (64, 64))
+    by_row = jnp.sum(jnp.where(row == col, by_col, 0), axis=1, keepdims=True)
+    rank = jnp.sum(jnp.where((by_row == by_col) & (row < col), 1, 0), axis=0, keepdims=True)
+    slot = owners[...] * 32 + rank
+    slots = lax.broadcasted_iota(jnp.int32, (128, 64), 0)
+    selector[...] = jnp.where(slots == slot, 1.0, 0.0).astype(BF16)
+
+
     for load in loads:
         load.wait()
 
@@ -244,47 +286,6 @@
             send_rows(
                 remote(source.at[:, cut], target.at[:, cut], index + n, {"ha": to, "wa": side})
             )
-
-    lane = lax.broadcasted_iota(jnp.int32, (1, 128), 1)
-
-    def column_of(axis):
-        index = lax.broadcasted_iota(jnp.int32, (384, 384), axis)
-        return sum((index >= edge).astype(jnp.int32) for edge in (96, 192, 288))
-
-    ones[...] = jnp.where(column_of(0) == column_of(1), 1.0, 0.0).astype(BF16)
-
-    for load in small:
-        load.wait()
-    by_column = (((1,), (1,)), ((), ()))
-    by_z = jnp.concatenate([latent_weight[...]] * QB, axis=0)
-    rest = down_bias[...]
-    pieces = []
-    for _ in range(3):
-        piece = rest.astype(BF16)
-        pieces.append(piece.astype(F32))
-        rest = rest - pieces[-1]
-    pieces = jnp.concatenate(pieces + [jnp.zeros((13, C), F32)], axis=0).astype(BF16)
-    lbias_row = jnp.sum(
-        lax.dot_general(pieces, by_z, by_column, preferred_element_type=F32),
-        axis=0,
-        keepdims=True,
-    ) + jnp.concatenate([latent_bias[...]] * QB, axis=1)
-
-    lbias[...] = lbias_row
-    bias = conv_bias[...]
-    bias = jnp.concatenate([bias[:, 64:]] + [bias] * 3 + [bias[:, :64]], axis=1)
-    for j in range(3):
-        cbias[j] = bias[:, 128 * j : 128 * (j + 1)]
-
-    gain[...] = jnp.concatenate([norm_gain[...]] * 4, axis=1) * (0.5 * C**0.5)
-    row = lax.broadcasted_iota(jnp.int32, (64, 64), 0)
-    col = lax.broadcasted_iota(jnp.int32, (64, 64), 1)
-    by_col = jnp.broadcast_to(owners[...], (64, 64))
-    by_row = jnp.sum(jnp.where(row == col, by_col, 0), axis=1, keepdims=True)
-    rank = jnp.sum(jnp.where((by_row == by_col) & (row < col), 1, 0), axis=0, keepdims=True)
-    slot = owners[...] * 32 + rank
-    slots = lax.broadcasted_iota(jnp.int32, (128, 64), 0)
-    selector[...] = jnp.where(slots == slot, 1.0, 0.0).astype(BF16)
 
 
     load_conv.wait()
@@ -404,14 +405,54 @@
                     inner[0, tile + 1, pl.ds(f * 16, 16)] = (d1 + d2).astype(BF16)
                     inner[1, tile + 1, pl.ds(f * 16, 16)] = (d2 - d1).astype(BF16)
 
-    for n in range(4):
+    def tile_a(k, j):
+        return 3 * k + j + 1
+
+    def tile_b(i, j):
+        return EXT + 1 + i if j == 0 else 3 * i + j - 1
+
+    def join(planes):
+        for m in range(2):
+            planes[m, 0] = planes[m, EXT]
+            for i in range(14):
+                later = planes[m, 3 * i + 2]
+                sooner = planes[m, 41 if i == 0 else 3 * i - 1]
+                planes[m, EXT + 1 + i] = jnp.where(lane < 64, later, sooner)
+
+    def product(planes, m, at, base, tile_of, weights):
+        rows = []
+        for w in range(7):
+            pieces = [
+                planes[m, tile_of(base + w, j), pl.ds(a * 16, 64)]
+                for a in range(3)
+                for j in range(3)
+            ]
+            rows.append(jnp.concatenate(pieces, axis=1))
+        return jnp.dot(
+            jnp.concatenate(rows, axis=0),
+            weights[pl.ds(at * 1152, 1152)],
+            preferred_element_type=F32,
+        )
+
+    def inner_products(side, step):
+        tile_of, weights = ((tile_a, wa_w), (tile_b, wb_w))[side]
+        for m in range(2):
+            prod[side, 1 + m, pl.ds(448 * step, 448)] = product(
+                inner, m, 1 + m, (6 + side) * step, tile_of, weights
+            )
+
+    for n in range(3):
         groups([3 * n, 3 * n + 1, 3 * n + 2], False)
+    inner_products(0, 0)
+    groups([9, 10, 11], False)
 
     for copy in col_copies:
         copy.wait_recv()
     groups([12, 13], True)
+    join(inner)
     for copy in row_copies:
         copy.wait_recv()
+    inner_products(0, 1)
 
     def halo_rows(tile):
         if tile >= OWN:
@@ -459,36 +500,6 @@
             x32[tile + 1] = jnp.where(lane < 32, before, here)
             before = here
 
-    def tile_a(k, j):
-        return 3 * k + j + 1
-
-    def tile_b(i, j):
-        return EXT + 1 + i if j == 0 else 3 * i + j - 1
-
-    def join(planes):
-        @pl.loop(0, 2)
-        def _(m):
-            planes[m, 0] = planes[m, EXT]
-            for i in range(14):
-                later = planes[m, 3 * i + 2]
-                sooner = planes[m, 41 if i == 0 else 3 * i - 1]
-                planes[m, EXT + 1 + i] = jnp.where(lane < 64, later, sooner)
-
-    def product(planes, m, at, base, tile_of, weights):
-        rows = []
-        for w in range(7):
-            pieces = [
-                planes[m, tile_of(base + w, j), pl.ds(a * 16, 64)]
-                for a in range(3)
-                for j in range(3)
-            ]
-            rows.append(jnp.concatenate(pieces, axis=1))
-        return jnp.dot(
-            jnp.concatenate(rows, axis=0),
-            weights[pl.ds(at * 1152, 1152)],
-            preferred_element_type=F32,
-        )
-
     def outer_planes(tile):
         for f in range(6):
             d0, d1, d2, d3 = (act[tile, pl.ds(f * FS + 7 + r, 16, 2)] for r in range(4))
@@ -501,15 +512,10 @@
             l32[tile, 3 + a, pl.ds(0, T)] = d1 + d2
             l32[tile, 6 + a, pl.ds(0, T)] = d2 - d1
 
-    join(inner)
-
     for step in range(2):
         for n in range(21):
             outer_planes(21 * step + n)
-        rows = pl.ds(448 * step, 448)
-        for m in range(2):
-            prod[0, 1 + m, rows] = product(inner, m, 1 + m, 6 * step, tile_a, wa_w)
-            prod[1, 1 + m, rows] = product(inner, m, 1 + m, 7 * step, tile_b, wb_w)
+        inner_products(1, step)
 
     join(outer)
     cut_right = jnp.where((lane >= 32) & (wa == n_wa - 1), 0.0, 1.0).astype(F32)
@@ -520,6 +526,7 @@
             prod[0, 3 * m, rows] = product(outer, m, 3 * m, 6 * step, tile_a, wa_w)
             prod[1, 3 * m, rows] = product(outer, m, 3 * m, 7 * step, tile_b, wb_w)
 
+    def epilogue(step):
         def both_rows(side, window, half, at):
             row = 64 * window + (64 if side == 0 and window > 6 else 0) + at
             cut = (pl.ds(row, 32), pl.ds(128 * half, 128))
@@ -575,11 +582,17 @@
         h = (x32[3 * i + 1] + part[:, 128:] + cbias[0]) * has_below
         h32[3 * i + 1] = h * cut_right if i == 13 else h
 
-    rows = []
-    for k in range(13):
-        pieces = [hb[parity, 3 * k + j + 1] for parity in range(2) for j in range(4)]
-        rows.append(jnp.concatenate(pieces, axis=1))
-    main = jnp.dot(jnp.concatenate(rows, axis=0), down_w[...], preferred_element_type=F32)
+    def downsample(ks):
+        rows = []
+        for k in ks:
+            pieces = [hb[parity, 3 * k + j + 1] for parity in range(2) for j in range(4)]
+            rows.append(jnp.concatenate(pieces, axis=1))
+        return jnp.dot(jnp.concatenate(rows, axis=0), down_w[...], preferred_element_type=F32)
+
+    epilogue(0)
+    main_0 = downsample(range(6))
+    epilogue(1)
+    main_1 = downsample(range(6, 13))
     rows = [
         jnp.concatenate([h32[3 * min(k, 12) + j + 1] for j in range(4)], axis=1) for k in range(14)
     ]
@@ -596,7 +609,7 @@
         for j in range(4 if b < 3 else 1):
             k = 4 * b + j
             fits = (lane >= 32 * j) & (lane < 32 * (j + 1))
-            part = main[64 * k : 64 * (k + 1)]
+            part = main_0[64 * k : 64 * (k + 1)] if k < 6 else main_1[64 * (k - 6) : 64 * (k - 5)]
             turned = pltpu.roll(part, 32 * j, 1) if j else part
             here = jnp.where(fits, turned, here)
             turned = pltpu.roll(part, (32 * j + 96) % 128, 1) if j != 1 else part

time: 29.1 us -> 28.1 us (0.966)
  Pallas kernels: 26.6 us -> 25.7 us
    pallas_call x1, Pallas kernels: 26.6 us -> 25.7 us  [per_device(): pl.pallas_call(functools.partial(kernel, n_ha, n_wa), out_shape=jax.Shape...]
where the time goes in v9:
time: 28.1 us; the launch traced here: 28 us
  Pallas kernels  25.7 us (91%)
  local copies, waits for them, and re-layouts  1.66 us (6%)
  between operations  0.66 us (2%)
    pallas_call x1, Pallas kernels, per_device(): pl.pallas_call(functools.partial(kernel, n_ha, n_wa), out_shape=jax.Shape...  25.7 us
    pallas_call x1, local copies, waits for them, and re-layouts, per_device(): pl.pallas_call(functools.partial(kernel, n_ha, n_wa), out_shape=jax.Shape...  1.66 us

profile of v9, /device:TPU:0, one launch (start us, length us, event | category | flops | bytes accessed | tf_op | source)
XLA Modules:
  0.0 28.0 jit_solution(1471581235913846709)
XLA Ops:
  0.7 25.7 %encoder_step.1 = bf16[1,1,1,128,416]{4,3,2,1,0:T(8,128)(2,1)} custom-call(bf16[1,4,32,4992]{3,2,1,0:T(8,128)(2,1)} %frames.1, bf16[1,2,32,4992]{3,2,1,0:T(8,128)(2,1)} %cache.1, s32[1,64]{1,0:T(1,128)} %bitcast.7, s32[1]{0:T(128)S(6)} %copy.13.valid, f32[1,96]{1,0:T(1,128)} %bitcast.8, bf16[27,9216]{1,0:T(8,128)(2,1)} %conv_weight.1, f32[1,96]{1,0:T(1,128)} %bitcast.9, ...), custom_call_target="tpu_custom_call" | custom-call | tf_op jit(solution)/shard_map/encoder_step/pallas_call | solution.py:672
  26.3 1.7 %copy.12 = bf16[1,1,1,128,416]{3,4,2,1,0:T(8,128)(2,1)} copy(bf16[1,1,1,128,416]{4,3,2,1,0:T(8,128)(2,1)} %encoder_step.1) | data formatting | bytes 212992 | tf_op jit(solution)/shard_map/encoder_step/pallas_call | solution.py:672

commit v10 on v9

--- a/solution.py
+++ b/solution.py
@@ -291,8 +291,7 @@
     load_conv.wait()
     load_down.wait()
 
-    @pl.loop(0, C // 4, unroll=4)
-    def _(g):
+    for g in range(C // 4):
         win = lanes(3 * g, 3)
         for weight, count, at in ((conv_taps, 27, 0), (down_taps, 9, 27)):
             x = weight[:, win].astype(F32)
@@ -306,8 +305,7 @@
             for u in range(4):
                 taps[pl.ds(at * C + 4 * g + u, count, C)] = jnp.where(lane < C, parts[u], 0.0)
 
-    @pl.loop(0, 3)
-    def _(a):
+    for a in range(3):
         for c in range(0, C, 16):
             g = [
                 [taps[pl.ds((9 * a + 3 * r + s) * C + c, 16)] for s in range(3)] for r in range(3)

time: 28.1 us -> 27.5 us (0.979)
  Pallas kernels: 25.7 us -> 25.1 us
    pallas_call x1, Pallas kernels: 25.7 us -> 25.1 us  [per_device(): pl.pallas_call(functools.partial(kernel, n_ha, n_wa), out_shape=jax.Shape...]
where the time goes in v10:
time: 27.5 us; the launch traced here: 27.4 us
  Pallas kernels  25.1 us (91%)
  local copies, waits for them, and re-layouts  1.66 us (6%)
  between operations  0.66 us (2%)
    pallas_call x1, Pallas kernels, per_device(): pl.pallas_call(functools.partial(kernel, n_ha, n_wa), out_shape=jax.Shape...  25.1 us
    pallas_call x1, local copies, waits for them, and re-layouts, per_device(): pl.pallas_call(functools.partial(kernel, n_ha, n_wa), out_shape=jax.Shape...  1.66 us

profile of v10, /device:TPU:0, one launch (start us, length us, event | category | flops | bytes accessed | tf_op | source)
XLA Modules:
  0.0 27.4 jit_solution(5935474729466860143)
XLA Ops:
  0.7 25.1 %encoder_step.1 = bf16[1,1,1,128,416]{4,3,2,1,0:T(8,128)(2,1)} custom-call(bf16[1,4,32,4992]{3,2,1,0:T(8,128)(2,1)} %frames.1, bf16[1,2,32,4992]{3,2,1,0:T(8,128)(2,1)} %cache.1, s32[1,64]{1,0:T(1,128)} %bitcast.7, s32[1]{0:T(128)S(6)} %copy.13.valid, f32[1,96]{1,0:T(1,128)} %bitcast.8, bf16[27,9216]{1,0:T(8,128)(2,1)} %conv_weight.1, f32[1,96]{1,0:T(1,128)} %bitcast.9, ...), custom_call_target="tpu_custom_call" | custom-call | tf_op jit(solution)/shard_map/encoder_step/pallas_call | solution.py:670
  25.8 1.7 %copy.12 = bf16[1,1,1,128,416]{3,4,2,1,0:T(8,128)(2,1)} copy(bf16[1,1,1,128,416]{4,3,2,1,0:T(8,128)(2,1)} %encoder_step.1) | data formatting | bytes 212992 | tf_op jit(solution)/shard_map/encoder_step/pallas_call | solution.py:670

commit v11 on v10

--- a/solution.py
+++ b/solution.py
@@ -442,15 +442,15 @@
     for n in range(3):
         groups([3 * n, 3 * n + 1, 3 * n + 2], False)
     inner_products(0, 0)
-    groups([9, 10, 11], False)
+    groups([9, 10, 11, 12], False)
+    inner_products(0, 1)
 
     for copy in col_copies:
         copy.wait_recv()
-    groups([12, 13], True)
+    groups([13], True)
     join(inner)
     for copy in row_copies:
         copy.wait_recv()
-    inner_products(0, 1)
 
     def halo_rows(tile):
         if tile >= OWN:

time: 27.5 us -> 27.5 us (level)
  no operation moved by 1% of the time
where the time goes in v11:
time: 27.5 us; the launch traced here: 27.4 us
  Pallas kernels  25 us (91%)
  local copies, waits for them, and re-layouts  1.66 us (6%)
  between operations  0.66 us (2%)
    pallas_call x1, Pallas kernels, per_device(): pl.pallas_call(functools.partial(kernel, n_ha, n_wa), out_shape=jax.Shape...  25 us
    pallas_call x1, local copies, waits for them, and re-layouts, per_device(): pl.pallas_call(functools.partial(kernel, n_ha, n_wa), out_shape=jax.Shape...  1.66 us

profile of v11, /device:TPU:0, one launch (start us, length us, event | category | flops | bytes accessed | tf_op | source)
XLA Modules:
  0.0 27.4 jit_solution(12671491770553690392)
XLA Ops:
  0.7 25.0 %encoder_step.1 = bf16[1,1,1,128,416]{4,3,2,1,0:T(8,128)(2,1)} custom-call(bf16[1,4,32,4992]{3,2,1,0:T(8,128)(2,1)} %frames.1, bf16[1,2,32,4992]{3,2,1,0:T(8,128)(2,1)} %cache.1, s32[1,64]{1,0:T(1,128)} %bitcast.7, s32[1]{0:T(128)S(6)} %copy.13.valid, f32[1,96]{1,0:T(1,128)} %bitcast.8, bf16[27,9216]{1,0:T(8,128)(2,1)} %conv_weight.1, f32[1,96]{1,0:T(1,128)} %bitcast.9, ...), custom_call_target="tpu_custom_call" | custom-call | tf_op jit(solution)/shard_map/encoder_step/pallas_call | solution.py:670
  25.7 1.7 %copy.12 = bf16[1,1,1,128,416]{3,4,2,1,0:T(8,128)(2,1)} copy(bf16[1,1,1,128,416]{4,3,2,1,0:T(8,128)(2,1)} %encoder_step.1) | data formatting | bytes 212992 | tf_op jit(solution)/shard_map/encoder_step/pallas_call | solution.py:670
